TPU v7x, 256 devices: a whole 4x4x8 slice. The times are simulated.
256 devices in a mesh: patch: 128 (over x, y, z), feat: 2 (over core).
Axes of the slice: x: 4, y: 4, z: 8, core: 2. Of those that a mesh axis runs over, the one named last changes fastest.
Arguments:
- node_feats: bfloat16 [81920, 512], P('patch', 'feat'), may hold values from -6 to 6
- cotangent: bfloat16 [81920, 512], P('patch', 'feat'), may hold values from -6 to 6
- send_weight: bfloat16 [512, 512], P(None, 'feat'), may hold values from -0.25 to 0.25
- recv_weight: bfloat16 [512, 512], P(None, 'feat'), may hold values from -0.25 to 0.25
- out_weight: bfloat16 [512, 512], P('feat'), may hold values from -0.125 to 0.125
- edge_bias: float32 [512], P('feat'), may hold values from -1 to 1
- sender: int32 [1048576], P('patch'), may hold values from 0 to 2943, as said below
- receiver: int32 [1048576], P('patch'), may hold values from 0 to 640, as said below
- wanted: int32 [128, 128, 16], P('patch'), may hold values from 0 to 79
Outputs:
- updated: bfloat16 [81920, 512], P('patch', 'feat')
- grad_nodes: bfloat16 [81920, 512], P('patch', 'feat')
- grad_send: float32 [512, 512], P(None, 'feat')
- grad_recv: float32 [512, 512], P(None, 'feat')
- grad_out: float32 [512, 512], P('feat')
- grad_bias: float32 [512], P('feat')
Inputs may be any that keep to these rules, and one draw needn't show every extreme that they name: `sender`: values below 896 name rows of the own and neighbouring patches, larger ones a listed coarse node; every patch has a slot with 0 and one with the largest value. `receiver`: 640 marks an empty slot; empty slots stand after the live ones; one patch has all 8192 slots live, every other patch at least three quarters of them.
All inputs are finite; a program needn't handle non-finite values.
Results may differ from a plain program's by a relative error of at most 0.006.
Values may be sent and summed in bfloat16 or wider, within the bound.
A program may use at most 128 MiB of HBM per device.

v0:
```python
import jax
import jax.numpy as jnp
from jax import lax
from jax.sharding import PartitionSpec as P

HALO = 128
COARSE_DEV = 80
QUOTA = 16


def padded(x, sides, width):
    for axis, dim in sides:
        size, length = (lax.axis_size(axis), x.shape[dim])
        up = [(i, (i + 1) % size) for i in range(size)]
        down = [(j, i) for i, j in up]
        last = lax.slice_in_dim(x, length - width, length, axis=dim)
        initial = lax.slice_in_dim(x, 0, width, axis=dim)
        before = lax.ppermute(last, axis, up)
        after = lax.ppermute(initial, axis, down)
        x = jnp.concatenate([before, x, after], axis=dim)
    return x


def shifted(x, axis, by):
    size = lax.axis_size(axis)
    return lax.ppermute(x, axis, [(i, (i + by) % size) for i in range(size)])


def shards(
    node_feats, cotangent, send_weight, recv_weight, out_weight, edge_bias, sender, receiver, wanted
):
    patch_count = lax.axis_size("patch")
    row_count = node_feats.shape[0]
    half_width = node_feats.shape[1]
    whole_feats = lax.all_gather(node_feats, "feat", axis=1, tiled=True)
    proj_send = jnp.dot(whole_feats, send_weight, preferred_element_type=jnp.float32).astype(
        jnp.bfloat16
    )
    proj_recv = jnp.dot(whole_feats, recv_weight, preferred_element_type=jnp.float32)
    rimmed = padded(proj_send, (("patch", 0),), HALO)
    wanted_rows = wanted.reshape(patch_count, QUOTA)
    owner_base = jnp.arange(patch_count, dtype=jnp.int32)[:, None] * COARSE_DEV
    coarse_index = (owner_base + wanted_rows).reshape(-1)
    coarse_table = lax.all_gather(proj_send[:COARSE_DEV], "patch", axis=0, tiled=True)
    far_rows = jnp.take(coarse_table, coarse_index, axis=0)
    send_table = jnp.concatenate([rimmed, far_rows], axis=0)
    recv_ext = jnp.concatenate([proj_recv, jnp.zeros((1, half_width), jnp.float32)], axis=0)
    pre_act = (
        jnp.take(send_table, sender, axis=0).astype(jnp.float32)
        + jnp.take(recv_ext, receiver, axis=0)
        + edge_bias
    )
    edge_sum = jax.ops.segment_sum(jax.nn.silu(pre_act), receiver, num_segments=row_count + 1)[
        :row_count
    ].astype(jnp.bfloat16)
    partial_mix = jnp.dot(edge_sum, out_weight, preferred_element_type=jnp.float32)
    mixed_sum = lax.psum_scatter(partial_mix, "feat", scatter_dimension=1, tiled=True)
    updated = (node_feats.astype(jnp.float32) + mixed_sum).astype(jnp.bfloat16)
    cot_whole = lax.all_gather(cotangent, "feat", axis=1, tiled=True)
    grad_out = lax.dot_general(
        edge_sum, cot_whole, (((0,), (0,)), ((), ())), preferred_element_type=jnp.float32
    )
    grad_sum = lax.dot_general(
        cot_whole, out_weight, (((1,), (1,)), ((), ())), preferred_element_type=jnp.float32
    )
    grad_ext = jnp.concatenate([grad_sum, jnp.zeros((1, half_width), jnp.float32)], axis=0)
    sigmoid_act = jax.nn.sigmoid(pre_act)
    grad_pre = (
        jnp.take(grad_ext, receiver, axis=0) * sigmoid_act * (1.0 + pre_act * (1.0 - sigmoid_act))
    )
    grad_bias = jnp.sum(grad_pre, axis=0)
    grad_recv_rows = jax.ops.segment_sum(grad_pre, receiver, num_segments=row_count + 1)[:row_count]
    grad_table = jax.ops.segment_sum(
        grad_pre, sender, num_segments=row_count + 2 * HALO + patch_count * QUOTA
    )
    from_above = shifted(grad_table[:HALO].astype(jnp.bfloat16), "patch", -1).astype(jnp.float32)
    from_below = shifted(
        grad_table[row_count + HALO : row_count + 2 * HALO].astype(jnp.bfloat16), "patch", 1
    ).astype(jnp.float32)
    grad_send_rows = grad_table[HALO : HALO + row_count]
    grad_send_rows = grad_send_rows.at[:HALO].add(from_below).at[row_count - HALO :].add(from_above)
    far_grads = grad_table[row_count + 2 * HALO :].reshape(patch_count, QUOTA, half_width)
    summed_far = jax.ops.segment_sum(
        far_grads.reshape(-1, half_width), coarse_index, num_segments=patch_count * COARSE_DEV
    )
    owned_grads = lax.psum_scatter(summed_far, "patch", scatter_dimension=0, tiled=True)
    grad_send_rows = grad_send_rows.at[:COARSE_DEV].add(owned_grads)
    send_grad_b = grad_send_rows.astype(jnp.bfloat16)
    recv_grad_b = grad_recv_rows.astype(jnp.bfloat16)
    grad_send = lax.dot_general(
        whole_feats, send_grad_b, (((0,), (0,)), ((), ())), preferred_element_type=jnp.float32
    )
    grad_recv = lax.dot_general(
        whole_feats, recv_grad_b, (((0,), (0,)), ((), ())), preferred_element_type=jnp.float32
    )
    grad_send, grad_recv, grad_out, grad_bias = lax.psum(
        (grad_send, grad_recv, grad_out, grad_bias), "patch"
    )
    back_terms = lax.dot_general(
        send_grad_b, send_weight, (((1,), (1,)), ((), ())), preferred_element_type=jnp.float32
    )
    back_terms = back_terms + lax.dot_general(
        recv_grad_b, recv_weight, (((1,), (1,)), ((), ())), preferred_element_type=jnp.float32
    )
    grad_inputs = lax.psum_scatter(back_terms, "feat", scatter_dimension=1, tiled=True)
    grad_nodes = (cotangent.astype(jnp.float32) + grad_inputs).astype(jnp.bfloat16)
    return (updated, grad_nodes, grad_send, grad_recv, grad_out, grad_bias)


def solution(mesh):
    in_specs = (
        P("patch", "feat"),
        P("patch", "feat"),
        P(None, "feat"),
        P(None, "feat"),
        P("feat", None),
        P("feat"),
        P("patch"),
        P("patch"),
        P("patch", None, None),
    )
    out_specs = (
        P("patch", "feat"),
        P("patch", "feat"),
        P(None, "feat"),
        P(None, "feat"),
        P("feat", None),
        P("feat"),
    )
    return jax.shard_map(shards, mesh=mesh, in_specs=in_specs, out_specs=out_specs, check_vma=False)
```

profile of v0, /device:TPU:8, one launch (start us, length us, event | category | flops | bytes accessed | tf_op | source)
XLA Modules:
  0.0 1309.5 jit_solution(8788539615723007136)
XLA Ops:
  7.2 2.6 all_gather.9
  12.0 2.0 collective-permute-start
  14.0 3.9 collective-permute-start.1
  19.2 2.5 all_gather.11
  23.5 31.4 %gather_fusion.2 = f32[8192,256]{1,0:T(8,128)} fusion(f32[641,256]{1,0:T(8,128)S(1)} %concatenate.16, s32[8192]{0:T(1024)S(1)} %fusion.26), kind=kCustom, calls=%fused_computation.clone | custom fusion | bytes 16809984 | tf_op jit(solution)/shard_map/jit(_take)/gather | solution.py:50
  54.8 31.4 %gather_fusion.3 = f32[8192,256]{1,0:T(8,128)} fusion(f32[641,256]{1,0:T(8,128)S(1)} %concatenate.17, s32[8192]{0:T(1024)S(1)} %fusion.26), kind=kCustom, calls=%fused_computation.1.clone | custom fusion | bytes 16809984 | tf_op jit(solution)/shard_map/jit(_take)/gather | solution.py:69
  86.3 47.1 %all-gather.2.cloned.1.call-done = bf16[10240,256]{1,0:T(8,128)(2,1)} async-done(((bf16[80,256]{1,0:T(8,128)(2,1)}), bf16[10240,256]{1,0:T(8,128)(2,1)}) %all-gather.2.cloned.1.call-update) | async-done | bytes 5242896 | tf_op jit(solution)/shard_map/all_gather | solution.py:44
  133.4 9.8 gather_fusion
  143.8 32.9 %gather_fusion.1 = bf16[8192,256]{1,0:T(8,128)(2,1)} fusion(bf16[2944,256]{1,0:T(8,128)(2,1)S(1)} %pad_maximum_fusion, s32[8192]{0:T(1024)S(1)} %fusion.25), kind=kCustom, calls=%fused_computation.3 | custom fusion | bytes 8421376 | tf_op jit(solution)/shard_map/jit(_take)/gather | solution.py:49
  176.7 10.9 fusion.27
  187.7 45.3 %scatter_custom_fusion.1 = f32[2944,256]{1,0:T(8,128)S(1)} fusion(s32[8192]{0:T(1024)S(1)} %copy-done.4, f32[8192,256]{1,0:T(8,128)} %get-tuple-element.59, f32[]{:T(128)} %constant.120.clone.1), kind=kCustom, calls=%fused_computation.24 | custom fusion | flops 2097152 | bytes 3015168 | tf_op jit(solution)/shard_map/scatter-add | solution.py:73
  233.0 16.2 %scatter_custom_fusion.2 = f32[10240,256]{1,0:T(8,128)} fusion(s32[2048]{0:T(1024)S(1)} %bitcast.19, f32[]{:T(128)} %constant.120.clone.1, f32[2944,256]{1,0:T(8,128)S(1)} %scatter_custom_fusion.1), kind=kCustom, calls=%fused_computation.15 | custom fusion | flops 524288 | bytes 12582916 | tf_op jit(solution)/shard_map/scatter-add | solution.py:83
  249.3 51.6 %scatter_custom_fusion = f32[641,256]{1,0:T(8,128)} fusion(s32[8192]{0:T(1024)S(1)} %copy-done.5, f32[8192,256]{1,0:T(8,128)} %gather_fusion.2, f32[]{:T(128)} %constant.119.clone.2, f32[]{:T(128)} %constant.128.clone.1, f32[256]{0:T(256)S(1)} %copy-done.6, pred[8192]{0:T(1024)(128)(4,1)S(1)} %get-tuple-element.66, bf16[8192,256]{1,0:T(8,128)(2,1)} %gather_fusion.1, ...), kind=kCustom, calls=%fused_computation.12 | custom fusion | flops 20971520 | bytes 13256718 | tf_op jit(solution)/shard_map/scatter-add | solution.py:53
  300.9 2.5 fusion.22
  303.5 45.8 %scatter_custom_fusion.3 = f32[641,256]{1,0:T(8,128)} fusion(s32[8192]{0:T(1024)} %param.24, f32[8192,256]{1,0:T(8,128)} %get-tuple-element.59, f32[]{:T(128)} %constant.120.clone.1), kind=kCustom, calls=%fused_computation.35 | custom fusion | flops 2097152 | bytes 656896 | tf_op jit(solution)/shard_map/scatter-add | solution.py:72
  350.9 2.5 fusion.23
  353.3 2.5 convolution_bitcast_fusion
  356.7 5.0 collective-permute-start.3
  365.2 575.4 %reduce-scatter.6.cloned.1.call-done = f32[80,256]{1,0:T(8,128)} async-done(((f32[10240,256]{1,0:T(8,128)}), f32[80,256]{1,0:T(8,128)}) %reduce-scatter.6.cloned.1.call-update) | async-done | bytes 81936 | tf_op jit(solution)/shard_map/reduce_scatter | solution.py:86
  942.1 2.5 convolution_bitcast_fusion.1
  946.1 2.6 convolution_add_fusion
  948.7 344.4 %psum.31 = f32[256]{0:T(256)} all-reduce(f32[256]{0:T(256)S(1)} %get-tuple-element.58), channel_id=1, replica_groups=mesh['patch'=128,'feat'=2] {'patch'}, use_global_device_ids=true, to_apply=%region_11.13 | all-reduce | flops 256 | bytes 2048 | tf_op jit(solution)/shard_map/psum | solution.py:96
  1295.1 2.0 copy.19
  1297.1 2.0 copy.20
  (64 shorter events, 20.7 us)
Async XLA Ops:
  7.2 14.5 %copy-start = (bf16[256,512]{1,0:T(8,128)(2,1)S(1)}, bf16[256,512]{1,0:T(8,128)(2,1)}, u32[]{:S(2)}) copy-start(bf16[256,512]{1,0:T(8,128)(2,1)} %param.21) | copy-start | bytes 786436
  7.2 16.3 %copy-start.5 = (s32[8192]{0:T(1024)S(1)}, s32[8192]{0:T(1024)}, u32[]{:S(2)}) copy-start(s32[8192]{0:T(1024)} %param.24) | copy-start | bytes 98308
  7.2 126.2 %all-gather.2.cloned.1.call-start = ((), (), s32[]{:S(2)}) async-start(), calls=%async_computation.3 | async-start | bytes 5283840 | tf_op jit(solution)/shard_map/all_gather | solution.py:44
  9.9 12.2 copy-start.1
  12.0 928.6 %reduce-scatter.6.cloned.1.call-start = ((), (), s32[]{:S(2)}) async-start(), calls=%async_computation.5 | async-start | bytes 10567680 | tf_op jit(solution)/shard_map/reduce_scatter | solution.py:86
  12.0 131.6 %collective-permute-start = (bf16[128,256]{1,0:T(8,128)(2,1)S(1)}, bf16[128,256]{1,0:T(8,128)(2,1)S(1)}, u32[]{:S(2)}, u32[]{:S(2)}) collective-permute-start(bf16[128,256]{1,0:T(8,128)(2,1)S(1)} %get-tuple-element.64), channel_id=1, source_target_pairs={{0,2},{2,4},{4,6},{6,8},{8,10},{10,12},{12,14},{14,16},{16,18},{18... | collective-permute-start | bytes 196616 | tf_op jit(solution)/shard_map/ppermute | solution.py:18
  14.0 129.6 %collective-permute-start.1 = (bf16[128,256]{1,0:T(8,128)(2,1)S(1)}, bf16[128,256]{1,0:T(8,128)(2,1)S(1)}, u32[]{:S(2)}, u32[]{:S(2)}) collective-permute-start(bf16[128,256]{1,0:T(8,128)(2,1)S(1)} %get-tuple-element.65), channel_id=1, source_target_pairs={{2,0},{4,2},{6,4},{8,6},{10,8},{12,10},{14,12},{16,14},{18,16},{20... | collective-permute-start | bytes 196616 | tf_op jit(solution)/shard_map/ppermute | solution.py:19
  21.7 1.7 copy-start.2
  54.8 31.4 %copy-start.4 = (s32[8192]{0:T(1024)S(1)}, s32[8192]{0:T(1024)}, u32[]{:S(2)}) copy-start(s32[8192]{0:T(1024)} %param.23) | copy-start | bytes 98308
  143.8 32.9 %copy-start.6 = (f32[256]{0:T(256)S(1)}, f32[256]{0:T(256)}, u32[]{:S(2)}) copy-start(f32[256]{0:T(256)} %param.22) | copy-start | bytes 3076
  249.2 1043.9 %reduce-scatter.4.cloned.1.call-start = ((), (), s32[]{:S(2)}) async-start(), calls=%async_computation.4 | async-start | bytes 1966080 | tf_op jit(solution)/shard_map/reduce_scatter | solution.py:57
  303.4 641.2 %copy-start.3 = (bf16[512,256]{1,0:T(8,128)(2,1)S(1)}, bf16[512,256]{1,0:T(8,128)(2,1)}, u32[]{:S(2)}) copy-start(bf16[512,256]{1,0:T(8,128)(2,1)} %param.19) | copy-start | bytes 786436
  303.5 991.6 %all-reduce.5.cloned.1.call-start = ((), (), s32[]{:S(2)}) async-start(), calls=%async_computation.7 | async-start | bytes 3145728 | tf_op jit(solution)/shard_map/psum | solution.py:96
  349.4 12.3 collective-permute-start.2
  356.7 6.9 collective-permute-start.3
  944.6 354.6 %reduce-scatter.8.cloned.1.call-start = ((), (), s32[]{:S(2)}) async-start(), calls=%async_computation.6 | async-start | bytes 1966080 | tf_op jit(solution)/shard_map/reduce_scatter | solution.py:105
Sparse Core Ops, SparseCore 0:
  12.1 121.2 all-gather.1
  249.4 691.1 reduce-scatter.5
  943.1 26.8 reduce-scatter.3
  977.1 225.6 all-reduce.4
  1205.1 11.6 reduce-scatter.7
where the time goes:
time: 1330 us; the launch traced here: 1310 us
  waiting for transfers between devices  624 us (47%)
  blocking collectives  350 us (26%)
  other arithmetic  178 us (13%)
  local copies, waits for them, and re-layouts  114 us (9%)
  matrix products  17 us (1%)
  between operations  14 us (1%)
    reduce_scatter x1, waiting for transfers between devices, shards(): lax.psum_scatter(summed_far, 'patch', scatter_dimension=0, tiled=True)  575 us
    psum x1, blocking collectives, shards(): lax.psum((grad_send, grad_recv, grad_out, grad_bias), 'patch')  344 us
    scatter-add x1, other arithmetic, shards(): jax.ops.segment_sum(jax.nn.silu(pre_act), receiver, num_segments=row_coun...  51.6 us
    all_gather x1, waiting for transfers between devices, shards(): lax.all_gather(proj_send[:COARSE_DEV], 'patch', axis=0, tiled=True)  47.1 us
    scatter-add x1, other arithmetic, shards(): jax.ops.segment_sum(grad_pre, receiver, num_segments=row_count + 1)  45.8 us
    scatter-add x1, other arithmetic, shards(): jax.ops.segment_sum(grad_pre, sender, num_segments=row_count + 2 * HALO +...  45.3 us
    gather x1, local copies, waits for them, and re-layouts, shards(): jnp.take(send_table, sender, axis=0).astype(jnp.float32)  32.9 us
    gather x1, local copies, waits for them, and re-layouts, shards(): jnp.take(grad_ext, receiver, axis=0) * sigmoid_act  31.4 us
  transfers between devices with their start and end apart: 9, of which 3 were waited for; matrix products, arithmetic and copies ran while one was open for 15% of the time, Pallas kernels for 0%

commit v1 on v0

v1 whole, which is shorter than its diff:
```python
import functools

import jax
import jax.numpy as jnp
from jax import lax
from jax.experimental import pallas as pl
from jax.experimental.pallas import tpu as pltpu
from jax.sharding import PartitionSpec as P

HALO = 128
COARSE = 80
QUOTA = 16
ROWS = 640
HALF = 256
EDGES = 8192
NEAR = ROWS + 2 * HALO
BLOCK = 256
TILE = 256
MESH = pl.DeviceIdType.MESH
F32 = jnp.float32
BF16 = jnp.bfloat16
I32 = jnp.int32
NN = (((1,), (0,)), ((), ()))
TN = (((0,), (0,)), ((), ()))
NT = (((1,), (1,)), ((), ()))


def mm(a, b, dims=NN):
    return lax.dot_general(a, b, dims, preferred_element_type=F32)


def place(n_patch, ring):
    me = lax.axis_index("patch")
    feat = lax.axis_index("feat")
    return me, lax.div(me, ring), lax.rem(me, ring), feat


def meet(n_patch, ring):
    planes = n_patch // ring
    me, xy, z, feat = place(n_patch, ring)
    barrier = pltpu.get_barrier_semaphore()

    def greet(patch, core):
        pl.semaphore_signal(barrier, inc=1, device_id=(patch, core), device_id_type=MESH)

    def greet_plane(d, carry):
        greet(lax.rem(xy + d, planes) * ring + z, feat)
        return carry

    def greet_ring(d, carry):
        greet(xy * ring + lax.rem(z + d, ring), feat)
        return carry

    lax.fori_loop(1, planes, greet_plane, 0)
    lax.fori_loop(1, ring, greet_ring, 0)
    greet(lax.rem(me + 1, n_patch), feat)
    greet(lax.rem(me + n_patch - 1, n_patch), feat)
    greet(me, 1 - feat)
    pl.semaphore_wait(barrier, planes - 1 + ring - 1 + 3)


def remote(src, dst, send, recv, patch, core):
    return pltpu.make_async_remote_copy(
        src_ref=src, dst_ref=dst, send_sem=send, recv_sem=recv,
        device_id=(patch, core), device_id_type=MESH,
    )


def loop(low, high, body):
    def step(i, carry):
        body(i)
        return carry

    lax.fori_loop(low, high, step, 0)


def forward_kernel(
    n_patch, ring,
    feats, cot, lists,
    table, cots, asked,
    coarse, packed,
    zs_s, zs_r, ls_s, ls_r, ps_s, ps_r, fs_s, fs_r, hs_s, hs_r, os_s, os_r, loc,
):
    planes = n_patch // ring
    per = ring * QUOTA
    me, xy, z, feat = place(n_patch, ring)
    up = lax.rem(me + 1, n_patch)
    down = lax.rem(me + n_patch - 1, n_patch)
    other = 1 - feat
    meet(n_patch, ring)

    def ring_peer(d):
        return lax.rem(z + d, ring)

    def plane_peer(d):
        return lax.rem(xy + d, planes)

    def plane_from(d):
        return lax.rem(xy + planes - d, planes)

    def ring_from(d):
        return lax.rem(z + ring - d, ring)

    def coarse_copy(d):
        return remote(feats.at[0:COARSE], coarse.at[z, 0:COARSE], zs_s.at[d], zs_r.at[d], xy * ring + ring_peer(d), feat)

    def list_copy(d):
        to = plane_peer(d)
        return remote(
            lists.at[pl.ds(to * QUOTA, QUOTA)], asked.at[pl.ds(xy * QUOTA, QUOTA)],
            ls_s.at[d], ls_r.at[d], to * ring + z, feat,
        )

    def far_rows(p):
        return table.at[feat, pl.ds(NEAR + p * per, per)]

    def plane_copy(d):
        to = plane_peer(d)
        return remote(packed.at[to], far_rows(xy), ps_s.at[d], ps_r.at[d], to * ring + z, feat)

    loop(1, ring, lambda d: coarse_copy(d).start())
    loop(1, planes, lambda d: list_copy(d).start())
    own_list = pltpu.make_async_copy(lists.at[pl.ds(xy * QUOTA, QUOTA)], asked.at[pl.ds(xy * QUOTA, QUOTA)], loc.at[0])
    own_list.start()
    own_coarse = pltpu.make_async_copy(feats.at[0:COARSE], coarse.at[z, 0:COARSE], loc.at[1])
    own_coarse.start()
    low_rim = table.at[feat, 0:HALO]
    high_rim = table.at[feat, HALO + ROWS : NEAR]
    to_up = remote(feats.at[ROWS - HALO : ROWS], low_rim, hs_s.at[0], hs_r.at[0], up, feat)
    to_down = remote(feats.at[0:HALO], high_rim, hs_s.at[1], hs_r.at[1], down, feat)
    to_up.start()
    to_down.start()
    own_rows = table.at[feat, HALO : HALO + ROWS]
    swap_own = remote(feats, own_rows, os_s.at[0], os_r.at[0], me, other)
    swap_cot = remote(cot, cots.at[feat], os_s.at[1], os_r.at[1], me, other)
    swap_own.start()
    swap_cot.start()
    keep_own = pltpu.make_async_copy(feats, own_rows, loc.at[2])
    keep_cot = pltpu.make_async_copy(cot, cots.at[feat], loc.at[3])
    keep_own.start()
    keep_cot.start()

    for k in range(ring):
        coarse[k, COARSE:HALO] = jnp.zeros((HALO - COARSE, HALF), BF16)

    own_list.wait()
    own_coarse.wait()

    def wait_list(d):
        at = asked.at[pl.ds(plane_from(d) * QUOTA, QUOTA)]
        remote(at, at, ls_s.at[d], ls_r.at[d], me, other).wait_recv()

    def wait_coarse(d):
        at = coarse.at[ring_from(d), 0:COARSE]
        remote(at, at, zs_s.at[d], zs_r.at[d], me, other).wait_recv()

    loop(1, planes, wait_list)
    loop(1, ring, wait_coarse)
    lane = lax.broadcasted_iota(I32, (planes * QUOTA, HALO), 1)
    for k in range(ring):
        pick = jnp.where(asked[:, k : k + 1] == lane, 1.0, 0.0).astype(BF16)
        rows = mm(pick, coarse[k]).astype(BF16)
        packed[:, k * QUOTA : (k + 1) * QUOTA, :] = rows.reshape(planes, QUOTA, HALF)
    loop(1, planes, lambda d: plane_copy(d).start())
    own_far = pltpu.make_async_copy(packed.at[xy], far_rows(xy), loc.at[4])
    own_far.start()
    swap_far = remote(packed.at[xy], far_rows(xy), fs_s.at[0], fs_r.at[0], me, other)
    swap_far.start()

    def pass_on(p, slot):
        at = far_rows(p)
        return remote(at, at, fs_s.at[slot], fs_r.at[slot], me, other)

    def rim_copy(rim, slot):
        return remote(rim, rim, os_s.at[slot], os_r.at[slot], me, other)

    to_up.wait()
    rim_copy(low_rim, 2).start()
    to_down.wait()
    rim_copy(high_rim, 3).start()

    def forward_one(d):
        at = far_rows(plane_from(d))
        remote(at, at, ps_s.at[d], ps_r.at[d], me, other).wait_recv()
        pass_on(plane_from(d), d).start()

    loop(1, planes, forward_one)

    loop(1, planes, lambda d: list_copy(d).wait_send())
    loop(1, ring, lambda d: coarse_copy(d).wait_send())
    loop(1, planes, lambda d: plane_copy(d).wait_send())
    keep_own.wait()
    keep_cot.wait()
    own_far.wait()
    swap_own.wait()
    swap_cot.wait()
    swap_far.wait()
    rim_copy(low_rim, 2).wait()
    rim_copy(high_rim, 3).wait()
    loop(1, planes, lambda d: pass_on(plane_from(d), d).wait())


def forward_exchange(n_patch, ring, feats, cot, lists):
    planes = n_patch // ring
    table_rows = NEAR + n_patch * QUOTA
    vmem = pl.BlockSpec(memory_space=pltpu.VMEM)
    anyspace = pl.BlockSpec(memory_space=pl.ANY)
    dma = pltpu.SemaphoreType.DMA
    return pl.pallas_call(
        functools.partial(forward_kernel, n_patch, ring),
        out_shape=(
            jax.ShapeDtypeStruct((2, table_rows, HALF), BF16),
            jax.ShapeDtypeStruct((2, ROWS, HALF), BF16),
            jax.ShapeDtypeStruct((planes * QUOTA, HALO), I32),
        ),
        in_specs=[vmem] * 3,
        out_specs=(anyspace, anyspace, vmem),
        scratch_shapes=[
            pltpu.VMEM((ring, HALO, HALF), BF16),
            pltpu.VMEM((planes, ring * QUOTA, HALF), BF16),
            dma((ring,)), dma((ring,)),
            dma((planes,)), dma((planes,)),
            dma((planes,)), dma((planes,)),
            dma((planes,)), dma((planes,)),
            dma((2,)), dma((2,)),
            dma((4,)), dma((4,)),
            dma((5,)),
        ],
        compiler_params=pltpu.CompilerParams(
            collective_id=0, has_side_effects=True, vmem_limit_bytes=32 * 2**20
        ),
        name="forward_exchange",
    )(feats, cot, lists)


def edge_kernel(
    table_rows, chunk_count,
    bounds,
    keys, table, cots, send_w, recv_w, out_w, bias,
    far_out, rim_out, own_out, wire, mix, back,
    send_s, pair_s, gsum, dtab, acc, cols, pre_s, gat_s,
):
    tiles = pl.cdiv(table_rows, TILE)
    padded = tiles * TILE
    own = slice(HALO, HALO + ROWS)

    for start in range(0, table_rows, 736 if table_rows % 736 == 0 else 128):
        size = 736 if table_rows % 736 == 0 else 128
        rows = slice(start, start + size)
        send_s[rows, :] = (
            mm(table[0, rows, :], send_w[0:HALF, :]) + mm(table[1, rows, :], send_w[HALF:, :])
        ).astype(BF16)
    if padded > table_rows:
        send_s[table_rows:padded, :] = jnp.zeros((padded - table_rows, HALF), BF16)
    pair_s[:, 0:HALF] = (
        mm(table[0, own, :], recv_w[0:HALF, :]) + mm(table[1, own, :], recv_w[HALF:, :]) + bias[...]
    ).astype(BF16)
    grad_sum = mm(cots[0], out_w[:, 0:HALF], NT) + mm(cots[1], out_w[:, HALF:], NT)
    gsum[...] = grad_sum
    pair_s[:, HALF:] = grad_sum.astype(BF16)
    dtab[...] = jnp.zeros_like(dtab)
    acc[...] = jnp.zeros_like(acc)

    turned = jnp.transpose(keys[...])
    for r in range(EDGES // 128):
        cols[r] = jnp.broadcast_to(turned[:, r : r + 1], (128, 128))

    lane = lax.broadcasted_iota(I32, (BLOCK, 128), 1)
    sub = lax.broadcasted_iota(I32, (ROWS, 128), 0)
    sub_t = lax.broadcasted_iota(I32, (TILE, 128), 0)

    def hot(mask):
        return jnp.where(mask, 1.0, 0.0).astype(BF16)

    def block(b, carry):
        col = cols[pl.ds(2 * b, 2)].reshape(BLOCK, 128)
        recv_col = jnp.bitwise_and(col, 1023)
        send_col = jnp.right_shift(col, 10)
        pick = jnp.concatenate([hot(recv_col == lane + 128 * j) for j in range(ROWS // 128)], axis=1)
        both = mm(pick, pair_s[...])
        pre_s[...] = both[:, 0:HALF]
        gat_s[...] = both[:, HALF:]
        first = bounds[2 * b]
        last = bounds[2 * b + 1]

        def gather(t, c):
            shifted = send_col - t * TILE
            oh = jnp.concatenate([hot(shifted == lane), hot(shifted == lane + 128)], axis=1)
            pre_s[...] += mm(oh, send_s[pl.ds(pl.multiple_of(t * TILE, TILE), TILE), :])
            return c

        lax.fori_loop(first, last + 1, gather, 0)
        pre = pre_s[...]
        sig = 0.5 * jnp.tanh(0.5 * pre) + 0.5
        hidden = pre * sig
        slope = sig + hidden * (1.0 - sig)
        row = keys[pl.ds(2 * b, 2), :]
        recv_row = jnp.bitwise_and(row, 1023)
        send_row = jnp.right_shift(row, 10)
        spread = jnp.concatenate([hot(sub == recv_row[0:1]), hot(sub == recv_row[1:2])], axis=1)
        acc[...] += mm(spread, jnp.concatenate([hidden, slope], axis=1).astype(BF16))
        grad_pre = (gat_s[...] * slope).astype(BF16)

        def scatter(t, c):
            shifted = send_row - t * TILE
            oh = jnp.concatenate([hot(sub_t == shifted[0:1]), hot(sub_t == shifted[1:2])], axis=1)
            dtab[pl.ds(pl.multiple_of(t * TILE, TILE), TILE), :] += mm(oh, grad_pre)
            return c

        lax.fori_loop(first, last + 1, scatter, 0)
        return carry

    lax.fori_loop(0, EDGES // BLOCK, block, 0)

    edge_sum = acc[:, 0:HALF].astype(BF16)
    mixed = mm(edge_sum, out_w[...])
    mix[0] = mixed[:, 0:HALF]
    mix[1] = mixed[:, HALF:]
    recv_grad = gsum[...] * acc[:, HALF:]
    bias_part = jnp.sum(recv_grad, axis=0, keepdims=True)
    recv_grad_b = recv_grad.astype(BF16)
    back[...] = mm(recv_grad_b, recv_w[...], NT)
    own_out[...] = dtab[own, :]
    far_out[...] = dtab[NEAR:table_rows, :].astype(BF16)
    rim_out[0] = dtab[0:HALO, :].astype(BF16)
    rim_out[1] = dtab[HALO + ROWS : NEAR, :].astype(BF16)

    chunk = 3072 // chunk_count

    def put(start, value):
        at = 0
        while at < value.shape[0]:
            c, r = divmod(start + at, chunk)
            size = min(chunk - r, value.shape[0] - at)
            wire[c, r : r + size, :] = value[at : at + size, :]
            at += size

    def put_weight(start, value):
        value = value.astype(BF16)
        for j in range(value.shape[1] // 128):
            put(start + j * value.shape[0], value[:, j * 128 : (j + 1) * 128])

    dtab_b = dtab[0:table_rows, :].astype(BF16)
    send_grad = jnp.concatenate([mm(table[0], dtab_b, TN), mm(table[1], dtab_b, TN)], axis=0)
    put_weight(0, send_grad)
    recv_w_grad = jnp.concatenate(
        [mm(table[0, own, :], recv_grad_b, TN), mm(table[1, own, :], recv_grad_b, TN)], axis=0
    )
    put_weight(1024, recv_w_grad)
    put_weight(2048, jnp.concatenate([mm(edge_sum, cots[0], TN), mm(edge_sum, cots[1], TN)], axis=1))
    sub16 = lax.broadcasted_iota(I32, (16, 128), 0)
    tail = jnp.where(sub16 == 0, bias_part[:, 0:128], jnp.where(sub16 == 1, bias_part[:, 128:], 0.0)).astype(BF16)
    for c in range(chunk_count):
        wire[c, chunk : chunk + 16, :] = tail


def edge_pass(n_patch, ring, bounds, keys, table, cots, send_w, recv_w, out_w, bias):
    planes = n_patch // ring
    table_rows = NEAR + n_patch * QUOTA
    padded = pl.cdiv(table_rows, TILE) * TILE
    vmem = pl.BlockSpec(memory_space=pltpu.VMEM)
    return pl.pallas_call(
        functools.partial(edge_kernel, table_rows, planes),
        out_shape=(
            jax.ShapeDtypeStruct((n_patch * QUOTA, HALF), BF16),
            jax.ShapeDtypeStruct((2, HALO, HALF), BF16),
            jax.ShapeDtypeStruct((ROWS, HALF), F32),
            jax.ShapeDtypeStruct((planes, 3072 // planes + 16, 128), BF16),
            jax.ShapeDtypeStruct((2, ROWS, HALF), F32),
            jax.ShapeDtypeStruct((ROWS, 2 * HALF), F32),
        ),
        in_specs=[pl.BlockSpec(memory_space=pltpu.SMEM)] + [vmem] * 7,
        out_specs=(vmem,) * 6,
        scratch_shapes=[
            pltpu.VMEM((padded, HALF), BF16),
            pltpu.VMEM((ROWS, 2 * HALF), BF16),
            pltpu.VMEM((ROWS, HALF), F32),
            pltpu.VMEM((padded, HALF), F32),
            pltpu.VMEM((ROWS, 2 * HALF), F32),
            pltpu.VMEM((EDGES // 128, 128, 128), I32),
            pltpu.VMEM((BLOCK, HALF), F32),
            pltpu.VMEM((BLOCK, HALF), F32),
        ],
        compiler_params=pltpu.CompilerParams(vmem_limit_bytes=48 * 2**20),
        name="edge_pass",
    )(bounds, keys, table, cots, send_w, recv_w, out_w, bias)


def backward_kernel(
    n_patch, ring,
    feats, cot, send_w, asked, far, rims, own, wire, mix, back,
    updated, grad_nodes, g_send, g_recv, g_out, g_bias,
    far_r, wire_r, rim_r, mix_r, back_s, back_r, zfar_s, zfar_r, zsum_s, zsum_r, zall, plane_s, plane_all,
    rs_s, rs_r, fs_s, fs_r, zf_s, zf_r, zs_s, zs_r, za_s, za_r, pa_s, pa_r, hs_s, hs_r, os_s, os_r,
):
    planes = n_patch // ring
    per = ring * QUOTA
    chunk = 3072 // planes
    part = chunk // ring
    me, xy, z, feat = place(n_patch, ring)
    up = lax.rem(me + 1, n_patch)
    down = lax.rem(me + n_patch - 1, n_patch)
    other = 1 - feat
    meet(n_patch, ring)

    def ring_peer(d):
        return lax.rem(z + d, ring)

    def plane_peer(d):
        return lax.rem(xy + d, planes)

    def plane_from(d):
        return lax.rem(xy + planes - d, planes)

    def ring_from(d):
        return lax.rem(z + ring - d, ring)

    def wire_copy(d):
        to = plane_peer(d)
        return remote(wire.at[to], wire_r.at[xy], rs_s.at[d], rs_r.at[d], to * ring + z, feat)

    def far_copy(d):
        to = plane_peer(d)
        return remote(far.at[pl.ds(to * per, per)], far_r.at[xy], fs_s.at[d], fs_r.at[d], to * ring + z, feat)

    def arrived(at, send, recv):
        remote(at, at, send, recv, me, other).wait_recv()

    loop(1, planes, lambda d: wire_copy(d).start())
    swap_mix = remote(mix.at[other], mix_r, os_s.at[0], os_r.at[0], me, other)
    swap_mix.start()
    to_down = remote(rims.at[0], rim_r.at[1], hs_s.at[0], hs_r.at[0], down, feat)
    to_up = remote(rims.at[1], rim_r.at[0], hs_s.at[1], hs_r.at[1], up, feat)
    to_down.start()
    to_up.start()
    loop(1, planes, lambda d: far_copy(d).start())

    wire_r[xy] = wire[xy]
    far_r[xy] = far[pl.ds(pl.multiple_of(xy * per, per), per), :]
    swap_mix.wait()
    updated[...] = (feats[...].astype(F32) + mix[feat] + mix_r[...]).astype(BF16)

    loop(1, planes, lambda d: arrived(wire_r.at[plane_from(d)], rs_s.at[d], rs_r.at[d]))
    total = wire_r[0].astype(F32)
    for p in range(1, planes):
        total = total + wire_r[p].astype(F32)
    for k in range(ring):
        zsum_s[k, 0:part, :] = total[k * part : (k + 1) * part, :]
        zsum_s[k, part : part + 8, :] = total[chunk : chunk + 8, :]

    def zsum_copy(d):
        to = ring_peer(d)
        return remote(zsum_s.at[to], zsum_r.at[z], zs_s.at[d], zs_r.at[d], xy * ring + to, feat)

    loop(1, ring, lambda d: zsum_copy(d).start())
    zsum_r[z] = zsum_s[z]

    loop(1, planes, lambda d: arrived(far_r.at[plane_from(d)], fs_s.at[d], fs_r.at[d]))
    lane = lax.broadcasted_iota(I32, (planes * QUOTA, HALO), 1)
    for k in range(ring):
        pick = jnp.where(asked[:, k : k + 1] == lane, 1.0, 0.0).astype(BF16)
        rows = far_r[:, k * QUOTA : (k + 1) * QUOTA, :].reshape(planes * QUOTA, HALF)
        zfar_s[k] = mm(pick, rows, TN)[0:COARSE].astype(BF16)

    def zfar_copy(d):
        to = ring_peer(d)
        return remote(zfar_s.at[to], zfar_r.at[z], zf_s.at[d], zf_r.at[d], xy * ring + to, feat)

    loop(1, ring, lambda d: arrived(zsum_r.at[ring_from(d)], zs_s.at[d], zs_r.at[d]))
    whole = zsum_r[0]
    for k in range(1, ring):
        whole = whole + zsum_r[k]
    g_bias[...] = jnp.concatenate([whole[part : part + 1], whole[part + 1 : part + 2]], axis=1)
    zall[z] = whole[0:part]

    def zall_copy(d):
        return remote(zall.at[z], zall.at[z], za_s.at[d], za_r.at[d], xy * ring + ring_peer(d), feat)

    loop(1, ring, lambda d: zall_copy(d).start())
    loop(1, ring, lambda d: zfar_copy(d).start())
    zfar_r[z] = zfar_s[z]
    loop(1, ring, lambda d: arrived(zall.at[ring_from(d)], za_s.at[d], za_r.at[d]))
    plane_s[...] = zall[...].reshape(chunk, 128).astype(BF16)

    def all_rows(p):
        return plane_all.at[pl.ds(pl.multiple_of(p * chunk, chunk), chunk)]

    def plane_copy(d):
        return remote(plane_s, all_rows(xy), pa_s.at[d], pa_r.at[d], plane_peer(d) * ring + z, feat)

    loop(1, planes, lambda d: plane_copy(d).start())
    plane_all[pl.ds(pl.multiple_of(xy * chunk, chunk), chunk), :] = plane_s[...]

    loop(1, ring, lambda d: arrived(zfar_r.at[ring_from(d)], zf_s.at[d], zf_r.at[d]))
    to_down.wait()
    to_up.wait()
    coarse = zfar_r[0].astype(F32)
    for k in range(1, ring):
        coarse = coarse + zfar_r[k].astype(F32)
    coarse = coarse + own[0:COARSE, :] + rim_r[0, 0:COARSE, :].astype(F32)
    rest = own[COARSE:HALO, :] + rim_r[0, COARSE:HALO, :].astype(F32)
    last = own[ROWS - HALO : ROWS, :] + rim_r[1].astype(F32)
    send_grad = jnp.concatenate([coarse, rest, own[HALO : ROWS - HALO, :], last], axis=0).astype(BF16)
    terms = back[...] + mm(send_grad, send_w[...], NT)
    back_s[0] = terms[:, 0:HALF]
    back_s[1] = terms[:, HALF:]
    swap_back = remote(back_s.at[other], back_r, os_s.at[1], os_r.at[1], me, other)
    swap_back.start()
    swap_back.wait()
    grad_nodes[...] = (cot[...].astype(F32) + back_s[feat] + back_r[...]).astype(BF16)

    loop(1, planes, lambda d: arrived(all_rows(plane_from(d)), pa_s.at[d], pa_r.at[d]))
    for j in range(2):
        cols = slice(128 * j, 128 * (j + 1))
        g_send[:, cols] = plane_all[512 * j : 512 * (j + 1), :].astype(F32)
        g_recv[:, cols] = plane_all[1024 + 512 * j : 1024 + 512 * (j + 1), :].astype(F32)
    for j in range(4):
        g_out[:, 128 * j : 128 * (j + 1)] = plane_all[2048 + 256 * j : 2048 + 256 * (j + 1), :].astype(F32)

    loop(1, planes, lambda d: wire_copy(d).wait_send())
    loop(1, planes, lambda d: far_copy(d).wait_send())
    loop(1, planes, lambda d: plane_copy(d).wait_send())
    loop(1, ring, lambda d: zsum_copy(d).wait_send())
    loop(1, ring, lambda d: zfar_copy(d).wait_send())
    loop(1, ring, lambda d: zall_copy(d).wait_send())


def backward_exchange(n_patch, ring, *args):
    planes = n_patch // ring
    chunk = 3072 // planes
    part = chunk // ring
    vmem = pl.BlockSpec(memory_space=pltpu.VMEM)
    dma = pltpu.SemaphoreType.DMA
    return pl.pallas_call(
        functools.partial(backward_kernel, n_patch, ring),
        out_shape=(
            jax.ShapeDtypeStruct((ROWS, HALF), BF16),
            jax.ShapeDtypeStruct((ROWS, HALF), BF16),
            jax.ShapeDtypeStruct((2 * HALF, HALF), F32),
            jax.ShapeDtypeStruct((2 * HALF, HALF), F32),
            jax.ShapeDtypeStruct((HALF, 2 * HALF), F32),
            jax.ShapeDtypeStruct((1, HALF), F32),
        ),
        in_specs=[vmem] * len(args),
        out_specs=(vmem,) * 6,
        scratch_shapes=[
            pltpu.VMEM((planes, ring * QUOTA, HALF), BF16),
            pltpu.VMEM((planes, chunk + 16, 128), BF16),
            pltpu.VMEM((2, HALO, HALF), BF16),
            pltpu.VMEM((ROWS, HALF), F32),
            pltpu.VMEM((2, ROWS, HALF), F32),
            pltpu.VMEM((ROWS, HALF), F32),
            pltpu.VMEM((ring, COARSE, HALF), BF16),
            pltpu.VMEM((ring, COARSE, HALF), BF16),
            pltpu.VMEM((ring, part + 8, 128), F32),
            pltpu.VMEM((ring, part + 8, 128), F32),
            pltpu.VMEM((ring, part, 128), F32),
            pltpu.VMEM((chunk, 128), BF16),
            pltpu.VMEM((3072, 128), BF16),
            dma((planes,)), dma((planes,)),
            dma((planes,)), dma((planes,)),
            dma((ring,)), dma((ring,)),
            dma((ring,)), dma((ring,)),
            dma((ring,)), dma((ring,)),
            dma((planes,)), dma((planes,)),
            dma((2,)), dma((2,)),
            dma((2,)), dma((2,)),
        ],
        compiler_params=pltpu.CompilerParams(
            collective_id=1, has_side_effects=True, vmem_limit_bytes=48 * 2**20
        ),
        name="backward_exchange",
    )(*args)


def shards(n_patch, ring, feats, cot, send_w, recv_w, out_w, bias, sender, receiver, wanted):
    planes = n_patch // ring
    keys = lax.sort(sender * 1024 + receiver, is_stable=False)
    ends = keys.reshape(EDGES // BLOCK, BLOCK)
    bounds = jnp.stack([ends[:, 0], ends[:, BLOCK - 1]], axis=1).reshape(-1) // (1024 * TILE)
    keys = keys.reshape(EDGES // 128, 128)
    lists = wanted.reshape(planes, ring, QUOTA).transpose(0, 2, 1).reshape(planes * QUOTA, ring)
    lists = jnp.pad(lists, ((0, 0), (0, HALO - ring)))
    table, cots, asked = forward_exchange(n_patch, ring, feats, cot, lists)
    far, rims, own, wire, mix, back = edge_pass(
        n_patch, ring, bounds, keys, table, cots, send_w, recv_w, out_w, bias.reshape(1, HALF)
    )
    updated, grad_nodes, g_send, g_recv, g_out, g_bias = backward_exchange(
        n_patch, ring, feats, cot, send_w, asked, far, rims, own, wire, mix, back
    )
    return (updated, grad_nodes, g_send, g_recv, g_out, g_bias.reshape(HALF))


def solution(mesh):
    n_patch = mesh.shape["patch"]
    ring = 8 if n_patch % 128 == 0 else 2
    in_specs = (
        P("patch", "feat"),
        P("patch", "feat"),
        P(None, "feat"),
        P(None, "feat"),
        P("feat", None),
        P("feat"),
        P("patch"),
        P("patch"),
        P("patch", None, None),
    )
    out_specs = (
        P("patch", "feat"),
        P("patch", "feat"),
        P(None, "feat"),
        P(None, "feat"),
        P("feat", None),
        P("feat"),
    )
    return jax.shard_map(
        functools.partial(shards, n_patch, ring), mesh=mesh, in_specs=in_specs, out_specs=out_specs, check_vma=False
    )
```

time: 1330 us -> 155 us (0.12); the launches traced: 1310 us -> 154 us
  waiting for transfers between devices: 624 us -> 0 us
  blocking collectives: 350 us -> 0 us
  other arithmetic: 178 us -> 6.53 us
  Pallas kernels: 0 us -> 137 us
  local copies, waits for them, and re-layouts: 114 us -> 10.1 us
  matrix products: 17 us -> 0 us
    reduce_scatter x3 -> x0, waiting for transfers between devices: 575 us -> none  [the longest x1 575 us: shards(): lax.psum_scatter(summed_far, 'patch', scatter_dimension=0, tiled=True)]
    psum x1 -> x0, blocking collectives: 344 us -> none  [shards(): lax.psum((grad_send, grad_recv, grad_out, grad_bias), 'patch')]
    scatter-add x7 -> x0, other arithmetic: 163 us -> none  [the longest x1 51.6 us: shards(): jax.ops.segment_sum(jax.nn.silu(pre_act), receiver, num_segments=row_coun...]
    pallas_call x0 -> x3, Pallas kernels: none -> 137 us  [the longest x1 55.3 us: backward_exchange(): pl.pallas_call(functools.partial(backward_kernel, n_patch, ring), out_sha...]
    gather x4 -> x0, local copies, waits for them, and re-layouts: 105 us -> none  [the longest x1 32.9 us: shards(): jnp.take(send_table, sender, axis=0).astype(jnp.float32)]
    all_gather x1 -> x0, waiting for transfers between devices: 47.1 us -> none  [shards(): lax.all_gather(proj_send[:COARSE_DEV], 'patch', axis=0, tiled=True)]
    dot_general x9 -> x0, matrix products: 17 us -> none  [the longest x1 2.58 us: shards(): lax.dot_general(recv_grad_b, recv_weight, (((1,), (1,)), ((), ())), prefe...]
  transfers between devices with their start and end apart: 9 -> 0, of which waited for: 3 -> 0; matrix products, arithmetic and copies ran while one was open for 15% -> 0% of each run, Pallas kernels for 0% -> 0%
where the time goes in v1:
time: 155 us; the launch traced here: 154 us
  Pallas kernels  137 us (88%)
  local copies, waits for them, and re-layouts  10.1 us (7%)
  other arithmetic  6.53 us (4%)
    pallas_call x1, Pallas kernels, backward_exchange(): pl.pallas_call(functools.partial(backward_kernel, n_patch, ring), out_sha...  55.3 us
    pallas_call x1, Pallas kernels, edge_pass(): pl.pallas_call(functools.partial(edge_kernel, table_rows, planes), out_sh...  46.7 us
    pallas_call x1, Pallas kernels, forward_exchange(): pl.pallas_call(functools.partial(forward_kernel, n_patch, ring), out_shap...  34.8 us
    unnamed x27, local copies, waits for them, and re-layouts  9.84 us
    sort x1, other arithmetic, shards(): keys = lax.sort(sender * 1024 + receiver, is_stable=False)  5.59 us

profile of v1, /device:TPU:8, one launch (start us, length us, event | category | flops | bytes accessed | tf_op | source)
XLA Modules:
  0.0 154.3 jit_solution(7126467225024671000)
XLA Ops:
  0.6 0.0 copy-start.6
  0.7 0.8 multiply_add_fusion
  1.5 5.6 %sort.7 = s32[8192]{0:T(1024)S(1)} sort(s32[8192]{0:T(1024)S(1)} %multiply_add_fusion), dimensions={0}, to_apply=%region_0.0 | sort | flops 106496 | bytes 65536 | tf_op jit(solution)/shard_map/sort | solution.py:578
  7.1 0.1 fusion
  7.2 0.1 pad_add_fusion
  7.3 0.1 reshape.36
  7.4 0.8 copy.26
  8.2 0.1 copy.27
  8.3 0.0 copy-start.1
  8.3 1.0 copy-done.1
  9.3 1.0 copy-done.3
  10.3 34.8 %forward_exchange.1 = (bf16[2,2944,256]{2,1,0:T(8,128)(2,1)S(1)}, bf16[2,640,256]{2,1,0:T(8,128)(2,1)S(1)}, s32[256,128]{1,0:T(8,128)S(1)}) custom-call(bf16[640,256]{1,0:T(8,128)(2,1)S(1)} %copy-done.1, bf16[640,256]{1,0:T(8,128)(2,1)S(1)} %copy-done.3, s32[256,128]{1,0:T(8,128)S(1)} %pad.4.lists), custom_call_target="tpu_custom_call" | custom-call | tf_op jit(solution)/shard_map/forward_exchange/pallas_call | solution.py:209
  45.1 1.6 %copy-done = bf16[2,2944,256]{2,1,0:T(8,128)(2,1)} copy-done((bf16[2,2944,256]{2,1,0:T(8,128)(2,1)}, bf16[2,2944,256]{2,1,0:T(8,128)(2,1)S(1)}, u32[]{:S(2)}) %copy-start) | copy-done | bytes 3014680
  46.7 0.0 copy-start.2
  46.7 0.0 copy-start.4
  46.8 46.7 %edge_pass.1 = (bf16[2048,256]{1,0:T(8,128)(2,1)S(1)}, bf16[2,128,256]{2,1,0:T(8,128)(2,1)S(1)}, f32[640,256]{1,0:T(8,128)S(1)}, bf16[16,208,128]{2,1,0:T(8,128)...) custom-call(s32[64]{0:T(128)S(1)} %and_select_fusion.bounds, s32[64,128]{1,0:T(8,128)S(1)} %bitcast.7, ...), custom_call_target="tpu_custom_call" | custom-call | tf_op jit(solution)/shard_map/edge_pass/pallas_call | solution.py:362
  93.4 1.1 copy-done.5
  94.5 55.3 %backward_exchange.1 = (bf16[640,256]{1,0:T(8,128)(2,1)S(1)}, bf16[640,256]{1,0:T(8,128)(2,1)S(1)}, f32[512,256]{1,0:T(8,128)S(1)}, f32[512,256]{1,0:T(8,128)S(1...) custom-call(bf16[640,256]{1,0:T(8,128)(2,1)S(1)} %copy-done.2, bf16[640,256]{1,0:T(8,128)(2,1)S(1)} %copy-done.4, ...), custom_call_target="tpu_custom_call" | custom-call | tf_op jit(solution)/shard_map/backward_exchange/pallas_call | solution.py:534
  149.9 0.7 copy.34
  150.6 0.7 copy.35
  151.3 0.8 copy.36
  152.1 0.8 copy.37
  152.9 0.8 copy.38
  153.7 0.6 copy.39
  (15 shorter events, 0.1 us)
Async XLA Ops:
  0.6 46.1 %copy-start.6 = (bf16[512,256]{1,0:T(8,128)(2,1)S(1)}, bf16[512,256]{1,0:T(8,128)(2,1)}, u32[]{:S(2)}) copy-start(bf16[512,256]{1,0:T(8,128)(2,1)} %send_w.3) | copy-start | bytes 786436
  0.6 46.1 %copy-start.9 = (f32[256]{0:T(256)S(1)}, f32[256]{0:T(256)}, u32[]{:S(2)}) copy-start(f32[256]{0:T(256)} %param.14) | copy-start | bytes 3076
  0.7 46.1 %copy-start.8 = (bf16[256,512]{1,0:T(8,128)(2,1)S(1)}, bf16[256,512]{1,0:T(8,128)(2,1)}, u32[]{:S(2)}) copy-start(bf16[256,512]{1,0:T(8,128)(2,1)} %out_w.1) | copy-start | bytes 786436
  0.7 46.1 %copy-start.7 = (bf16[512,256]{1,0:T(8,128)(2,1)S(1)}, bf16[512,256]{1,0:T(8,128)(2,1)}, u32[]{:S(2)}) copy-start(bf16[512,256]{1,0:T(8,128)(2,1)} %recv_w.1) | copy-start | bytes 786436
  8.3 1.0 copy-start.1
  9.3 1.0 copy-start.3
  45.1 1.6 %copy-start = (bf16[2,2944,256]{2,1,0:T(8,128)(2,1)}, bf16[2,2944,256]{2,1,0:T(8,128)(2,1)S(1)}, u32[]{:S(2)}) copy-start(bf16[2,2944,256]{2,1,0:T(8,128)(2,1)S(1)} %get-tuple-element.22.table) | copy-start | bytes 9043972
  46.7 47.8 %copy-start.2 = (bf16[640,256]{1,0:T(8,128)(2,1)S(1)}, bf16[640,256]{1,0:T(8,128)(2,1)}, u32[]{:S(2)}) copy-start(bf16[640,256]{1,0:T(8,128)(2,1)} %feats.3) | copy-start | bytes 983044
  46.7 47.8 %copy-start.4 = (bf16[640,256]{1,0:T(8,128)(2,1)S(1)}, bf16[640,256]{1,0:T(8,128)(2,1)}, u32[]{:S(2)}) copy-start(bf16[640,256]{1,0:T(8,128)(2,1)} %cot.3) | copy-start | bytes 983044
  93.4 1.1 copy-start.5

commit v2 on v1

--- a/solution.py
+++ b/solution.py
@@ -16,10 +16,16 @@
 NEAR = ROWS + 2 * HALO
 BLOCK = 256
 TILE = 256
+BLOCKS = EDGES // BLOCK
+ITEMS = 44
+UNROLL = 11
+WIDE = 8
+SPAN = 1024
 MESH = pl.DeviceIdType.MESH
 F32 = jnp.float32
 BF16 = jnp.bfloat16
 I32 = jnp.int32
+I16 = jnp.int16
 NN = (((1,), (0,)), ((), ()))
 TN = (((0,), (0,)), ((), ()))
 NT = (((1,), (1,)), ((), ()))
@@ -238,7 +244,7 @@
     bounds,
     keys, table, cots, send_w, recv_w, out_w, bias,
     far_out, rim_out, own_out, wire, mix, back,
-    send_s, pair_s, gsum, dtab, acc, cols, pre_s, gat_s,
+    send_s, pair_s, gsum, dtab, acc, cols, cols_r, pre_s, act_s, gat_s, item_b, item_t,
 ):
     tiles = pl.cdiv(table_rows, TILE)
     padded = tiles * TILE
@@ -263,54 +269,101 @@
 
     turned = jnp.transpose(keys[...])
     for r in range(EDGES // 128):
-        cols[r] = jnp.broadcast_to(turned[:, r : r + 1], (128, 128))
-
-    lane = lax.broadcasted_iota(I32, (BLOCK, 128), 1)
-    sub = lax.broadcasted_iota(I32, (ROWS, 128), 0)
-    sub_t = lax.broadcasted_iota(I32, (TILE, 128), 0)
+        spread = jnp.broadcast_to(turned[:, r : r + 1], (128, 128))
+        cols[r] = jnp.right_shift(spread, 10).astype(I16)
+        cols_r[r] = jnp.bitwise_and(spread, 1023).astype(I16)
+
+    def list_block(b, at):
+        def push(t, at):
+            item_b[at] = b
+            item_t[at] = t
+            return at + 1
+
+        return lax.fori_loop(bounds[2 * b], bounds[2 * b + 1] + 1, push, at)
+
+    count = lax.fori_loop(0, BLOCKS, list_block, 0)
+
+    def fill(at, c):
+        item_b[at] = 0
+        item_t[at] = tiles
+        return c
+
+    lax.fori_loop(count, ITEMS, fill, 0)
+
+    lane = lax.broadcasted_iota(I32, (BLOCK, 128), 1).astype(I16)
+    sub = lax.broadcasted_iota(I32, (ROWS, 128), 0).astype(I16)
+    sub_t = lax.broadcasted_iota(I32, (TILE, 128), 0).astype(I16)
 
     def hot(mask):
-        return jnp.where(mask, 1.0, 0.0).astype(BF16)
+        return jnp.where(mask, BF16(1.0), BF16(0.0))
+
+    def down(row, rows):
+        packed = jnp.broadcast_to(row, (16, 128)).astype(I16)
+        return jnp.concatenate([packed] * (rows // 16), axis=0)
+
+    def rows_of(b, size=BLOCK):
+        return pl.ds(pl.multiple_of(b * size, size), size)
+
+    def gather_item(i):
+        b = item_b[i]
+        t = item_t[i]
+        shifted = cols[pl.ds(2 * b, 2)].reshape(BLOCK, 128) - jnp.full((BLOCK, 128), t * TILE, I32).astype(I16)
+        oh = jnp.concatenate([hot(shifted == lane), hot(shifted == lane + I16(128))], axis=1)
+        return b, mm(oh, send_s[rows_of(jnp.minimum(t, tiles - 1)), :])
+
+    def gather(i, c):
+        parts = [gather_item(i * UNROLL + u) for u in range(UNROLL)]
+        for b, part in parts:
+            pre_s[rows_of(b), :] += part
+        return c
+
+    def clear(b, c):
+        pre_s[rows_of(b), :] = jnp.zeros((BLOCK, HALF), F32)
+        return c
+
+    lax.fori_loop(0, BLOCKS, clear, 0)
+    lax.fori_loop(0, ITEMS // UNROLL, gather, 0)
 
     def block(b, carry):
-        col = cols[pl.ds(2 * b, 2)].reshape(BLOCK, 128)
-        recv_col = jnp.bitwise_and(col, 1023)
-        send_col = jnp.right_shift(col, 10)
-        pick = jnp.concatenate([hot(recv_col == lane + 128 * j) for j in range(ROWS // 128)], axis=1)
-        both = mm(pick, pair_s[...])
-        pre_s[...] = both[:, 0:HALF]
-        gat_s[...] = both[:, HALF:]
-        first = bounds[2 * b]
-        last = bounds[2 * b + 1]
-
-        def gather(t, c):
-            shifted = send_col - t * TILE
-            oh = jnp.concatenate([hot(shifted == lane), hot(shifted == lane + 128)], axis=1)
-            pre_s[...] += mm(oh, send_s[pl.ds(pl.multiple_of(t * TILE, TILE), TILE), :])
-            return c
-
-        lax.fori_loop(first, last + 1, gather, 0)
-        pre = pre_s[...]
-        sig = 0.5 * jnp.tanh(0.5 * pre) + 0.5
-        hidden = pre * sig
-        slope = sig + hidden * (1.0 - sig)
-        row = keys[pl.ds(2 * b, 2), :]
-        recv_row = jnp.bitwise_and(row, 1023)
-        send_row = jnp.right_shift(row, 10)
-        spread = jnp.concatenate([hot(sub == recv_row[0:1]), hot(sub == recv_row[1:2])], axis=1)
-        acc[...] += mm(spread, jnp.concatenate([hidden, slope], axis=1).astype(BF16))
-        grad_pre = (gat_s[...] * slope).astype(BF16)
-
-        def scatter(t, c):
-            shifted = send_row - t * TILE
-            oh = jnp.concatenate([hot(sub_t == shifted[0:1]), hot(sub_t == shifted[1:2])], axis=1)
-            dtab[pl.ds(pl.multiple_of(t * TILE, TILE), TILE), :] += mm(oh, grad_pre)
-            return c
-
-        lax.fori_loop(first, last + 1, scatter, 0)
+        for u in range(WIDE):
+            bu = b * WIDE + u
+            recv_col = cols_r[pl.ds(2 * bu, 2)].reshape(BLOCK, 128)
+            pick = jnp.concatenate([hot(recv_col == lane + I16(128 * j)) for j in range(ROWS // 128)], axis=1)
+            both = mm(pick, pair_s[...])
+            pre = pre_s[rows_of(bu), :] + both[:, 0:HALF]
+            sig = 0.5 * jnp.tanh(0.5 * pre) + 0.5
+            hidden = pre * sig
+            slope = sig + hidden * (1.0 - sig)
+            act_s[rows_of(bu), 0:HALF] = hidden.astype(BF16)
+            act_s[rows_of(bu), HALF:] = slope.astype(BF16)
+            gat_s[rows_of(bu), :] = (both[:, HALF:] * slope).astype(BF16)
         return carry
 
-    lax.fori_loop(0, EDGES // BLOCK, block, 0)
+    lax.fori_loop(0, BLOCKS // WIDE, block, 0)
+
+    def collect(i, c):
+        rows = keys[pl.ds(pl.multiple_of(i * (SPAN // 128), SPAN // 128), SPAN // 128), :]
+        recv_row = jnp.bitwise_and(rows, 1023)
+        spread = jnp.concatenate([hot(sub == down(recv_row[j : j + 1], ROWS)) for j in range(SPAN // 128)], axis=1)
+        acc[...] += mm(spread, act_s[rows_of(i, SPAN), :])
+        return c
+
+    lax.fori_loop(0, EDGES // SPAN, collect, 0)
+
+    def scatter_item(i):
+        b = item_b[i]
+        t = item_t[i]
+        shifted = jnp.right_shift(keys[pl.ds(2 * b, 2), :], 10) - t * TILE
+        oh = jnp.concatenate([hot(sub_t == down(shifted[0:1], TILE)), hot(sub_t == down(shifted[1:2], TILE))], axis=1)
+        return jnp.minimum(t, tiles - 1), mm(oh, gat_s[rows_of(b), :])
+
+    def scatter(i, c):
+        parts = [scatter_item(i * UNROLL + u) for u in range(UNROLL)]
+        for t, part in parts:
+            dtab[rows_of(t), :] += part
+        return c
+
+    lax.fori_loop(0, ITEMS // UNROLL, scatter, 0)
 
     edge_sum = acc[:, 0:HALF].astype(BF16)
     mixed = mm(edge_sum, out_w[...])
@@ -377,11 +430,15 @@
             pltpu.VMEM((ROWS, HALF), F32),
             pltpu.VMEM((padded, HALF), F32),
             pltpu.VMEM((ROWS, 2 * HALF), F32),
-            pltpu.VMEM((EDGES // 128, 128, 128), I32),
-            pltpu.VMEM((BLOCK, HALF), F32),
-            pltpu.VMEM((BLOCK, HALF), F32),
+            pltpu.VMEM((EDGES // 128, 128, 128), I16),
+            pltpu.VMEM((EDGES // 128, 128, 128), I16),
+            pltpu.VMEM((EDGES, HALF), F32),
+            pltpu.VMEM((EDGES, 2 * HALF), BF16),
+            pltpu.VMEM((EDGES, HALF), BF16),
+            pltpu.SMEM((ITEMS,), I32),
+            pltpu.SMEM((ITEMS,), I32),
         ],
-        compiler_params=pltpu.CompilerParams(vmem_limit_bytes=48 * 2**20),
+        compiler_params=pltpu.CompilerParams(vmem_limit_bytes=56 * 2**20),
         name="edge_pass",
     )(bounds, keys, table, cots, send_w, recv_w, out_w, bias)
 

time: 155 us -> 143 us (0.923)
  Pallas kernels: 137 us -> 120 us
  local copies, waits for them, and re-layouts: 10.1 us -> 14.3 us
    pallas_call x1, Pallas kernels: 46.7 us -> 30.3 us  [edge_pass(): pl.pallas_call(functools.partial(edge_kernel, table_rows, planes), out_sh...]
    unnamed x27 -> x31, local copies, waits for them, and re-layouts: 9.84 us -> 14 us
where the time goes in v2:
time: 143 us; the launch traced here: 142 us
  Pallas kernels  120 us (84%)
  local copies, waits for them, and re-layouts  14.3 us (10%)
  other arithmetic  6.98 us (5%)
    pallas_call x1, Pallas kernels, backward_exchange(): pl.pallas_call(functools.partial(backward_kernel, n_patch, ring), out_sha...  55 us
    pallas_call x1, Pallas kernels, forward_exchange(): pl.pallas_call(functools.partial(forward_kernel, n_patch, ring), out_shap...  34.8 us
    pallas_call x1, Pallas kernels, edge_pass(): pl.pallas_call(functools.partial(edge_kernel, table_rows, planes), out_sh...  30.3 us
    unnamed x31, local copies, waits for them, and re-layouts  14 us
    sort x1, other arithmetic, shards(): keys = lax.sort(sender * 1024 + receiver, is_stable=False)  5.59 us

profile of v2, /device:TPU:8, one launch (start us, length us, event | category | flops | bytes accessed | tf_op | source)
XLA Modules:
  0.0 142.1 jit_solution(6163975005424545524)
XLA Ops:
  0.6 0.8 multiply_add_fusion
  1.4 5.6 %sort.7 = s32[8192]{0:T(1024)S(1)} sort(s32[8192]{0:T(1024)S(1)} %multiply_add_fusion), dimensions={0}, to_apply=%region_0.0 | sort | flops 106496 | bytes 65536 | tf_op jit(solution)/shard_map/sort | solution.py:635
  7.1 0.1 pad_add_fusion
  7.2 0.1 reshape.36
  7.3 0.5 and_select_fusion.bounds
  7.8 0.8 copy.26
  8.6 0.1 copy.27
  8.7 1.0 copy-done.1
  9.7 1.0 copy-done.3
  10.7 34.8 %forward_exchange.1 = (bf16[2,2944,256]{2,1,0:T(8,128)(2,1)S(1)}, bf16[2,640,256]{2,1,0:T(8,128)(2,1)S(1)}, s32[256,128]{1,0:T(8,128)S(1)}) custom-call(bf16[640,256]{1,0:T(8,128)(2,1)S(1)} %copy-done.1, bf16[640,256]{1,0:T(8,128)(2,1)S(1)} %copy-done.3, s32[256,128]{1,0:T(8,128)S(1)} %pad.4.lists), custom_call_target="tpu_custom_call" | custom-call | tf_op jit(solution)/shard_map/forward_exchange/pallas_call | solution.py:215
  45.5 1.6 %copy-done = bf16[2,2944,256]{2,1,0:T(8,128)(2,1)} copy-done((bf16[2,2944,256]{2,1,0:T(8,128)(2,1)}, bf16[2,2944,256]{2,1,0:T(8,128)(2,1)S(1)}, u32[]{:S(2)}) %copy-start) | copy-done | bytes 3014680
  47.1 0.9 copy-done.9
  48.0 30.3 %edge_pass.1 = (bf16[2048,256]{1,0:T(8,128)(2,1)}, bf16[2,128,256]{2,1,0:T(8,128)(2,1)}, f32[640,256]{1,0:T(8,128)}, bf16[16,208,128]{2,1,0:T(8,128)(2,1)}, f32[2,640,256]{2,1,0:T(8,128)}, /*index=5*/f32[640,512]{1,0:T(8,128)}) custom-call(s32[64]{0:T(128)} %and_select_fusion.bounds, s32[64,128]{1,0:T(8,128)} %bitcast.9, bf16[2,2944,256]{2,1,0:T(8,128)(2,1)} %copy-done, ...), custom_call_target="tpu_custom_call" | custom-call | tf_op jit(solution)/shard_map/edge_pass/pallas_call | solution.py:415
  78.3 1.2 copy-done.5
  79.5 1.2 copy-done.7
  80.7 1.1 copy-done.8
  81.8 0.9 copy-done.10
  82.7 55.0 %backward_exchange.1 = (bf16[640,256]{1,0:T(8,128)(2,1)S(1)}, bf16[640,256]{1,0:T(8,128)(2,1)S(1)}, f32[512,256]{1,0:T(8,128)S(1)}, f32[512,256]{1,0:T(8,128)S(1...) custom-call(bf16[640,256]{1,0:T(8,128)(2,1)S(1)} %copy-done.2, bf16[640,256]{1,0:T(8,128)(2,1)S(1)} %copy-done.4, ...), custom_call_target="tpu_custom_call" | custom-call | tf_op jit(solution)/shard_map/backward_exchange/pallas_call | solution.py:591
  137.7 0.7 copy.34
  138.4 0.7 copy.35
  139.2 0.8 copy.36
  140.0 0.8 copy.37
  140.8 0.8 copy.38
  141.5 0.6 copy.39
  (19 shorter events, 0.1 us)
Async XLA Ops:
  7.0 41.0 %copy-start.11 = (s32[8192]{0:T(1024)}, s32[8192]{0:T(1024)S(1)}, u32[]{:S(2)}) copy-start(s32[8192]{0:T(1024)S(1)} %sort.7) | copy-start | bytes 98308
  8.7 1.0 copy-start.1
  9.7 1.0 copy-start.3
  45.5 1.6 %copy-start = (bf16[2,2944,256]{2,1,0:T(8,128)(2,1)}, bf16[2,2944,256]{2,1,0:T(8,128)(2,1)S(1)}, u32[]{:S(2)}) copy-start(bf16[2,2944,256]{2,1,0:T(8,128)(2,1)S(1)} %get-tuple-element.22.table) | copy-start | bytes 9043972
  47.1 0.9 copy-start.9
  48.0 30.3 %copy-start.2 = (bf16[640,256]{1,0:T(8,128)(2,1)S(1)}, bf16[640,256]{1,0:T(8,128)(2,1)}, u32[]{:S(2)}) copy-start(bf16[640,256]{1,0:T(8,128)(2,1)} %feats.3) | copy-start | bytes 983044
  48.0 30.3 %copy-start.4 = (bf16[640,256]{1,0:T(8,128)(2,1)S(1)}, bf16[640,256]{1,0:T(8,128)(2,1)}, u32[]{:S(2)}) copy-start(bf16[640,256]{1,0:T(8,128)(2,1)} %cot.3) | copy-start | bytes 983044
  48.0 30.3 %copy-start.6 = (bf16[512,256]{1,0:T(8,128)(2,1)S(1)}, bf16[512,256]{1,0:T(8,128)(2,1)}, u32[]{:S(2)}) copy-start(bf16[512,256]{1,0:T(8,128)(2,1)} %send_w.3) | copy-start | bytes 786436
  78.3 1.2 copy-start.5
  79.5 1.2 copy-start.7
  80.7 1.1 copy-start.8
  81.8 0.9 copy-start.10

commit v3 on v0

v3 whole, which is shorter than its diff:
```python
import functools

import jax
import jax.numpy as jnp
from jax import lax
from jax.experimental import pallas as pl
from jax.experimental.pallas import tpu as pltpu
from jax.sharding import PartitionSpec as P

HALO = 128
COARSE = 80
QUOTA = 16
ROWS = 640
HALF = 256
EDGES = 8192
NEAR = ROWS + 2 * HALO
BLOCK = 256
BLOCKS = EDGES // BLOCK
TILE = 256
SPAN = 1024
UNROLL = 11
PAIRS = EDGES // 128
RING = 8
PER = RING * QUOTA
ORDER = (0, 1, 7, 2, 6, 3, 5, 4)
GROUPS = ((0, 1), (1, 3), (3, 8))
MESH = pl.DeviceIdType.MESH
F32 = jnp.float32
BF16 = jnp.bfloat16
I32 = jnp.int32
I16 = jnp.int16
NN = (((1,), (0,)), ((), ()))
TN = (((0,), (0,)), ((), ()))
NT = (((1,), (1,)), ((), ()))


def mm(a, b, dims=NN):
    return lax.dot_general(a, b, dims, preferred_element_type=F32)


def loop(low, high, body):
    def step(i, carry):
        body(i)
        return carry

    lax.fori_loop(low, high, step, 0)


def hot(mask):
    return jnp.where(mask, BF16(1.0), BF16(0.0))


def hot32(mask):
    return jnp.where(mask, 1.0, 0.0).astype(BF16)


def down(row, rows):
    packed = jnp.broadcast_to(row, (16, 128)).astype(I16)
    return jnp.concatenate([packed] * (rows // 16), axis=0)


def rows_of(b, size=BLOCK):
    return pl.ds(pl.multiple_of(b * size, size), size)


def remote(src, dst, send, recv, patch, core):
    return pltpu.make_async_remote_copy(
        src_ref=src, dst_ref=dst, send_sem=send, recv_sem=recv,
        device_id=(patch, core), device_id_type=MESH,
    )


def sort_steps(first, last):
    return [(k, j) for k in range(first, last + 1) for j in range(k - 1, -1, -1)]


def bitonic(xs, steps):
    lane = lax.broadcasted_iota(I32, (8, 128), 1)
    sub = lax.broadcasted_iota(I32, (8, 128), 0)

    def bit(j, v):
        if j >= 13:
            return True
        if j < 3:
            return (v >> j) & 1 == 0
        if j < 6:
            return jnp.bitwise_and(sub, 1 << (j - 3)) == 0
        return jnp.bitwise_and(lane, 1 << (j - 6)) == 0

    def pick(cond, a, b):
        if isinstance(cond, bool):
            return a if cond else b
        return jnp.where(cond, a, b)

    for k, j in steps:
        out = list(xs)
        if j < 3:
            for v in range(8):
                if v & (1 << j):
                    continue
                w = v | (1 << j)
                small, large = jnp.minimum(xs[v], xs[w]), jnp.maximum(xs[v], xs[w])
                rising = bit(k, v)
                out[v], out[w] = pick(rising, small, large), pick(rising, large, small)
        else:
            axis, size, far = (0, 8, 1 << (j - 3)) if j < 6 else (1, 128, 1 << (j - 6))
            low = bit(j, 0)
            for v in range(8):
                x = xs[v]
                mate = jnp.where(low, pltpu.roll(x, size - far, axis), pltpu.roll(x, far, axis))
                rising = bit(k, v)
                if isinstance(rising, bool):
                    least = low if rising else jnp.logical_not(low)
                else:
                    least = low == rising
                out[v] = jnp.where(least, jnp.minimum(x, mate), jnp.maximum(x, mate))
        xs = out
    return xs


def layer_kernel(
    n_patch,
    sender, receiver, lists, bias, feats, cot, send_w_in, recv_w_in, out_w_in,
    updated, grad_nodes, weights_out, bias_out,
    table, cots, send_w, recv_w, out_w, asked, asked_z, coarse, packed,
    keys, turned, plan_v, plan, cols_s, cols_r, rows_k, pairs_k,
    send_s, pair_s, gsum, pre_s, gat_s, items, act_a, act_b, acc, dtab,
    far_s, rim_s, mix, mix_r, back, back_s, back_r,
    wire_a, wire_b, wire_ar, wire_br, far_r, rim_r,
    zfar_s, zfar_r, zsum_s, zsum_r, zall, plane_s, plane_all,
    loc, zs_s, zs_r, ls_s, ls_r, ps_s, ps_r, pass_s, pass_r, hs_s, hs_r, os_s, os_r,
    wa_s, wa_r, wb_s, wb_r, fb_s, fb_r, hb_s, hb_r, zf_s, zf_r, zw_s, zw_r, za_s, za_r, pa_s, pa_r,
):
    planes = n_patch // RING
    table_rows = NEAR + n_patch * QUOTA
    tiles = pl.cdiv(table_rows, TILE)
    padded = tiles * TILE
    n_items = pl.cdiv(BLOCKS + tiles - 1, UNROLL) * UNROLL
    own = slice(HALO, HALO + ROWS)
    me = lax.axis_index("patch")
    feat = lax.axis_index("feat")
    other = 1 - feat
    xy, z = lax.div(me, RING), lax.rem(me, RING)
    up = lax.rem(me + 1, n_patch)
    below = lax.rem(me + n_patch - 1, n_patch)

    def ring_peer(d):
        return xy * RING + lax.rem(z + d, RING)

    def plane_at(d):
        return lax.rem(xy + d, planes)

    def plane_from(d):
        return lax.rem(xy + planes - d, planes)

    def ring_from(d):
        return lax.rem(z + RING - d, RING)

    def arrived(at, send, recv):
        remote(at, at, send, recv, me, other).wait_recv()

    own_rows = table.at[feat, HALO : HALO + ROWS]
    local = [
        pltpu.make_async_copy(feats.at[0:COARSE], coarse.at[0, 0:COARSE], loc.at[0]),
        pltpu.make_async_copy(feats, own_rows, loc.at[1]),
        pltpu.make_async_copy(cot, cots.at[feat], loc.at[2]),
        pltpu.make_async_copy(send_w_in, send_w, loc.at[3]),
        pltpu.make_async_copy(recv_w_in, recv_w, loc.at[4]),
        pltpu.make_async_copy(out_w_in, out_w, loc.at[5]),
        pltpu.make_async_copy(lists.at[rows_of(xy, QUOTA)], asked.at[rows_of(xy, QUOTA)], loc.at[6]),
    ]
    for copy in local:
        copy.start()

    barrier = pltpu.get_barrier_semaphore()

    def greet(patch, core):
        pl.semaphore_signal(barrier, inc=1, device_id=(patch, core), device_id_type=MESH)

    loop(1, RING, lambda d: greet(ring_peer(d), feat))
    loop(1, planes, lambda d: greet(plane_at(d) * RING + z, feat))
    greet(up, feat)
    greet(below, feat)
    greet(me, other)
    pl.semaphore_wait(barrier, planes - 1 + RING - 1 + 3)

    def coarse_copy(d):
        return remote(feats.at[0:COARSE], coarse.at[RING - d, 0:COARSE], zs_s.at[d], zs_r.at[RING - d], ring_peer(d), feat)

    def list_copy(d):
        to = plane_at(d)
        return remote(lists.at[rows_of(to, QUOTA)], asked.at[rows_of(xy, QUOTA)], ls_s.at[d], ls_r.at[d], to * RING + z, feat)

    def far_rows(p, low=0, high=RING):
        return table.at[feat, pl.ds(pl.multiple_of(NEAR + p * PER + low * QUOTA, QUOTA), (high - low) * QUOTA)]

    def plane_copy(g, d):
        low, high = GROUPS[g]
        to = plane_at(d)
        return remote(
            packed.at[to, low * QUOTA : high * QUOTA], far_rows(xy, low, high), ps_s.at[g, d], ps_r.at[g, d], to * RING + z, feat
        )

    def swap(ref, slot):
        return remote(ref, ref, os_s.at[slot], os_r.at[slot], me, other)

    loop(1, planes, lambda d: list_copy(d).start())
    for d in ORDER[1:]:
        coarse_copy(d).start()
    low_rim = table.at[feat, 0:HALO]
    high_rim = table.at[feat, HALO + ROWS : NEAR]
    to_up = remote(feats.at[ROWS - HALO : ROWS], low_rim, hs_s.at[0], hs_r.at[0], up, feat)
    to_below = remote(feats.at[0:HALO], high_rim, hs_s.at[1], hs_r.at[1], below, feat)
    to_up.start()
    to_below.start()
    swap_own = remote(feats, own_rows, os_s.at[0], os_r.at[0], me, other)
    swap_cot = remote(cot, cots.at[feat], os_s.at[1], os_r.at[1], me, other)
    swap_own.start()
    swap_cot.start()

    lane32 = lax.broadcasted_iota(I32, (planes * QUOTA, HALO), 1)
    for k in range(RING):
        coarse[k, COARSE:HALO] = jnp.zeros((HALO - COARSE, HALF), BF16)

    def pack(g):
        for at in range(*GROUPS[g]):
            k = ORDER[at]
            pick = hot32(asked_z[:, k : k + 1] == lane32)
            rows = mm(pick, coarse[k]).astype(BF16)
            packed[:, at * QUOTA : (at + 1) * QUOTA, :] = rows.reshape(planes, QUOTA, HALF)
        loop(1, planes, lambda d: plane_copy(g, d).start())

    s = sender[...]
    j = s - NEAR
    away = jnp.bitwise_and(jnp.right_shift(j, 4) - z, RING - 1)
    spot = jnp.where(away <= 4, jnp.maximum(2 * away - 1, 0), 2 * RING - 2 * away)
    row = NEAR + j - jnp.bitwise_and(j, PER - 1) + spot * QUOTA + jnp.bitwise_and(j, QUOTA - 1)
    word = jnp.where(s < NEAR, s, row) * 1024 + receiver[...]
    xs = [word[8 * v : 8 * v + 8] for v in range(8)]

    local[6].wait()
    loop(1, planes, lambda d: arrived(asked.at[rows_of(plane_from(d), QUOTA)], ls_s.at[d], ls_r.at[d]))
    asked_z[...] = pltpu.roll(asked[...], lax.rem(128 - z, 128), 1)
    local[0].wait()
    pack(0)
    for k in ORDER[1:3]:
        arrived(coarse.at[k, 0:COARSE], zs_s.at[k], zs_r.at[k])
    pack(1)
    xs = bitonic(xs, sort_steps(1, 9))
    for k in ORDER[3:]:
        arrived(coarse.at[k, 0:COARSE], zs_s.at[k], zs_r.at[k])
    pack(2)
    own_far = pltpu.make_async_copy(packed.at[xy], far_rows(xy), loc.at[7])
    own_far.start()
    swap_far = remote(packed.at[xy], far_rows(xy), pass_s.at[0], pass_r.at[0], me, other)
    swap_far.start()
    xs = bitonic(xs, sort_steps(10, 13))

    for v in range(8):
        keys[8 * v : 8 * v + 8, :] = xs[v]
    flat = keys[...]
    turned[...] = jnp.transpose(jnp.concatenate([flat, flat], axis=0))
    lane64 = lax.broadcasted_iota(I32, (PAIRS, 128), 1)
    rows_k[...] = jnp.where(
        lane64 < 64, turned[pl.ds(0, PAIRS, stride=2), :], turned[pl.ds(1, PAIRS, stride=2), :]
    )
    for r in range(128):
        spread = jnp.broadcast_to(flat[:, r : r + 1], (64, 128))
        rows = slice(64 * (r % 4), 64 * (r % 4) + 64)
        cols_s[r // 4, rows, :] = jnp.right_shift(spread, 10).astype(I16)
        cols_r[r // 4, rows, :] = jnp.bitwise_and(spread, 1023).astype(I16)
    for b in range(BLOCKS):
        pairs_k[b] = jnp.concatenate([rows_k[2 * b : 2 * b + 2, :], jnp.zeros((6, 128), I32)], axis=0)

    tall = lax.broadcasted_iota(I32, (128, 128), 0)
    wide = lax.broadcasted_iota(I32, (128, 128), 1)
    heads = jnp.logical_and(jnp.bitwise_and(tall, 3) == 0, tall > 0)
    first_tile = jnp.right_shift(jnp.broadcast_to(turned[:, 0:1], (128, 128)), 18)
    first_item = first_tile + jnp.right_shift(tall, 2)
    block_of = jnp.sum(jnp.where(jnp.logical_and(heads, first_item <= wide), 1, 0), axis=0, keepdims=True)
    last_of = jnp.sum(jnp.where(jnp.logical_and(heads, first_tile <= wide), 1, 0), axis=0, keepdims=True) + wide[0:1]
    first_of = jnp.right_shift(flat[0:1], 18) + jnp.right_shift(wide[0:1], 2)
    plan_v[...] = jnp.concatenate([block_of, last_of, first_of, jnp.zeros((5, 128), I32)], axis=0)
    to_scalars = pltpu.make_async_copy(plan_v, plan, loc.at[8])
    to_scalars.start()
    to_scalars.wait()

    for copy in local[1:6]:
        copy.wait()
    swap_own.wait()
    swap_cot.wait()
    pair_s[:, 0:HALF] = (
        mm(table[0, own, :], recv_w[0:HALF, :]) + mm(table[1, own, :], recv_w[HALF:, :]) + bias[...]
    ).astype(BF16)
    grad_sum = mm(cots[0], out_w[:, 0:HALF], NT) + mm(cots[1], out_w[:, HALF:], NT)
    gsum[...] = grad_sum
    pair_s[:, HALF:] = grad_sum.astype(BF16)
    acc[...] = jnp.zeros_like(acc)
    lane = lax.broadcasted_iota(I32, (BLOCK, 128), 1).astype(I16)
    sub = lax.broadcasted_iota(I32, (ROWS, 128), 0).astype(I16)
    sub_t = lax.broadcasted_iota(I32, (TILE, 128), 0).astype(I16)

    def receive(i):
        for u in range(4):
            b = 4 * i + u
            col = cols_r[b]
            pick = jnp.concatenate([hot(col == lane + I16(128 * m)) for m in range(ROWS // 128)], axis=1)
            both = mm(pick, pair_s[...])
            pre_s[b] = both[:, 0:HALF]
            gat_s[b] = both[:, HALF:].astype(BF16)

    loop(0, BLOCKS // 4, receive)

    def pass_on(p, slot):
        return remote(far_rows(p), far_rows(p), pass_s.at[slot], pass_r.at[slot], me, other)

    to_up.wait()
    swap(low_rim, 2).start()
    to_below.wait()
    swap(high_rim, 3).start()

    def hand_on(d):
        for g, (low, high) in enumerate(GROUPS):
            arrived(far_rows(plane_from(d), low, high), ps_s.at[g, d], ps_r.at[g, d])
        pass_on(plane_from(d), d).start()

    loop(1, planes, hand_on)
    own_far.wait()
    swap_far.wait()
    swap(low_rim, 2).wait()
    swap(high_rim, 3).wait()
    loop(1, planes, lambda d: pass_on(plane_from(d), d).wait())

    size = 736 if table_rows % 736 == 0 else 128
    for start in range(0, table_rows, size):
        part = slice(start, start + size)
        value = (mm(table[0, part, :], send_w[0:HALF, :]) + mm(table[1, part, :], send_w[HALF:, :])).astype(BF16)
        at = 0
        while at < size:
            t, r = divmod(start + at, TILE)
            count = min(TILE - r, size - at)
            send_s[t, r : r + count, :] = value[at : at + count]
            at += count
    if padded > table_rows:
        send_s[tiles - 1, table_rows - padded + TILE :, :] = jnp.zeros((padded - table_rows, HALF), BF16)
    send_s[tiles] = jnp.zeros((TILE, HALF), BF16)

    def gather(i):
        for u in range(UNROLL):
            at = i * UNROLL + u
            b = plan[0, at]
            before = plan[0, jnp.maximum(at - 1, 0)]
            t = at - b
            col = cols_s[b] - jnp.full((BLOCK, 128), t * TILE, I32).astype(I16)
            pick = jnp.concatenate([hot(col == lane), hot(col == lane + I16(128))], axis=1)
            part = mm(pick, send_s[t])
            keep = 1.0 - (b - before).astype(F32)
            items[at] = part + keep * items[jnp.maximum(at - 1, 0)]

    items[0] = jnp.zeros((BLOCK, HALF), F32)
    loop(0, n_items // UNROLL, gather)

    def messages(i, act):
        for u in range(SPAN // BLOCK):
            b = i * (SPAN // BLOCK) + u
            last = jnp.where(b == BLOCKS - 1, BLOCKS + tiles - 1, plan[2, jnp.minimum(4 * b + 4, 127)]) - 1
            pre = pre_s[b] + items[last]
            sig = 0.5 * jnp.tanh(0.5 * pre) + 0.5
            hidden = pre * sig
            slope = sig + hidden * (1.0 - sig)
            act[u * BLOCK : (u + 1) * BLOCK, 0:HALF] = hidden.astype(BF16)
            act[u * BLOCK : (u + 1) * BLOCK, HALF:] = slope.astype(BF16)
            gat_s[b] = (gat_s[b].astype(F32) * slope).astype(BF16)

    def collect(i, act):
        words = jnp.bitwise_and(rows_k[rows_of(i, SPAN // 128), :], 1023)
        spread = jnp.concatenate([hot(sub == down(words[m : m + 1], ROWS)) for m in range(SPAN // 128)], axis=1)
        acc[...] += mm(spread, act[...])

    act_b[...] = jnp.zeros_like(act_b)

    def two_spans(i):
        messages(2 * i, act_a)
        collect(jnp.maximum(2 * i - 1, 0), act_b)
        messages(2 * i + 1, act_b)
        collect(2 * i, act_a)

    loop(0, EDGES // SPAN // 2, two_spans)
    collect(EDGES // SPAN - 1, act_b)

    edge_sum = acc[:, 0:HALF].astype(BF16)
    mixed = mm(edge_sum, out_w[...])
    mix[0] = mixed[:, 0:HALF]
    mix[1] = mixed[:, HALF:]
    swap_mix = remote(mix.at[other], mix_r, os_s.at[4], os_r.at[4], me, other)
    swap_mix.start()
    recv_grad = gsum[...] * acc[:, HALF:]
    bias_part = jnp.sum(recv_grad, axis=0, keepdims=True)
    recv_grad_b = recv_grad.astype(BF16)

    chunk_a, chunk_b = 2048 // planes, 1024 // planes

    def put(wire, chunk, start, value):
        value = value.astype(BF16)
        for m in range(value.shape[1] // 128):
            at = 0
            while at < value.shape[0]:
                c, r = divmod(start + m * value.shape[0] + at, chunk)
                count = min(chunk - r, value.shape[0] - at)
                wire[c, r : r + count, :] = value[at : at + count, m * 128 : (m + 1) * 128]
                at += count

    put(
        wire_a, chunk_a, 0,
        jnp.concatenate([mm(table[0, own, :], recv_grad_b, TN), mm(table[1, own, :], recv_grad_b, TN)], axis=0),
    )
    put(wire_a, chunk_a, 1024, jnp.concatenate([mm(edge_sum, cots[0], TN), mm(edge_sum, cots[1], TN)], axis=1))
    sub16 = lax.broadcasted_iota(I32, (16, 128), 0)
    tail = jnp.where(sub16 == 0, bias_part[:, 0:128], jnp.where(sub16 == 1, bias_part[:, 128:], 0.0)).astype(BF16)
    for c in range(planes):
        wire_a[c, chunk_a : chunk_a + 16, :] = tail

    def wire_copy(src, dst, send, recv, d):
        to = plane_at(d)
        return remote(src.at[to], dst.at[xy], send.at[d], recv.at[d], to * RING + z, feat)

    loop(1, planes, lambda d: wire_copy(wire_a, wire_ar, wa_s, wa_r, d).start())
    wire_ar[xy] = wire_a[xy]

    def scatter(i):
        for u in range(UNROLL):
            at = i * UNROLL + u
            b = plan[0, at]
            before = plan[0, jnp.maximum(at - 1, 0)]
            t = at - b
            words = jnp.right_shift(pairs_k[b], 10) - t * TILE
            spread = jnp.concatenate([hot(sub_t == down(words[0:1], TILE)), hot(sub_t == down(words[1:2], TILE))], axis=1)
            part = mm(spread, gat_s[b])
            keep = (b - before).astype(F32)
            items[at] = part + keep * items[jnp.maximum(at - 1, 0)]

    items[0] = jnp.zeros((BLOCK, HALF), F32)
    loop(0, n_items // UNROLL, scatter)
    for t in range(tiles):
        dtab[t * TILE : (t + 1) * TILE, :] = items[plan[1, t]]

    dtab_b = dtab[0:table_rows, :].astype(BF16)
    put(wire_b, chunk_b, 0, jnp.concatenate([mm(table[0], dtab_b, TN), mm(table[1], dtab_b, TN)], axis=0))
    loop(1, planes, lambda d: wire_copy(wire_b, wire_br, wb_s, wb_r, d).start())
    wire_br[xy] = wire_b[xy]
    rim_s[0] = dtab[0:HALO, :].astype(BF16)
    rim_s[1] = dtab[HALO + ROWS : NEAR, :].astype(BF16)
    back_below = remote(rim_s.at[0], rim_r.at[1], hb_s.at[0], hb_r.at[0], below, feat)
    back_up = remote(rim_s.at[1], rim_r.at[0], hb_s.at[1], hb_r.at[1], up, feat)
    back_below.start()
    back_up.start()
    far_s[...] = dtab[NEAR:table_rows, :].astype(BF16)

    def far_copy(d):
        to = plane_at(d)
        return remote(far_s.at[rows_of(to, PER)], far_r.at[xy], fb_s.at[d], fb_r.at[d], to * RING + z, feat)

    loop(1, planes, lambda d: far_copy(d).start())
    far_r[xy] = far_s[rows_of(xy, PER), :]
    back[...] = mm(recv_grad_b, recv_w[...], NT)
    swap_mix.wait()
    updated[...] = (table[feat, own, :].astype(F32) + mix[feat] + mix_r[...]).astype(BF16)

    part_a, part_b = chunk_a // RING, chunk_b // RING
    part = part_a + part_b
    loop(1, planes, lambda d: arrived(wire_ar.at[plane_from(d)], wa_s.at[d], wa_r.at[d]))
    total = wire_ar[0].astype(F32)
    for p in range(1, planes):
        total = total + wire_ar[p].astype(F32)
    for k in range(RING):
        zsum_s[k, 0:part_a, :] = total[k * part_a : (k + 1) * part_a, :]
        zsum_s[k, part : part + 8, :] = total[chunk_a : chunk_a + 8, :]
    loop(1, planes, lambda d: arrived(wire_br.at[plane_from(d)], wb_s.at[d], wb_r.at[d]))
    total = wire_br[0].astype(F32)
    for p in range(1, planes):
        total = total + wire_br[p].astype(F32)
    for k in range(RING):
        zsum_s[k, part_a:part, :] = total[k * part_b : (k + 1) * part_b, :]

    def zsum_copy(d):
        to = lax.rem(z + d, RING)
        return remote(zsum_s.at[to], zsum_r.at[z], zw_s.at[d], zw_r.at[d], ring_peer(d), feat)

    loop(1, RING, lambda d: zsum_copy(d).start())
    zsum_r[z] = zsum_s[z]
    loop(1, RING, lambda d: arrived(zsum_r.at[ring_from(d)], zw_s.at[d], zw_r.at[d]))
    whole = zsum_r[0]
    for k in range(1, RING):
        whole = whole + zsum_r[k]
    bias_out[...] = jnp.concatenate([whole[part : part + 1], whole[part + 1 : part + 2]], axis=1)
    zall[z] = whole[0:part]

    def zall_copy(d):
        return remote(zall.at[z], zall.at[z], za_s.at[d], za_r.at[d], ring_peer(d), feat)

    loop(1, RING, lambda d: zall_copy(d).start())
    loop(1, RING, lambda d: arrived(zall.at[ring_from(d)], za_s.at[d], za_r.at[d]))
    for k in range(RING):
        plane_s[k * part_a : (k + 1) * part_a, :] = zall[k, 0:part_a, :].astype(BF16)
    plane_s[chunk_a:, :] = zall[:, part_a:part, :].reshape(chunk_b, 128).astype(BF16)

    def all_copy(d):
        return remote(plane_s, plane_all.at[xy], pa_s.at[d], pa_r.at[d], plane_at(d) * RING + z, feat)

    loop(1, planes, lambda d: all_copy(d).start())
    plane_all[xy] = plane_s[...]

    loop(1, planes, lambda d: arrived(far_r.at[plane_from(d)], fb_s.at[d], fb_r.at[d]))
    for at in range(RING):
        k = ORDER[at]
        pick = hot32(asked_z[:, k : k + 1] == lane32)
        rows = far_r[:, at * QUOTA : (at + 1) * QUOTA, :].reshape(planes * QUOTA, HALF)
        zfar_s[k] = mm(pick, rows, TN)[0:COARSE].astype(BF16)

    def zfar_copy(d):
        return remote(zfar_s.at[d], zfar_r.at[d], zf_s.at[d], zf_r.at[d], ring_peer(d), feat)

    loop(1, RING, lambda d: zfar_copy(d).start())
    zfar_r[0] = zfar_s[0]
    back_below.wait()
    back_up.wait()
    loop(1, RING, lambda d: arrived(zfar_r.at[d], zf_s.at[d], zf_r.at[d]))
    head = zfar_r[0].astype(F32)
    for k in range(1, RING):
        head = head + zfar_r[k].astype(F32)
    head = head + dtab[HALO : HALO + COARSE, :] + rim_r[0, 0:COARSE, :].astype(F32)
    rest = dtab[HALO + COARSE : 2 * HALO, :] + rim_r[0, COARSE:HALO, :].astype(F32)
    end = dtab[ROWS : ROWS + HALO, :] + rim_r[1].astype(F32)
    send_grad = jnp.concatenate([head, rest, dtab[2 * HALO : ROWS, :], end], axis=0).astype(BF16)
    terms = back[...] + mm(send_grad, send_w[...], NT)
    back_s[0] = terms[:, 0:HALF]
    back_s[1] = terms[:, HALF:]
    swap_back = remote(back_s.at[other], back_r, os_s.at[5], os_r.at[5], me, other)
    swap_back.start()
    swap_back.wait()
    grad_nodes[...] = (cots[feat].astype(F32) + back_s[feat] + back_r[...]).astype(BF16)

    loop(1, planes, lambda d: arrived(plane_all.at[plane_from(d)], pa_s.at[d], pa_r.at[d]))
    weights_out[...] = plane_all[...]

    loop(1, planes, lambda d: list_copy(d).wait_send())
    loop(1, RING, lambda d: coarse_copy(d).wait_send())
    for g in range(len(GROUPS)):
        loop(1, planes, lambda d: plane_copy(g, d).wait_send())
    loop(1, planes, lambda d: wire_copy(wire_a, wire_ar, wa_s, wa_r, d).wait_send())
    loop(1, planes, lambda d: wire_copy(wire_b, wire_br, wb_s, wb_r, d).wait_send())
    loop(1, planes, lambda d: far_copy(d).wait_send())
    loop(1, planes, lambda d: all_copy(d).wait_send())
    loop(1, RING, lambda d: zsum_copy(d).wait_send())
    loop(1, RING, lambda d: zall_copy(d).wait_send())
    loop(1, RING, lambda d: zfar_copy(d).wait_send())


def layer(n_patch, *args):
    planes = n_patch // RING
    table_rows = NEAR + n_patch * QUOTA
    tiles = pl.cdiv(table_rows, TILE)
    padded = tiles * TILE
    n_items = pl.cdiv(BLOCKS + tiles - 1, UNROLL) * UNROLL
    chunk_a, chunk_b = 2048 // planes, 1024 // planes
    part = (chunk_a + chunk_b) // RING
    vmem = pl.BlockSpec(memory_space=pltpu.VMEM)
    anyspace = pl.BlockSpec(memory_space=pl.ANY)
    dma = pltpu.SemaphoreType.DMA

    def both(*shape):
        return [dma(shape), dma(shape)]

    return pl.pallas_call(
        functools.partial(layer_kernel, n_patch),
        out_shape=(
            jax.ShapeDtypeStruct((ROWS, HALF), BF16),
            jax.ShapeDtypeStruct((ROWS, HALF), BF16),
            jax.ShapeDtypeStruct((planes, chunk_a + chunk_b, 128), BF16),
            jax.ShapeDtypeStruct((1, HALF), F32),
        ),
        in_specs=[vmem] * 4 + [anyspace] * 5,
        out_specs=(vmem,) * 4,
        scratch_shapes=[
            pltpu.VMEM((2, table_rows, HALF), BF16),
            pltpu.VMEM((2, ROWS, HALF), BF16),
            pltpu.VMEM((2 * HALF, HALF), BF16),
            pltpu.VMEM((2 * HALF, HALF), BF16),
            pltpu.VMEM((HALF, 2 * HALF), BF16),
            pltpu.VMEM((planes * QUOTA, 128), I32),
            pltpu.VMEM((planes * QUOTA, 128), I32),
            pltpu.VMEM((RING, HALO, HALF), BF16),
            pltpu.VMEM((planes, PER, HALF), BF16),
            pltpu.VMEM((PAIRS, 128), I32),
            pltpu.VMEM((128, 128), I32),
            pltpu.VMEM((8, 128), I32),
            pltpu.SMEM((8, 128), I32),
            pltpu.VMEM((BLOCKS, BLOCK, 128), I16),
            pltpu.VMEM((BLOCKS, BLOCK, 128), I16),
            pltpu.VMEM((PAIRS, 128), I32),
            pltpu.VMEM((BLOCKS, 8, 128), I32),
            pltpu.VMEM((tiles + 1, TILE, HALF), BF16),
            pltpu.VMEM((ROWS, 2 * HALF), BF16),
            pltpu.VMEM((ROWS, HALF), F32),
            pltpu.VMEM((BLOCKS, BLOCK, HALF), F32),
            pltpu.VMEM((BLOCKS, BLOCK, HALF), BF16),
            pltpu.VMEM((n_items, BLOCK, HALF), F32),
            pltpu.VMEM((SPAN, 2 * HALF), BF16),
            pltpu.VMEM((SPAN, 2 * HALF), BF16),
            pltpu.VMEM((ROWS, 2 * HALF), F32),
            pltpu.VMEM((padded, HALF), F32),
            pltpu.VMEM((n_patch * QUOTA, HALF), BF16),
            pltpu.VMEM((2, HALO, HALF), BF16),
            pltpu.VMEM((2, ROWS, HALF), F32),
            pltpu.VMEM((ROWS, HALF), F32),
            pltpu.VMEM((ROWS, 2 * HALF), F32),
            pltpu.VMEM((2, ROWS, HALF), F32),
            pltpu.VMEM((ROWS, HALF), F32),
            pltpu.VMEM((planes, chunk_a + 16, 128), BF16),
            pltpu.VMEM((planes, chunk_b, 128), BF16),
            pltpu.VMEM((planes, chunk_a + 16, 128), BF16),
            pltpu.VMEM((planes, chunk_b, 128), BF16),
            pltpu.VMEM((planes, PER, HALF), BF16),
            pltpu.VMEM((2, HALO, HALF), BF16),
            pltpu.VMEM((RING, COARSE, HALF), BF16),
            pltpu.VMEM((RING, COARSE, HALF), BF16),
            pltpu.VMEM((RING, part + 8, 128), F32),
            pltpu.VMEM((RING, part + 8, 128), F32),
            pltpu.VMEM((RING, part, 128), F32),
            pltpu.VMEM((chunk_a + chunk_b, 128), BF16),
            pltpu.VMEM((planes, chunk_a + chunk_b, 128), BF16),
            dma((9,)),
            *both(RING), *both(planes), *both(len(GROUPS), planes), *both(planes), *both(2), *both(6),
            *both(planes), *both(planes), *both(planes), *both(2), *both(RING), *both(RING), *both(RING), *both(planes),
        ],
        compiler_params=pltpu.CompilerParams(
            collective_id=0, has_side_effects=True, vmem_limit_bytes=60 * 2**20
        ),
        name="layer",
    )(*args)


def finish_kernel(chunk_a, updated, grad_nodes, weights, bias, updated_o, grad_nodes_o, g_send, g_recv, g_out, g_bias):
    updated_o[...] = updated[...]
    grad_nodes_o[...] = grad_nodes[...]
    g_bias[...] = bias[...]
    planes, chunk, _ = weights.shape
    chunk_b = chunk - chunk_a
    a = weights[:, 0:chunk_a, :].reshape(planes * chunk_a, 128).astype(F32)
    b = weights[:, chunk_a:, :].reshape(planes * chunk_b, 128).astype(F32)
    for m in range(2):
        lanes = slice(128 * m, 128 * (m + 1))
        g_recv[:, lanes] = a[512 * m : 512 * (m + 1)]
        g_send[:, lanes] = b[512 * m : 512 * (m + 1)]
    for m in range(4):
        g_out[:, 128 * m : 128 * (m + 1)] = a[1024 + 256 * m : 1024 + 256 * (m + 1)]


def finish(n_patch, *args):
    vmem = pl.BlockSpec(memory_space=pltpu.VMEM)
    return pl.pallas_call(
        functools.partial(finish_kernel, 2048 // (n_patch // RING)),
        out_shape=(
            jax.ShapeDtypeStruct((ROWS, HALF), BF16),
            jax.ShapeDtypeStruct((ROWS, HALF), BF16),
            jax.ShapeDtypeStruct((2 * HALF, HALF), F32),
            jax.ShapeDtypeStruct((2 * HALF, HALF), F32),
            jax.ShapeDtypeStruct((HALF, 2 * HALF), F32),
            jax.ShapeDtypeStruct((1, HALF), F32),
        ),
        in_specs=[vmem] * 4,
        out_specs=(vmem,) * 6,
        compiler_params=pltpu.CompilerParams(vmem_limit_bytes=32 * 2**20),
        name="finish",
    )(*args)


def shards(n_patch, feats, cot, send_w, recv_w, out_w, bias, sender, receiver, wanted):
    planes = n_patch // RING
    lists = wanted.reshape(planes, RING, QUOTA).transpose(0, 2, 1).reshape(planes * QUOTA, RING)
    lists = jnp.pad(jnp.concatenate([lists, lists], axis=1), ((0, 0), (0, 128 - 2 * RING)))
    parts = layer(
        n_patch, sender.reshape(PAIRS, 128), receiver.reshape(PAIRS, 128), lists, bias.reshape(1, HALF),
        feats, cot, send_w, recv_w, out_w,
    )
    updated, grad_nodes, g_send, g_recv, g_out, g_bias = finish(n_patch, *parts)
    return (updated, grad_nodes, g_send, g_recv, g_out, g_bias.reshape(HALF))


def solution(mesh):
    n_patch = mesh.shape["patch"]
    in_specs = (
        P("patch", "feat"),
        P("patch", "feat"),
        P(None, "feat"),
        P(None, "feat"),
        P("feat", None),
        P("feat"),
        P("patch"),
        P("patch"),
        P("patch", None, None),
    )
    out_specs = (
        P("patch", "feat"),
        P("patch", "feat"),
        P(None, "feat"),
        P(None, "feat"),
        P("feat", None),
        P("feat"),
    )
    return jax.shard_map(
        functools.partial(shards, n_patch), mesh=mesh, in_specs=in_specs, out_specs=out_specs, check_vma=False
    )
```

time: 1330 us -> 109 us (0.08)
  the two profiles are of different devices: /device:TPU:8 before, /device:TPU:3 now
where the time goes in v3:
time: 109 us
  Pallas kernels  103 us (94%)
  local copies, waits for them, and re-layouts  5.34 us (5%)
    pallas_call x1, Pallas kernels, layer(): pl.pallas_call(functools.partial(layer_kernel, n_patch), out_shape=(jax.S...  101 us
    unnamed x9, local copies, waits for them, and re-layouts  4.47 us

profile of v3, /device:TPU:3, one launch (start us, length us, event | category | flops | bytes accessed | tf_op | source)
XLA Modules:
  0.0 108.8 jit_solution(1933039746454851344)
XLA Ops:
  0.6 0.8 copy.20
  1.4 0.1 reshape.33
  1.5 0.1 copy.22
  1.6 0.7 pad.4.lists
  2.3 101.3 %layer.1 = (bf16[640,256]{1,0:T(8,128)(2,1)}, bf16[640,256]{1,0:T(8,128)(2,1)}, bf16[16,192,128]{2,1,0:T(8,128)(2,1)}, f32[1,256]{1,0:T(1,128)}) custom-call(s32[64,128]{1,0:T(8,128)} %bitcast.10, s32[64,128]{1,0:T(8,128)} %bitcast.11, s32[256,128]{1,0:T(8,128)} %pad.4.lists, f32[1,256]{1,0:T(1,128)} %bitcast.12, bf16[640,256]{1,0:T(8,128)(2,1)} %feats.1, ...), custom_call_target="tpu_custom_call" | custom-call | tf_op jit(solution)/shard_map/layer/pallas_call | solution.py:574
  103.7 0.0 copy-start.3
  103.7 0.6 copy-done.3
  104.3 0.0 copy-start
  104.3 1.1 %copy-done = bf16[16,192,128]{2,1,0:T(8,128)(2,1)S(1)} copy-done((bf16[16,192,128]{2,1,0:T(8,128)(2,1)S(1)}, bf16[16,192,128]{2,1,0:T(8,128)(2,1)}, u32[]{:S(2)}) %copy-start) | copy-done | bytes 786456
  105.4 0.0 copy-start.1
  105.4 1.0 copy-done.1
  106.4 0.0 copy-start.2
  106.4 1.0 copy-done.2
  107.3 1.5 %finish.1 = (bf16[640,256]{1,0:T(8,128)(2,1)}, bf16[640,256]{1,0:T(8,128)(2,1)}, f32[512,256]{1,0:T(8,128)}, f32[512,256]{1,0:T(8,128)}, f32[256,512]{1,0:T(8,128)}, /*index=5*/f32[1,256]{1,0:T(1,128)}) custom-call(bf16[640,256]{1,0:T(8,128)(2,1)S(1)} %copy-done.1, bf16[640,256]{1,0:T(8,128)(2,1)S(1)} %copy-done.2, bf16[16,192,128]{2,1,0:T(8,128)(2,1)S(1)} %copy-done, ...), custom_call_target="tpu_custom_call" | custom-call | tf_op jit(solution)/shard_map/finish/pallas_call | solution.py:661
  (2 shorter events, 0.0 us)
Async XLA Ops:
  103.7 0.6 copy-start.3
  104.3 1.1 %copy-start = (bf16[16,192,128]{2,1,0:T(8,128)(2,1)S(1)}, bf16[16,192,128]{2,1,0:T(8,128)(2,1)}, u32[]{:S(2)}) copy-start(bf16[16,192,128]{2,1,0:T(8,128)(2,1)} %get-tuple-element.18.weights) | copy-start | bytes 2359300
  105.4 1.0 copy-start.1
  106.4 1.0 copy-start.2

commit v4 on v3

--- a/solution.py
+++ b/solution.py
@@ -24,6 +24,7 @@
 PER = RING * QUOTA
 ORDER = (0, 1, 7, 2, 6, 3, 5, 4)
 GROUPS = ((0, 1), (1, 3), (3, 8))
+HALVES = ((0, 3), (3, 8))
 MESH = pl.DeviceIdType.MESH
 F32 = jnp.float32
 BF16 = jnp.bfloat16
@@ -120,16 +121,16 @@
 
 def layer_kernel(
     n_patch,
-    sender, receiver, lists, bias, feats, cot, send_w_in, recv_w_in, out_w_in,
-    updated, grad_nodes, weights_out, bias_out,
+    sender, receiver, wanted, bias, feats, cot, send_w_in, recv_w_in, out_w_in,
+    updated, grad_nodes, plane_all, bias_out,
     table, cots, send_w, recv_w, out_w, asked, asked_z, coarse, packed,
-    keys, turned, plan_v, plan, cols_s, cols_r, rows_k, pairs_k,
+    lists, keys, turned, plan_v, plan, cols_s, cols_r, rows_k, pairs_k,
     send_s, pair_s, gsum, pre_s, gat_s, items, act_a, act_b, acc, dtab,
     far_s, rim_s, mix, mix_r, back, back_s, back_r,
     wire_a, wire_b, wire_ar, wire_br, far_r, rim_r,
-    zfar_s, zfar_r, zsum_s, zsum_r, zall, plane_s, plane_all,
+    zfar_s, zfar_r, zsum_s, zsum_r, zall, plane_s, psum_s, psum_r, updated_v, nodes_v,
     loc, zs_s, zs_r, ls_s, ls_r, ps_s, ps_r, pass_s, pass_r, hs_s, hs_r, os_s, os_r,
-    wa_s, wa_r, wb_s, wb_r, fb_s, fb_r, hb_s, hb_r, zf_s, zf_r, zw_s, zw_r, za_s, za_r, pa_s, pa_r,
+    wa_s, wa_r, wb_s, wb_r, fb_s, fb_r, hb_s, hb_r, zf_s, zf_r, zw_s, zw_r, za_s, za_r, pa_s, pa_r, pb_s, pb_r,
 ):
     planes = n_patch // RING
     table_rows = NEAR + n_patch * QUOTA
@@ -167,7 +168,6 @@
         pltpu.make_async_copy(send_w_in, send_w, loc.at[3]),
         pltpu.make_async_copy(recv_w_in, recv_w, loc.at[4]),
         pltpu.make_async_copy(out_w_in, out_w, loc.at[5]),
-        pltpu.make_async_copy(lists.at[rows_of(xy, QUOTA)], asked.at[rows_of(xy, QUOTA)], loc.at[6]),
     ]
     for copy in local:
         copy.start()
@@ -182,6 +182,12 @@
     greet(up, feat)
     greet(below, feat)
     greet(me, other)
+
+    grid = wanted[...]
+    lane_q = lax.broadcasted_iota(I32, (QUOTA, 128), 1)
+    for p in range(planes):
+        first = pltpu.roll(grid, (128 - RING * p) % 128, 1) if p else grid
+        lists[p * QUOTA : (p + 1) * QUOTA, :] = jnp.where(lane_q < RING, first, pltpu.roll(first, RING, 1))
     pl.semaphore_wait(barrier, planes - 1 + RING - 1 + 3)
 
     def coarse_copy(d):
@@ -238,7 +244,10 @@
     word = jnp.where(s < NEAR, s, row) * 1024 + receiver[...]
     xs = [word[8 * v : 8 * v + 8] for v in range(8)]
 
-    local[6].wait()
+    xs = bitonic(xs, sort_steps(1, 13))
+    for v in range(8):
+        keys[8 * v : 8 * v + 8, :] = xs[v]
+    asked[rows_of(xy, QUOTA), :] = lists[rows_of(xy, QUOTA), :]
     loop(1, planes, lambda d: arrived(asked.at[rows_of(plane_from(d), QUOTA)], ls_s.at[d], ls_r.at[d]))
     asked_z[...] = pltpu.roll(asked[...], lax.rem(128 - z, 128), 1)
     local[0].wait()
@@ -246,18 +255,6 @@
     for k in ORDER[1:3]:
         arrived(coarse.at[k, 0:COARSE], zs_s.at[k], zs_r.at[k])
     pack(1)
-    xs = bitonic(xs, sort_steps(1, 9))
-    for k in ORDER[3:]:
-        arrived(coarse.at[k, 0:COARSE], zs_s.at[k], zs_r.at[k])
-    pack(2)
-    own_far = pltpu.make_async_copy(packed.at[xy], far_rows(xy), loc.at[7])
-    own_far.start()
-    swap_far = remote(packed.at[xy], far_rows(xy), pass_s.at[0], pass_r.at[0], me, other)
-    swap_far.start()
-    xs = bitonic(xs, sort_steps(10, 13))
-
-    for v in range(8):
-        keys[8 * v : 8 * v + 8, :] = xs[v]
     flat = keys[...]
     turned[...] = jnp.transpose(jnp.concatenate([flat, flat], axis=0))
     lane64 = lax.broadcasted_iota(I32, (PAIRS, 128), 1)
@@ -283,9 +280,17 @@
     plan_v[...] = jnp.concatenate([block_of, last_of, first_of, jnp.zeros((5, 128), I32)], axis=0)
     to_scalars = pltpu.make_async_copy(plan_v, plan, loc.at[8])
     to_scalars.start()
+
+    for k in ORDER[3:]:
+        arrived(coarse.at[k, 0:COARSE], zs_s.at[k], zs_r.at[k])
+    pack(2)
+    own_far = pltpu.make_async_copy(packed.at[xy], far_rows(xy), loc.at[7])
+    own_far.start()
+    swap_far = remote(packed.at[xy], far_rows(xy), pass_s.at[0, 0], pass_r.at[0, 0], me, other)
+    swap_far.start()
     to_scalars.wait()
 
-    for copy in local[1:6]:
+    for copy in local[1:]:
         copy.wait()
     swap_own.wait()
     swap_cot.wait()
@@ -309,30 +314,34 @@
             pre_s[b] = both[:, 0:HALF]
             gat_s[b] = both[:, HALF:].astype(BF16)
 
-    loop(0, BLOCKS // 4, receive)
-
-    def pass_on(p, slot):
-        return remote(far_rows(p), far_rows(p), pass_s.at[slot], pass_r.at[slot], me, other)
+    loop(0, BLOCKS // 8, receive)
+
+    def pass_on(p, half, slot):
+        low, high = HALVES[half]
+        return remote(far_rows(p, low, high), far_rows(p, low, high), pass_s.at[half, slot], pass_r.at[half, slot], me, other)
+
+    def arrive(g, d):
+        low, high = GROUPS[g]
+        arrived(far_rows(plane_from(d), low, high), ps_s.at[g, d], ps_r.at[g, d])
+
+    def hand_first(d):
+        arrive(0, d)
+        arrive(1, d)
+        pass_on(plane_from(d), 0, d).start()
+
+    def hand_second(d):
+        arrive(2, d)
+        pass_on(plane_from(d), 1, d).start()
 
     to_up.wait()
     swap(low_rim, 2).start()
     to_below.wait()
     swap(high_rim, 3).start()
-
-    def hand_on(d):
-        for g, (low, high) in enumerate(GROUPS):
-            arrived(far_rows(plane_from(d), low, high), ps_s.at[g, d], ps_r.at[g, d])
-        pass_on(plane_from(d), d).start()
-
-    loop(1, planes, hand_on)
-    own_far.wait()
-    swap_far.wait()
-    swap(low_rim, 2).wait()
-    swap(high_rim, 3).wait()
-    loop(1, planes, lambda d: pass_on(plane_from(d), d).wait())
-
-    size = 736 if table_rows % 736 == 0 else 128
-    for start in range(0, table_rows, size):
+    loop(1, planes, hand_first)
+    loop(BLOCKS // 8, BLOCKS // 4, receive)
+    loop(1, planes, hand_second)
+
+    def project(start, size):
         part = slice(start, start + size)
         value = (mm(table[0, part, :], send_w[0:HALF, :]) + mm(table[1, part, :], send_w[HALF:, :])).astype(BF16)
         at = 0
@@ -341,9 +350,19 @@
             count = min(TILE - r, size - at)
             send_s[t, r : r + count, :] = value[at : at + count]
             at += count
+
+    swap(low_rim, 2).wait()
+    swap(high_rim, 3).wait()
+    project(0, NEAR)
     if padded > table_rows:
         send_s[tiles - 1, table_rows - padded + TILE :, :] = jnp.zeros((padded - table_rows, HALF), BF16)
     send_s[tiles] = jnp.zeros((TILE, HALF), BF16)
+    own_far.wait()
+    swap_far.wait()
+    for half in range(2):
+        loop(1, planes, lambda d: pass_on(plane_from(d), half, d).wait())
+    for start in range(NEAR, table_rows, 1024):
+        project(start, min(1024, table_rows - start))
 
     def gather(i):
         for u in range(UNROLL):
@@ -389,16 +408,11 @@
     collect(EDGES // SPAN - 1, act_b)
 
     edge_sum = acc[:, 0:HALF].astype(BF16)
-    mixed = mm(edge_sum, out_w[...])
-    mix[0] = mixed[:, 0:HALF]
-    mix[1] = mixed[:, HALF:]
-    swap_mix = remote(mix.at[other], mix_r, os_s.at[4], os_r.at[4], me, other)
-    swap_mix.start()
     recv_grad = gsum[...] * acc[:, HALF:]
     bias_part = jnp.sum(recv_grad, axis=0, keepdims=True)
     recv_grad_b = recv_grad.astype(BF16)
 
-    chunk_a, chunk_b = 2048 // planes, 1024 // planes
+    chunk_a, chunk_b = 2048 // planes, 1024 // RING
 
     def put(wire, chunk, start, value):
         value = value.astype(BF16)
@@ -426,6 +440,11 @@
 
     loop(1, planes, lambda d: wire_copy(wire_a, wire_ar, wa_s, wa_r, d).start())
     wire_ar[xy] = wire_a[xy]
+    mixed = mm(edge_sum, out_w[...])
+    mix[0] = mixed[:, 0:HALF]
+    mix[1] = mixed[:, HALF:]
+    swap_mix = remote(mix.at[other], mix_r, os_s.at[4], os_r.at[4], me, other)
+    swap_mix.start()
 
     def scatter(i):
         for u in range(UNROLL):
@@ -445,42 +464,46 @@
         dtab[t * TILE : (t + 1) * TILE, :] = items[plan[1, t]]
 
     dtab_b = dtab[0:table_rows, :].astype(BF16)
-    put(wire_b, chunk_b, 0, jnp.concatenate([mm(table[0], dtab_b, TN), mm(table[1], dtab_b, TN)], axis=0))
-    loop(1, planes, lambda d: wire_copy(wire_b, wire_br, wb_s, wb_r, d).start())
-    wire_br[xy] = wire_b[xy]
-    rim_s[0] = dtab[0:HALO, :].astype(BF16)
-    rim_s[1] = dtab[HALO + ROWS : NEAR, :].astype(BF16)
+    rim_s[0] = dtab_b[0:HALO]
+    rim_s[1] = dtab_b[HALO + ROWS : NEAR]
+    far_s[...] = dtab_b[NEAR:table_rows]
     back_below = remote(rim_s.at[0], rim_r.at[1], hb_s.at[0], hb_r.at[0], below, feat)
     back_up = remote(rim_s.at[1], rim_r.at[0], hb_s.at[1], hb_r.at[1], up, feat)
     back_below.start()
     back_up.start()
-    far_s[...] = dtab[NEAR:table_rows, :].astype(BF16)
-
-    def far_copy(d):
+
+    def far_copy(g, d):
+        low, high = GROUPS[g]
         to = plane_at(d)
-        return remote(far_s.at[rows_of(to, PER)], far_r.at[xy], fb_s.at[d], fb_r.at[d], to * RING + z, feat)
-
-    loop(1, planes, lambda d: far_copy(d).start())
+        src = far_s.at[pl.ds(pl.multiple_of(to * PER + low * QUOTA, QUOTA), (high - low) * QUOTA)]
+        return remote(src, far_r.at[xy, low * QUOTA : high * QUOTA], fb_s.at[g, d], fb_r.at[g, d], to * RING + z, feat)
+
+    for g in (2, 1, 0):
+        loop(1, planes, lambda d: far_copy(g, d).start())
+    put(wire_b, chunk_b, 0, jnp.concatenate([mm(table[0], dtab_b, TN), mm(table[1], dtab_b, TN)], axis=0))
+
+    def wire_b_copy(d):
+        to = lax.rem(z + d, RING)
+        return remote(wire_b.at[to], wire_br.at[z], wb_s.at[d], wb_r.at[d], ring_peer(d), feat)
+
+    loop(1, RING, lambda d: wire_b_copy(d).start())
+    wire_br[z] = wire_b[z]
     far_r[xy] = far_s[rows_of(xy, PER), :]
     back[...] = mm(recv_grad_b, recv_w[...], NT)
     swap_mix.wait()
-    updated[...] = (table[feat, own, :].astype(F32) + mix[feat] + mix_r[...]).astype(BF16)
-
-    part_a, part_b = chunk_a // RING, chunk_b // RING
-    part = part_a + part_b
+    updated_v[...] = (table[feat, own, :].astype(F32) + mix[feat] + mix_r[...]).astype(BF16)
+    keep_updated = pltpu.make_async_copy(updated_v, updated, loc.at[6])
+    keep_updated.start()
+
+    part = chunk_a // RING
+    chunk_c = chunk_b * RING // planes
     loop(1, planes, lambda d: arrived(wire_ar.at[plane_from(d)], wa_s.at[d], wa_r.at[d]))
     total = wire_ar[0].astype(F32)
     for p in range(1, planes):
         total = total + wire_ar[p].astype(F32)
     for k in range(RING):
-        zsum_s[k, 0:part_a, :] = total[k * part_a : (k + 1) * part_a, :]
+        zsum_s[k, 0:part, :] = total[k * part : (k + 1) * part, :]
         zsum_s[k, part : part + 8, :] = total[chunk_a : chunk_a + 8, :]
-    loop(1, planes, lambda d: arrived(wire_br.at[plane_from(d)], wb_s.at[d], wb_r.at[d]))
-    total = wire_br[0].astype(F32)
-    for p in range(1, planes):
-        total = total + wire_br[p].astype(F32)
-    for k in range(RING):
-        zsum_s[k, part_a:part, :] = total[k * part_b : (k + 1) * part_b, :]
 
     def zsum_copy(d):
         to = lax.rem(z + d, RING)
@@ -488,39 +511,67 @@
 
     loop(1, RING, lambda d: zsum_copy(d).start())
     zsum_r[z] = zsum_s[z]
+
+    loop(1, RING, lambda d: arrived(wire_br.at[ring_from(d)], wb_s.at[d], wb_r.at[d]))
+    total = wire_br[0].astype(F32)
+    for k in range(1, RING):
+        total = total + wire_br[k].astype(F32)
+    psum_s[...] = total.reshape(planes, chunk_b // planes, 128)
+
+    def psum_copy(d):
+        to = plane_at(d)
+        return remote(psum_s.at[to], psum_r.at[xy], pb_s.at[d], pb_r.at[d], to * RING + z, feat)
+
+    loop(1, planes, lambda d: psum_copy(d).start())
+    psum_r[xy] = psum_s[xy]
+
     loop(1, RING, lambda d: arrived(zsum_r.at[ring_from(d)], zw_s.at[d], zw_r.at[d]))
     whole = zsum_r[0]
     for k in range(1, RING):
         whole = whole + zsum_r[k]
     bias_out[...] = jnp.concatenate([whole[part : part + 1], whole[part + 1 : part + 2]], axis=1)
-    zall[z] = whole[0:part]
+    zall[z, 0:part, :] = whole[0:part]
+
+    loop(1, planes, lambda d: arrived(psum_r.at[plane_from(d)], pb_s.at[d], pb_r.at[d]))
+    whole = psum_r[0]
+    for p in range(1, planes):
+        whole = whole + psum_r[p]
+    zall[z, part:, :] = whole
 
     def zall_copy(d):
         return remote(zall.at[z], zall.at[z], za_s.at[d], za_r.at[d], ring_peer(d), feat)
 
     loop(1, RING, lambda d: zall_copy(d).start())
     loop(1, RING, lambda d: arrived(zall.at[ring_from(d)], za_s.at[d], za_r.at[d]))
-    for k in range(RING):
-        plane_s[k * part_a : (k + 1) * part_a, :] = zall[k, 0:part_a, :].astype(BF16)
-    plane_s[chunk_a:, :] = zall[:, part_a:part, :].reshape(chunk_b, 128).astype(BF16)
+    plane_s[0:chunk_a, :] = zall[:, 0:part, :].reshape(chunk_a, 128).astype(BF16)
+    plane_s[chunk_a:, :] = zall[:, part:, :].reshape(chunk_c, 128).astype(BF16)
 
     def all_copy(d):
         return remote(plane_s, plane_all.at[xy], pa_s.at[d], pa_r.at[d], plane_at(d) * RING + z, feat)
 
     loop(1, planes, lambda d: all_copy(d).start())
-    plane_all[xy] = plane_s[...]
-
-    loop(1, planes, lambda d: arrived(far_r.at[plane_from(d)], fb_s.at[d], fb_r.at[d]))
-    for at in range(RING):
-        k = ORDER[at]
-        pick = hot32(asked_z[:, k : k + 1] == lane32)
-        rows = far_r[:, at * QUOTA : (at + 1) * QUOTA, :].reshape(planes * QUOTA, HALF)
-        zfar_s[k] = mm(pick, rows, TN)[0:COARSE].astype(BF16)
+    keep_plane = pltpu.make_async_copy(plane_s, plane_all.at[xy], loc.at[7])
+    keep_plane.start()
+
+    def sum_owners(g):
+        low, high = GROUPS[g]
+        for d in range(1, planes):
+            arrived(far_r.at[plane_from(d), low * QUOTA : high * QUOTA], fb_s.at[g, d], fb_r.at[g, d])
+        for at in range(low, high):
+            k = ORDER[at]
+            pick = hot32(asked_z[:, k : k + 1] == lane32)
+            rows = far_r[:, at * QUOTA : (at + 1) * QUOTA, :].reshape(planes * QUOTA, HALF)
+            zfar_s[k] = mm(pick, rows, TN)[0:COARSE].astype(BF16)
+            if k:
+                zfar_copy(k).start()
 
     def zfar_copy(d):
         return remote(zfar_s.at[d], zfar_r.at[d], zf_s.at[d], zf_r.at[d], ring_peer(d), feat)
 
-    loop(1, RING, lambda d: zfar_copy(d).start())
+    sum_owners(2)
+
+    sum_owners(1)
+    sum_owners(0)
     zfar_r[0] = zfar_s[0]
     back_below.wait()
     back_up.wait()
@@ -538,18 +589,24 @@
     swap_back = remote(back_s.at[other], back_r, os_s.at[5], os_r.at[5], me, other)
     swap_back.start()
     swap_back.wait()
-    grad_nodes[...] = (cots[feat].astype(F32) + back_s[feat] + back_r[...]).astype(BF16)
+    nodes_v[...] = (cots[feat].astype(F32) + back_s[feat] + back_r[...]).astype(BF16)
+    keep_nodes = pltpu.make_async_copy(nodes_v, grad_nodes, loc.at[0])
+    keep_nodes.start()
 
     loop(1, planes, lambda d: arrived(plane_all.at[plane_from(d)], pa_s.at[d], pa_r.at[d]))
-    weights_out[...] = plane_all[...]
+    keep_updated.wait()
+    keep_nodes.wait()
+    keep_plane.wait()
 
     loop(1, planes, lambda d: list_copy(d).wait_send())
     loop(1, RING, lambda d: coarse_copy(d).wait_send())
     for g in range(len(GROUPS)):
         loop(1, planes, lambda d: plane_copy(g, d).wait_send())
     loop(1, planes, lambda d: wire_copy(wire_a, wire_ar, wa_s, wa_r, d).wait_send())
-    loop(1, planes, lambda d: wire_copy(wire_b, wire_br, wb_s, wb_r, d).wait_send())
-    loop(1, planes, lambda d: far_copy(d).wait_send())
+    loop(1, RING, lambda d: wire_b_copy(d).wait_send())
+    for g in range(len(GROUPS)):
+        loop(1, planes, lambda d: far_copy(g, d).wait_send())
+    loop(1, planes, lambda d: psum_copy(d).wait_send())
     loop(1, planes, lambda d: all_copy(d).wait_send())
     loop(1, RING, lambda d: zsum_copy(d).wait_send())
     loop(1, RING, lambda d: zall_copy(d).wait_send())
@@ -562,10 +619,10 @@
     tiles = pl.cdiv(table_rows, TILE)
     padded = tiles * TILE
     n_items = pl.cdiv(BLOCKS + tiles - 1, UNROLL) * UNROLL
-    chunk_a, chunk_b = 2048 // planes, 1024 // planes
-    part = (chunk_a + chunk_b) // RING
+    chunk_a, chunk_b, chunk_c = 2048 // planes, 1024 // RING, 1024 // planes
+    part = chunk_a // RING
     vmem = pl.BlockSpec(memory_space=pltpu.VMEM)
-    anyspace = pl.BlockSpec(memory_space=pl.ANY)
+    hbm = pl.BlockSpec(memory_space=pltpu.HBM)
     dma = pltpu.SemaphoreType.DMA
 
     def both(*shape):
@@ -576,11 +633,11 @@
         out_shape=(
             jax.ShapeDtypeStruct((ROWS, HALF), BF16),
             jax.ShapeDtypeStruct((ROWS, HALF), BF16),
-            jax.ShapeDtypeStruct((planes, chunk_a + chunk_b, 128), BF16),
+            jax.ShapeDtypeStruct((planes, chunk_a + chunk_c, 128), BF16),
             jax.ShapeDtypeStruct((1, HALF), F32),
         ),
-        in_specs=[vmem] * 4 + [anyspace] * 5,
-        out_specs=(vmem,) * 4,
+        in_specs=[vmem] * 4 + [hbm] * 5,
+        out_specs=(hbm,) * 3 + (vmem,),
         scratch_shapes=[
             pltpu.VMEM((2, table_rows, HALF), BF16),
             pltpu.VMEM((2, ROWS, HALF), BF16),
@@ -591,6 +648,7 @@
             pltpu.VMEM((planes * QUOTA, 128), I32),
             pltpu.VMEM((RING, HALO, HALF), BF16),
             pltpu.VMEM((planes, PER, HALF), BF16),
+            pltpu.VMEM((planes * QUOTA, 128), I32),
             pltpu.VMEM((PAIRS, 128), I32),
             pltpu.VMEM((128, 128), I32),
             pltpu.VMEM((8, 128), I32),
@@ -617,21 +675,25 @@
             pltpu.VMEM((2, ROWS, HALF), F32),
             pltpu.VMEM((ROWS, HALF), F32),
             pltpu.VMEM((planes, chunk_a + 16, 128), BF16),
-            pltpu.VMEM((planes, chunk_b, 128), BF16),
+            pltpu.VMEM((RING, chunk_b, 128), BF16),
             pltpu.VMEM((planes, chunk_a + 16, 128), BF16),
-            pltpu.VMEM((planes, chunk_b, 128), BF16),
+            pltpu.VMEM((RING, chunk_b, 128), BF16),
             pltpu.VMEM((planes, PER, HALF), BF16),
             pltpu.VMEM((2, HALO, HALF), BF16),
             pltpu.VMEM((RING, COARSE, HALF), BF16),
             pltpu.VMEM((RING, COARSE, HALF), BF16),
             pltpu.VMEM((RING, part + 8, 128), F32),
             pltpu.VMEM((RING, part + 8, 128), F32),
-            pltpu.VMEM((RING, part, 128), F32),
-            pltpu.VMEM((chunk_a + chunk_b, 128), BF16),
-            pltpu.VMEM((planes, chunk_a + chunk_b, 128), BF16),
+            pltpu.VMEM((RING, part + chunk_b // planes, 128), F32),
+            pltpu.VMEM((chunk_a + chunk_c, 128), BF16),
+            pltpu.VMEM((planes, chunk_b // planes, 128), F32),
+            pltpu.VMEM((planes, chunk_b // planes, 128), F32),
+            pltpu.VMEM((ROWS, HALF), BF16),
+            pltpu.VMEM((ROWS, HALF), BF16),
             dma((9,)),
-            *both(RING), *both(planes), *both(len(GROUPS), planes), *both(planes), *both(2), *both(6),
-            *both(planes), *both(planes), *both(planes), *both(2), *both(RING), *both(RING), *both(RING), *both(planes),
+            *both(RING), *both(planes), *both(len(GROUPS), planes), *both(2, planes), *both(2), *both(6),
+            *both(planes), *both(RING), *both(len(GROUPS), planes), *both(2), *both(RING), *both(RING), *both(RING),
+            *both(planes), *both(planes),
         ],
         compiler_params=pltpu.CompilerParams(
             collective_id=0, has_side_effects=True, vmem_limit_bytes=60 * 2**20
@@ -640,26 +702,41 @@
     )(*args)
 
 
-def finish_kernel(chunk_a, updated, grad_nodes, weights, bias, updated_o, grad_nodes_o, g_send, g_recv, g_out, g_bias):
-    updated_o[...] = updated[...]
-    grad_nodes_o[...] = grad_nodes[...]
+def finish_kernel(
+    chunk_a, updated, grad_nodes, weights, bias,
+    updated_o, grad_nodes_o, g_send, g_recv, g_out, g_bias,
+    weights_v, sems,
+):
+    copies = [
+        pltpu.make_async_copy(weights, weights_v, sems.at[0]),
+        pltpu.make_async_copy(updated, updated_o, sems.at[1]),
+        pltpu.make_async_copy(grad_nodes, grad_nodes_o, sems.at[2]),
+    ]
+    for copy in copies:
+        copy.start()
     g_bias[...] = bias[...]
-    planes, chunk, _ = weights.shape
-    chunk_b = chunk - chunk_a
-    a = weights[:, 0:chunk_a, :].reshape(planes * chunk_a, 128).astype(F32)
-    b = weights[:, chunk_a:, :].reshape(planes * chunk_b, 128).astype(F32)
+    copies[0].wait()
+    a = weights_v[:, 0:chunk_a, :].reshape(2048, 128).astype(F32)
     for m in range(2):
-        lanes = slice(128 * m, 128 * (m + 1))
-        g_recv[:, lanes] = a[512 * m : 512 * (m + 1)]
-        g_send[:, lanes] = b[512 * m : 512 * (m + 1)]
+        g_recv[:, 128 * m : 128 * (m + 1)] = a[512 * m : 512 * (m + 1)]
     for m in range(4):
         g_out[:, 128 * m : 128 * (m + 1)] = a[1024 + 256 * m : 1024 + 256 * (m + 1)]
-
-
-def finish(n_patch, *args):
+    each = 1024 // (RING * weights_v.shape[0])
+    b = weights_v[:, chunk_a:, :].astype(F32)
+    for k in range(RING):
+        rows = b[:, k * each : (k + 1) * each, :].reshape(1024 // RING, 128)
+        at = k * (1024 // RING) % 512
+        lanes = slice(128 * (k * 2 // RING), 128 * (k * 2 // RING) + 128)
+        g_send[at : at + 1024 // RING, lanes] = rows
+    copies[1].wait()
+    copies[2].wait()
+
+
+def finish(*args):
     vmem = pl.BlockSpec(memory_space=pltpu.VMEM)
+    hbm = pl.BlockSpec(memory_space=pltpu.HBM)
     return pl.pallas_call(
-        functools.partial(finish_kernel, 2048 // (n_patch // RING)),
+        functools.partial(finish_kernel, 2048 // args[2].shape[0]),
         out_shape=(
             jax.ShapeDtypeStruct((ROWS, HALF), BF16),
             jax.ShapeDtypeStruct((ROWS, HALF), BF16),
@@ -668,22 +745,23 @@
             jax.ShapeDtypeStruct((HALF, 2 * HALF), F32),
             jax.ShapeDtypeStruct((1, HALF), F32),
         ),
-        in_specs=[vmem] * 4,
+        in_specs=[hbm] * 3 + [vmem],
         out_specs=(vmem,) * 6,
-        compiler_params=pltpu.CompilerParams(vmem_limit_bytes=32 * 2**20),
+        scratch_shapes=[
+            pltpu.VMEM(args[2].shape, BF16),
+            pltpu.SemaphoreType.DMA((3,)),
+        ],
+        compiler_params=pltpu.CompilerParams(vmem_limit_bytes=62 * 2**20),
         name="finish",
     )(*args)
 
 
 def shards(n_patch, feats, cot, send_w, recv_w, out_w, bias, sender, receiver, wanted):
-    planes = n_patch // RING
-    lists = wanted.reshape(planes, RING, QUOTA).transpose(0, 2, 1).reshape(planes * QUOTA, RING)
-    lists = jnp.pad(jnp.concatenate([lists, lists], axis=1), ((0, 0), (0, 128 - 2 * RING)))
     parts = layer(
-        n_patch, sender.reshape(PAIRS, 128), receiver.reshape(PAIRS, 128), lists, bias.reshape(1, HALF),
+        n_patch, sender.reshape(PAIRS, 128), receiver.reshape(PAIRS, 128), wanted.reshape(n_patch, QUOTA).T, bias.reshape(1, HALF),
         feats, cot, send_w, recv_w, out_w,
     )
-    updated, grad_nodes, g_send, g_recv, g_out, g_bias = finish(n_patch, *parts)
+    updated, grad_nodes, g_send, g_recv, g_out, g_bias = finish(*parts)
     return (updated, grad_nodes, g_send, g_recv, g_out, g_bias.reshape(HALF))
 
 

time: 109 us -> 98.7 us (0.906)
  the two profiles are of different devices: /device:TPU:3 before, /device:TPU:8 now
where the time goes in v4:
time: 98.7 us; the launch traced here: 97.5 us
  Pallas kernels  96.7 us (98%)
    pallas_call x1, Pallas kernels, layer(): pl.pallas_call(functools.partial(layer_kernel, n_patch), out_shape=(jax.S...  93.3 us
    pallas_call x1, Pallas kernels, finish(): pl.pallas_call(functools.partial(finish_kernel, 2048 // args[2].shape[0])...  3.36 us

profile of v4, /device:TPU:8, one launch (start us, length us, event | category | flops | bytes accessed | tf_op | source)
XLA Modules:
  0.0 97.5 jit_solution(641075364622905746)
XLA Ops:
  0.6 93.3 %layer.1 = (bf16[640,256]{1,0:T(8,128)(2,1)}, bf16[640,256]{1,0:T(8,128)(2,1)}, bf16[16,192,128]{2,1,0:T(8,128)(2,1)}, f32[1,256]{1,0:T(1,128)}) custom-call(s32[64,128]{1,0:T(8,128)} %bitcast.7, s32[64,128]{1,0:T(8,128)} %bitcast.8, s32[16,128]{1,0:T(8,128)} %bitcast.9, f32[1,256]{1,0:T(1,128)} %bitcast.10, bf16[640,256]{1,0:T(8,128)(2,1)} %feats.1, ...), custom_call_target="tpu_custom_call" | custom-call | tf_op jit(solution)/shard_map/layer/pallas_call | solution.py:631
  94.0 3.4 %finish.1 = (bf16[640,256]{1,0:T(8,128)(2,1)}, bf16[640,256]{1,0:T(8,128)(2,1)}, f32[512,256]{1,0:T(8,128)}, f32[512,256]{1,0:T(8,128)}, f32[256,512]{1,0:T(8,128)}, /*index=5*/f32[1,256]{1,0:T(1,128)}) custom-call(bf16[640,256]{1,0:T(8,128)(2,1)} %get-tuple-element.16.updated, bf16[640,256]{1,0:T(8,128)(2,1)} %get-tuple-element.17.grad_nodes, ...), custom_call_target="tpu_custom_call" | custom-call | tf_op jit(solution)/shard_map/finish/pallas_call | solution.py:738

commit v5 on v4

--- a/solution.py
+++ b/solution.py
@@ -128,9 +128,9 @@
     send_s, pair_s, gsum, pre_s, gat_s, items, act_a, act_b, acc, dtab,
     far_s, rim_s, mix, mix_r, back, back_s, back_r,
     wire_a, wire_b, wire_ar, wire_br, far_r, rim_r,
-    zfar_s, zfar_r, zsum_s, zsum_r, zall, plane_s, psum_s, psum_r, updated_v, nodes_v,
+    zfar_s, zfar_r, zsum_s, zsum_r, zall, plane_s, zsum_bs, zsum_br, zall_b, plane_bs, updated_v, nodes_v,
     loc, zs_s, zs_r, ls_s, ls_r, ps_s, ps_r, pass_s, pass_r, hs_s, hs_r, os_s, os_r,
-    wa_s, wa_r, wb_s, wb_r, fb_s, fb_r, hb_s, hb_r, zf_s, zf_r, zw_s, zw_r, za_s, za_r, pa_s, pa_r, pb_s, pb_r,
+    wa_s, wa_r, wb_s, wb_r, fb_s, fb_r, hb_s, hb_r, zf_s, zf_r, zw_s, zw_r, za_s, za_r, pa_s, pa_r, pb_s, pb_r, zx_s, zx_r, zy_s, zy_r,
 ):
     planes = n_patch // RING
     table_rows = NEAR + n_patch * QUOTA
@@ -154,11 +154,13 @@
     def plane_from(d):
         return lax.rem(xy + planes - d, planes)
 
-    def ring_from(d):
-        return lax.rem(z + RING - d, RING)
-
     def arrived(at, send, recv):
         remote(at, at, send, recv, me, other).wait_recv()
+
+    def departed(at, send, recv):
+        remote(at, at, send, recv, me, other).wait_send()
+
+    others, around = planes - 1, RING - 1
 
     own_rows = table.at[feat, HALO : HALO + ROWS]
     local = [
@@ -191,11 +193,11 @@
     pl.semaphore_wait(barrier, planes - 1 + RING - 1 + 3)
 
     def coarse_copy(d):
-        return remote(feats.at[0:COARSE], coarse.at[RING - d, 0:COARSE], zs_s.at[d], zs_r.at[RING - d], ring_peer(d), feat)
+        return remote(feats.at[0:COARSE], coarse.at[RING - d, 0:COARSE], zs_s.at[0], zs_r.at[0 if d in (1, RING - 1) else 1], ring_peer(d), feat)
 
     def list_copy(d):
         to = plane_at(d)
-        return remote(lists.at[rows_of(to, QUOTA)], asked.at[rows_of(xy, QUOTA)], ls_s.at[d], ls_r.at[d], to * RING + z, feat)
+        return remote(lists.at[rows_of(to, QUOTA)], asked.at[rows_of(xy, QUOTA)], ls_s.at[0], ls_r.at[0], to * RING + z, feat)
 
     def far_rows(p, low=0, high=RING):
         return table.at[feat, pl.ds(pl.multiple_of(NEAR + p * PER + low * QUOTA, QUOTA), (high - low) * QUOTA)]
@@ -204,7 +206,7 @@
         low, high = GROUPS[g]
         to = plane_at(d)
         return remote(
-            packed.at[to, low * QUOTA : high * QUOTA], far_rows(xy, low, high), ps_s.at[g, d], ps_r.at[g, d], to * RING + z, feat
+            packed.at[to, low * QUOTA : high * QUOTA], far_rows(xy, low, high), ps_s.at[g], ps_r.at[g], to * RING + z, feat
         )
 
     def swap(ref, slot):
@@ -248,12 +250,11 @@
     for v in range(8):
         keys[8 * v : 8 * v + 8, :] = xs[v]
     asked[rows_of(xy, QUOTA), :] = lists[rows_of(xy, QUOTA), :]
-    loop(1, planes, lambda d: arrived(asked.at[rows_of(plane_from(d), QUOTA)], ls_s.at[d], ls_r.at[d]))
+    arrived(asked.at[0 : others * QUOTA], ls_s.at[0], ls_r.at[0])
     asked_z[...] = pltpu.roll(asked[...], lax.rem(128 - z, 128), 1)
     local[0].wait()
     pack(0)
-    for k in ORDER[1:3]:
-        arrived(coarse.at[k, 0:COARSE], zs_s.at[k], zs_r.at[k])
+    arrived(coarse.at[1:3, 0:COARSE], zs_s.at[0], zs_r.at[0])
     pack(1)
     flat = keys[...]
     turned[...] = jnp.transpose(jnp.concatenate([flat, flat], axis=0))
@@ -281,12 +282,11 @@
     to_scalars = pltpu.make_async_copy(plan_v, plan, loc.at[8])
     to_scalars.start()
 
-    for k in ORDER[3:]:
-        arrived(coarse.at[k, 0:COARSE], zs_s.at[k], zs_r.at[k])
+    arrived(coarse.at[2:7, 0:COARSE], zs_s.at[0], zs_r.at[1])
     pack(2)
     own_far = pltpu.make_async_copy(packed.at[xy], far_rows(xy), loc.at[7])
     own_far.start()
-    swap_far = remote(packed.at[xy], far_rows(xy), pass_s.at[0, 0], pass_r.at[0, 0], me, other)
+    swap_far = remote(packed.at[xy], far_rows(xy), pass_s.at[2], pass_r.at[2], me, other)
     swap_far.start()
     to_scalars.wait()
 
@@ -316,30 +316,23 @@
 
     loop(0, BLOCKS // 8, receive)
 
-    def pass_on(p, half, slot):
+    def pass_on(p, half):
         low, high = HALVES[half]
-        return remote(far_rows(p, low, high), far_rows(p, low, high), pass_s.at[half, slot], pass_r.at[half, slot], me, other)
-
-    def arrive(g, d):
-        low, high = GROUPS[g]
-        arrived(far_rows(plane_from(d), low, high), ps_s.at[g, d], ps_r.at[g, d])
-
-    def hand_first(d):
-        arrive(0, d)
-        arrive(1, d)
-        pass_on(plane_from(d), 0, d).start()
-
-    def hand_second(d):
-        arrive(2, d)
-        pass_on(plane_from(d), 1, d).start()
+        return remote(far_rows(p, low, high), far_rows(p, low, high), pass_s.at[half], pass_r.at[half], me, other)
+
+    def all_far(core, low, high):
+        return table.at[core, NEAR : NEAR + others * (high - low) * QUOTA]
 
     to_up.wait()
     swap(low_rim, 2).start()
     to_below.wait()
     swap(high_rim, 3).start()
-    loop(1, planes, hand_first)
+    for g in range(2):
+        arrived(all_far(feat, *GROUPS[g]), ps_s.at[g], ps_r.at[g])
+    loop(1, planes, lambda d: pass_on(plane_from(d), 0).start())
     loop(BLOCKS // 8, BLOCKS // 4, receive)
-    loop(1, planes, hand_second)
+    arrived(all_far(feat, *GROUPS[2]), ps_s.at[2], ps_r.at[2])
+    loop(1, planes, lambda d: pass_on(plane_from(d), 1).start())
 
     def project(start, size):
         part = slice(start, start + size)
@@ -360,7 +353,8 @@
     own_far.wait()
     swap_far.wait()
     for half in range(2):
-        loop(1, planes, lambda d: pass_on(plane_from(d), half, d).wait())
+        departed(all_far(feat, *HALVES[half]), pass_s.at[half], pass_r.at[half])
+        arrived(all_far(other, *HALVES[half]), pass_s.at[half], pass_r.at[half])
     for start in range(NEAR, table_rows, 1024):
         project(start, min(1024, table_rows - start))
 
@@ -412,7 +406,7 @@
     bias_part = jnp.sum(recv_grad, axis=0, keepdims=True)
     recv_grad_b = recv_grad.astype(BF16)
 
-    chunk_a, chunk_b = 2048 // planes, 1024 // RING
+    chunk_a, chunk_b = 2048 // planes, 1024 // planes
 
     def put(wire, chunk, start, value):
         value = value.astype(BF16)
@@ -436,7 +430,7 @@
 
     def wire_copy(src, dst, send, recv, d):
         to = plane_at(d)
-        return remote(src.at[to], dst.at[xy], send.at[d], recv.at[d], to * RING + z, feat)
+        return remote(src.at[to], dst.at[xy], send.at[0], recv.at[0], to * RING + z, feat)
 
     loop(1, planes, lambda d: wire_copy(wire_a, wire_ar, wa_s, wa_r, d).start())
     wire_ar[xy] = wire_a[xy]
@@ -464,6 +458,9 @@
         dtab[t * TILE : (t + 1) * TILE, :] = items[plan[1, t]]
 
     dtab_b = dtab[0:table_rows, :].astype(BF16)
+    put(wire_b, chunk_b, 0, jnp.concatenate([mm(table[0], dtab_b, TN), mm(table[1], dtab_b, TN)], axis=0))
+    loop(1, planes, lambda d: wire_copy(wire_b, wire_br, wb_s, wb_r, d).start())
+    wire_br[xy] = wire_b[xy]
     rim_s[0] = dtab_b[0:HALO]
     rim_s[1] = dtab_b[HALO + ROWS : NEAR]
     far_s[...] = dtab_b[NEAR:table_rows]
@@ -476,18 +473,10 @@
         low, high = GROUPS[g]
         to = plane_at(d)
         src = far_s.at[pl.ds(pl.multiple_of(to * PER + low * QUOTA, QUOTA), (high - low) * QUOTA)]
-        return remote(src, far_r.at[xy, low * QUOTA : high * QUOTA], fb_s.at[g, d], fb_r.at[g, d], to * RING + z, feat)
+        return remote(src, far_r.at[xy, low * QUOTA : high * QUOTA], fb_s.at[g], fb_r.at[g], to * RING + z, feat)
 
     for g in (2, 1, 0):
         loop(1, planes, lambda d: far_copy(g, d).start())
-    put(wire_b, chunk_b, 0, jnp.concatenate([mm(table[0], dtab_b, TN), mm(table[1], dtab_b, TN)], axis=0))
-
-    def wire_b_copy(d):
-        to = lax.rem(z + d, RING)
-        return remote(wire_b.at[to], wire_br.at[z], wb_s.at[d], wb_r.at[d], ring_peer(d), feat)
-
-    loop(1, RING, lambda d: wire_b_copy(d).start())
-    wire_br[z] = wire_b[z]
     far_r[xy] = far_s[rows_of(xy, PER), :]
     back[...] = mm(recv_grad_b, recv_w[...], NT)
     swap_mix.wait()
@@ -496,8 +485,7 @@
     keep_updated.start()
 
     part = chunk_a // RING
-    chunk_c = chunk_b * RING // planes
-    loop(1, planes, lambda d: arrived(wire_ar.at[plane_from(d)], wa_s.at[d], wa_r.at[d]))
+    arrived(wire_ar.at[0:others], wa_s.at[0], wa_r.at[0])
     total = wire_ar[0].astype(F32)
     for p in range(1, planes):
         total = total + wire_ar[p].astype(F32)
@@ -507,56 +495,63 @@
 
     def zsum_copy(d):
         to = lax.rem(z + d, RING)
-        return remote(zsum_s.at[to], zsum_r.at[z], zw_s.at[d], zw_r.at[d], ring_peer(d), feat)
+        return remote(zsum_s.at[to], zsum_r.at[z], zw_s.at[0], zw_r.at[0], ring_peer(d), feat)
 
     loop(1, RING, lambda d: zsum_copy(d).start())
     zsum_r[z] = zsum_s[z]
 
-    loop(1, RING, lambda d: arrived(wire_br.at[ring_from(d)], wb_s.at[d], wb_r.at[d]))
-    total = wire_br[0].astype(F32)
-    for k in range(1, RING):
-        total = total + wire_br[k].astype(F32)
-    psum_s[...] = total.reshape(planes, chunk_b // planes, 128)
-
-    def psum_copy(d):
-        to = plane_at(d)
-        return remote(psum_s.at[to], psum_r.at[xy], pb_s.at[d], pb_r.at[d], to * RING + z, feat)
-
-    loop(1, planes, lambda d: psum_copy(d).start())
-    psum_r[xy] = psum_s[xy]
-
-    loop(1, RING, lambda d: arrived(zsum_r.at[ring_from(d)], zw_s.at[d], zw_r.at[d]))
+    arrived(zsum_r.at[0:around], zw_s.at[0], zw_r.at[0])
     whole = zsum_r[0]
     for k in range(1, RING):
         whole = whole + zsum_r[k]
     bias_out[...] = jnp.concatenate([whole[part : part + 1], whole[part + 1 : part + 2]], axis=1)
-    zall[z, 0:part, :] = whole[0:part]
-
-    loop(1, planes, lambda d: arrived(psum_r.at[plane_from(d)], pb_s.at[d], pb_r.at[d]))
-    whole = psum_r[0]
+    zall[z] = whole[0:part]
+
+    def zall_copy(d):
+        return remote(zall.at[z], zall.at[z], za_s.at[0], za_r.at[0], ring_peer(d), feat)
+
+    loop(1, RING, lambda d: zall_copy(d).start())
+
+    arrived(wire_br.at[0:others], wb_s.at[0], wb_r.at[0])
+    total = wire_br[0].astype(F32)
     for p in range(1, planes):
-        whole = whole + psum_r[p]
-    zall[z, part:, :] = whole
-
-    def zall_copy(d):
-        return remote(zall.at[z], zall.at[z], za_s.at[d], za_r.at[d], ring_peer(d), feat)
-
-    loop(1, RING, lambda d: zall_copy(d).start())
-    loop(1, RING, lambda d: arrived(zall.at[ring_from(d)], za_s.at[d], za_r.at[d]))
-    plane_s[0:chunk_a, :] = zall[:, 0:part, :].reshape(chunk_a, 128).astype(BF16)
-    plane_s[chunk_a:, :] = zall[:, part:, :].reshape(chunk_c, 128).astype(BF16)
+        total = total + wire_br[p].astype(F32)
+    part_b = chunk_b // RING
+    zsum_bs[...] = total.reshape(RING, part_b, 128)
+
+    def zsum_b_copy(d):
+        to = lax.rem(z + d, RING)
+        return remote(zsum_bs.at[to], zsum_br.at[z], zx_s.at[0], zx_r.at[0], ring_peer(d), feat)
+
+    loop(1, RING, lambda d: zsum_b_copy(d).start())
+    zsum_br[z] = zsum_bs[z]
+
+    arrived(zall.at[0:around], za_s.at[0], za_r.at[0])
+    plane_s[...] = zall[...].reshape(chunk_a, 128).astype(BF16)
 
     def all_copy(d):
-        return remote(plane_s, plane_all.at[xy], pa_s.at[d], pa_r.at[d], plane_at(d) * RING + z, feat)
+        return remote(
+            plane_s, plane_all.at[xy, 0:chunk_a], pa_s.at[0], pa_r.at[0], plane_at(d) * RING + z, feat
+        )
 
     loop(1, planes, lambda d: all_copy(d).start())
-    keep_plane = pltpu.make_async_copy(plane_s, plane_all.at[xy], loc.at[7])
+    keep_plane = pltpu.make_async_copy(plane_s, plane_all.at[xy, 0:chunk_a], loc.at[7])
     keep_plane.start()
+
+    arrived(zsum_br.at[0:around], zx_s.at[0], zx_r.at[0])
+    whole = zsum_br[0]
+    for k in range(1, RING):
+        whole = whole + zsum_br[k]
+    zall_b[z] = whole
+
+    def zall_b_copy(d):
+        return remote(zall_b.at[z], zall_b.at[z], zy_s.at[0], zy_r.at[0], ring_peer(d), feat)
+
+    loop(1, RING, lambda d: zall_b_copy(d).start())
 
     def sum_owners(g):
         low, high = GROUPS[g]
-        for d in range(1, planes):
-            arrived(far_r.at[plane_from(d), low * QUOTA : high * QUOTA], fb_s.at[g, d], fb_r.at[g, d])
+        arrived(far_r.at[0:others, low * QUOTA : high * QUOTA], fb_s.at[g], fb_r.at[g])
         for at in range(low, high):
             k = ORDER[at]
             pick = hot32(asked_z[:, k : k + 1] == lane32)
@@ -566,16 +561,26 @@
                 zfar_copy(k).start()
 
     def zfar_copy(d):
-        return remote(zfar_s.at[d], zfar_r.at[d], zf_s.at[d], zf_r.at[d], ring_peer(d), feat)
+        return remote(zfar_s.at[d], zfar_r.at[d], zf_s.at[0], zf_r.at[0], ring_peer(d), feat)
+
+    def all_b_copy(d):
+        return remote(
+            plane_bs, plane_all.at[xy, chunk_a : chunk_a + chunk_b], pb_s.at[0], pb_r.at[0], plane_at(d) * RING + z, feat
+        )
 
     sum_owners(2)
+    arrived(zall_b.at[0:around], zy_s.at[0], zy_r.at[0])
+    plane_bs[...] = zall_b[...].reshape(chunk_b, 128).astype(BF16)
+    loop(1, planes, lambda d: all_b_copy(d).start())
+    keep_plane_b = pltpu.make_async_copy(plane_bs, plane_all.at[xy, chunk_a : chunk_a + chunk_b], loc.at[8])
+    keep_plane_b.start()
 
     sum_owners(1)
     sum_owners(0)
     zfar_r[0] = zfar_s[0]
     back_below.wait()
     back_up.wait()
-    loop(1, RING, lambda d: arrived(zfar_r.at[d], zf_s.at[d], zf_r.at[d]))
+    arrived(zfar_r.at[0:around], zf_s.at[0], zf_r.at[0])
     head = zfar_r[0].astype(F32)
     for k in range(1, RING):
         head = head + zfar_r[k].astype(F32)
@@ -593,24 +598,28 @@
     keep_nodes = pltpu.make_async_copy(nodes_v, grad_nodes, loc.at[0])
     keep_nodes.start()
 
-    loop(1, planes, lambda d: arrived(plane_all.at[plane_from(d)], pa_s.at[d], pa_r.at[d]))
+    arrived(plane_all.at[0:others, 0:chunk_a], pa_s.at[0], pa_r.at[0])
+    arrived(plane_all.at[0:others, chunk_a : chunk_a + chunk_b], pb_s.at[0], pb_r.at[0])
     keep_updated.wait()
     keep_nodes.wait()
     keep_plane.wait()
-
-    loop(1, planes, lambda d: list_copy(d).wait_send())
-    loop(1, RING, lambda d: coarse_copy(d).wait_send())
-    for g in range(len(GROUPS)):
-        loop(1, planes, lambda d: plane_copy(g, d).wait_send())
-    loop(1, planes, lambda d: wire_copy(wire_a, wire_ar, wa_s, wa_r, d).wait_send())
-    loop(1, RING, lambda d: wire_b_copy(d).wait_send())
-    for g in range(len(GROUPS)):
-        loop(1, planes, lambda d: far_copy(g, d).wait_send())
-    loop(1, planes, lambda d: psum_copy(d).wait_send())
-    loop(1, planes, lambda d: all_copy(d).wait_send())
-    loop(1, RING, lambda d: zsum_copy(d).wait_send())
-    loop(1, RING, lambda d: zall_copy(d).wait_send())
-    loop(1, RING, lambda d: zfar_copy(d).wait_send())
+    keep_plane_b.wait()
+
+    departed(lists.at[0 : others * QUOTA], ls_s.at[0], ls_r.at[0])
+    departed(coarse.at[1:RING, 0:COARSE], zs_s.at[0], zs_r.at[0])
+    for g, (low, high) in enumerate(GROUPS):
+        departed(all_far(feat, low, high), ps_s.at[g], ps_r.at[g])
+    departed(wire_a.at[0:others], wa_s.at[0], wa_r.at[0])
+    departed(wire_b.at[0:others], wb_s.at[0], wb_r.at[0])
+    for g, (low, high) in enumerate(GROUPS):
+        departed(far_r.at[0:others, low * QUOTA : high * QUOTA], fb_s.at[g], fb_r.at[g])
+    departed(plane_all.at[0:others, chunk_a : chunk_a + chunk_b], pb_s.at[0], pb_r.at[0])
+    departed(zsum_bs.at[0:around], zx_s.at[0], zx_r.at[0])
+    departed(zall_b.at[0:around], zy_s.at[0], zy_r.at[0])
+    departed(plane_all.at[0:others, 0:chunk_a], pa_s.at[0], pa_r.at[0])
+    departed(zsum_s.at[0:around], zw_s.at[0], zw_r.at[0])
+    departed(zall.at[0:around], za_s.at[0], za_r.at[0])
+    departed(zfar_s.at[0:around], zf_s.at[0], zf_r.at[0])
 
 
 def layer(n_patch, *args):
@@ -619,7 +628,7 @@
     tiles = pl.cdiv(table_rows, TILE)
     padded = tiles * TILE
     n_items = pl.cdiv(BLOCKS + tiles - 1, UNROLL) * UNROLL
-    chunk_a, chunk_b, chunk_c = 2048 // planes, 1024 // RING, 1024 // planes
+    chunk_a, chunk_b = 2048 // planes, 1024 // planes
     part = chunk_a // RING
     vmem = pl.BlockSpec(memory_space=pltpu.VMEM)
     hbm = pl.BlockSpec(memory_space=pltpu.HBM)
@@ -633,7 +642,7 @@
         out_shape=(
             jax.ShapeDtypeStruct((ROWS, HALF), BF16),
             jax.ShapeDtypeStruct((ROWS, HALF), BF16),
-            jax.ShapeDtypeStruct((planes, chunk_a + chunk_c, 128), BF16),
+            jax.ShapeDtypeStruct((planes, chunk_a + chunk_b, 128), BF16),
             jax.ShapeDtypeStruct((1, HALF), F32),
         ),
         in_specs=[vmem] * 4 + [hbm] * 5,
@@ -675,25 +684,25 @@
             pltpu.VMEM((2, ROWS, HALF), F32),
             pltpu.VMEM((ROWS, HALF), F32),
             pltpu.VMEM((planes, chunk_a + 16, 128), BF16),
-            pltpu.VMEM((RING, chunk_b, 128), BF16),
+            pltpu.VMEM((planes, chunk_b, 128), BF16),
             pltpu.VMEM((planes, chunk_a + 16, 128), BF16),
-            pltpu.VMEM((RING, chunk_b, 128), BF16),
+            pltpu.VMEM((planes, chunk_b, 128), BF16),
             pltpu.VMEM((planes, PER, HALF), BF16),
             pltpu.VMEM((2, HALO, HALF), BF16),
             pltpu.VMEM((RING, COARSE, HALF), BF16),
             pltpu.VMEM((RING, COARSE, HALF), BF16),
             pltpu.VMEM((RING, part + 8, 128), F32),
             pltpu.VMEM((RING, part + 8, 128), F32),
-            pltpu.VMEM((RING, part + chunk_b // planes, 128), F32),
-            pltpu.VMEM((chunk_a + chunk_c, 128), BF16),
-            pltpu.VMEM((planes, chunk_b // planes, 128), F32),
-            pltpu.VMEM((planes, chunk_b // planes, 128), F32),
+            pltpu.VMEM((RING, part, 128), F32),
+            pltpu.VMEM((chunk_a, 128), BF16),
+            pltpu.VMEM((RING, chunk_b // RING, 128), F32),
+            pltpu.VMEM((RING, chunk_b // RING, 128), F32),
+            pltpu.VMEM((RING, chunk_b // RING, 128), F32),
+            pltpu.VMEM((chunk_b, 128), BF16),
             pltpu.VMEM((ROWS, HALF), BF16),
             pltpu.VMEM((ROWS, HALF), BF16),
             dma((9,)),
-            *both(RING), *both(planes), *both(len(GROUPS), planes), *both(2, planes), *both(2), *both(6),
-            *both(planes), *both(RING), *both(len(GROUPS), planes), *both(2), *both(RING), *both(RING), *both(RING),
-            *both(planes), *both(planes),
+            *both(2), *both(1), *both(3), *both(3), *both(2), *both(6), *both(1), *both(1), *both(3), *both(2), *both(1), *both(1), *both(1), *both(1), *both(1), *both(1), *both(1),
         ],
         compiler_params=pltpu.CompilerParams(
             collective_id=0, has_side_effects=True, vmem_limit_bytes=60 * 2**20
@@ -721,13 +730,9 @@
         g_recv[:, 128 * m : 128 * (m + 1)] = a[512 * m : 512 * (m + 1)]
     for m in range(4):
         g_out[:, 128 * m : 128 * (m + 1)] = a[1024 + 256 * m : 1024 + 256 * (m + 1)]
-    each = 1024 // (RING * weights_v.shape[0])
-    b = weights_v[:, chunk_a:, :].astype(F32)
-    for k in range(RING):
-        rows = b[:, k * each : (k + 1) * each, :].reshape(1024 // RING, 128)
-        at = k * (1024 // RING) % 512
-        lanes = slice(128 * (k * 2 // RING), 128 * (k * 2 // RING) + 128)
-        g_send[at : at + 1024 // RING, lanes] = rows
+    b = weights_v[:, chunk_a:, :].reshape(1024, 128).astype(F32)
+    for m in range(2):
+        g_send[:, 128 * m : 128 * (m + 1)] = b[512 * m : 512 * (m + 1)]
     copies[1].wait()
     copies[2].wait()
 

time: 98.7 us -> 94.4 us (0.956)
  the two profiles are of different devices: /device:TPU:8 before, /device:TPU:3 now
where the time goes in v5:
time: 94.4 us; the launch traced here: 94.2 us
  Pallas kernels  93.6 us (99%)
    pallas_call x1, Pallas kernels, layer(): pl.pallas_call(functools.partial(layer_kernel, n_patch), out_shape=(jax.S...  90.2 us
    pallas_call x1, Pallas kernels, finish(): pl.pallas_call(functools.partial(finish_kernel, 2048 // args[2].shape[0])...  3.36 us

profile of v5, /device:TPU:3, one launch (start us, length us, event | category | flops | bytes accessed | tf_op | source)
XLA Modules:
  0.0 94.2 jit_solution(5120967318061723821)
XLA Ops:
  0.6 90.2 %layer.1 = (bf16[640,256]{1,0:T(8,128)(2,1)}, bf16[640,256]{1,0:T(8,128)(2,1)}, bf16[16,192,128]{2,1,0:T(8,128)(2,1)}, f32[1,256]{1,0:T(1,128)}) custom-call(s32[64,128]{1,0:T(8,128)} %bitcast.7, s32[64,128]{1,0:T(8,128)} %bitcast.8, s32[16,128]{1,0:T(8,128)} %bitcast.9, f32[1,256]{1,0:T(1,128)} %bitcast.10, bf16[640,256]{1,0:T(8,128)(2,1)} %feats.1, ...), custom_call_target="tpu_custom_call" | custom-call | tf_op jit(solution)/shard_map/layer/pallas_call | solution.py:640
  90.9 3.4 %finish.1 = (bf16[640,256]{1,0:T(8,128)(2,1)}, bf16[640,256]{1,0:T(8,128)(2,1)}, f32[512,256]{1,0:T(8,128)}, f32[512,256]{1,0:T(8,128)}, f32[256,512]{1,0:T(8,128)}, /*index=5*/f32[1,256]{1,0:T(1,128)}) custom-call(bf16[640,256]{1,0:T(8,128)(2,1)} %get-tuple-element.16.updated, bf16[640,256]{1,0:T(8,128)(2,1)} %get-tuple-element.17.grad_nodes, ...), custom_call_target="tpu_custom_call" | custom-call | tf_op jit(solution)/shard_map/finish/pallas_call | solution.py:743

commit v6 on v5

--- a/solution.py
+++ b/solution.py
@@ -23,8 +23,8 @@
 RING = 8
 PER = RING * QUOTA
 ORDER = (0, 1, 7, 2, 6, 3, 5, 4)
-GROUPS = ((0, 1), (1, 3), (3, 8))
-HALVES = ((0, 3), (3, 8))
+GROUPS = ((0, 1), (1, 3), (3, 5), (5, 8))
+HALVES = ((0, 5), (5, 8))
 MESH = pl.DeviceIdType.MESH
 F32 = jnp.float32
 BF16 = jnp.bfloat16
@@ -124,13 +124,13 @@
     sender, receiver, wanted, bias, feats, cot, send_w_in, recv_w_in, out_w_in,
     updated, grad_nodes, plane_all, bias_out,
     table, cots, send_w, recv_w, out_w, asked, asked_z, coarse, packed,
-    lists, keys, turned, plan_v, plan, cols_s, cols_r, rows_k, pairs_k,
+    lists, picks, keys, turned, plan_v, plan, cols_s, cols_r, rows_k, pairs_k,
     send_s, pair_s, gsum, pre_s, gat_s, items, act_a, act_b, acc, dtab,
     far_s, rim_s, mix, mix_r, back, back_s, back_r,
     wire_a, wire_b, wire_ar, wire_br, far_r, rim_r,
-    zfar_s, zfar_r, zsum_s, zsum_r, zall, plane_s, zsum_bs, zsum_br, zall_b, plane_bs, updated_v, nodes_v,
+    zfar_s, zfar_r, zsum_s, zsum_r, zall, plane_s, zsum_bs, zsum_br, plane_bs, updated_v, nodes_v,
     loc, zs_s, zs_r, ls_s, ls_r, ps_s, ps_r, pass_s, pass_r, hs_s, hs_r, os_s, os_r,
-    wa_s, wa_r, wb_s, wb_r, fb_s, fb_r, hb_s, hb_r, zf_s, zf_r, zw_s, zw_r, za_s, za_r, pa_s, pa_r, pb_s, pb_r, zx_s, zx_r, zy_s, zy_r,
+    wa_s, wa_r, wb_s, wb_r, fb_s, fb_r, hb_s, hb_r, zf_s, zf_r, zw_s, zw_r, za_s, za_r, pa_s, pa_r, pb_s, pb_r, zx_s, zx_r,
 ):
     planes = n_patch // RING
     table_rows = NEAR + n_patch * QUOTA
@@ -193,7 +193,7 @@
     pl.semaphore_wait(barrier, planes - 1 + RING - 1 + 3)
 
     def coarse_copy(d):
-        return remote(feats.at[0:COARSE], coarse.at[RING - d, 0:COARSE], zs_s.at[0], zs_r.at[0 if d in (1, RING - 1) else 1], ring_peer(d), feat)
+        return remote(feats.at[0:COARSE], coarse.at[RING - d, 0:COARSE], zs_s.at[0], zs_r.at[min(d, RING - d, 3) - 1], ring_peer(d), feat)
 
     def list_copy(d):
         to = plane_at(d)
@@ -256,6 +256,8 @@
     pack(0)
     arrived(coarse.at[1:3, 0:COARSE], zs_s.at[0], zs_r.at[0])
     pack(1)
+    arrived(coarse.at[1:3, 0:COARSE], zs_s.at[0], zs_r.at[1])
+    pack(2)
     flat = keys[...]
     turned[...] = jnp.transpose(jnp.concatenate([flat, flat], axis=0))
     lane64 = lax.broadcasted_iota(I32, (PAIRS, 128), 1)
@@ -281,9 +283,13 @@
     plan_v[...] = jnp.concatenate([block_of, last_of, first_of, jnp.zeros((5, 128), I32)], axis=0)
     to_scalars = pltpu.make_async_copy(plan_v, plan, loc.at[8])
     to_scalars.start()
-
-    arrived(coarse.at[2:7, 0:COARSE], zs_s.at[0], zs_r.at[1])
-    pack(2)
+    asked_t = jnp.transpose(asked_z[...])
+    tall_c = lax.broadcasted_iota(I32, (COARSE, planes * QUOTA), 0)
+    for k in range(RING):
+        picks[k] = hot32(asked_t[k : k + 1, :] == tall_c)
+
+    arrived(coarse.at[3:6, 0:COARSE], zs_s.at[0], zs_r.at[2])
+    pack(3)
     own_far = pltpu.make_async_copy(packed.at[xy], far_rows(xy), loc.at[7])
     own_far.start()
     swap_far = remote(packed.at[xy], far_rows(xy), pass_s.at[2], pass_r.at[2], me, other)
@@ -327,11 +333,11 @@
     swap(low_rim, 2).start()
     to_below.wait()
     swap(high_rim, 3).start()
-    for g in range(2):
+    for g in range(3):
         arrived(all_far(feat, *GROUPS[g]), ps_s.at[g], ps_r.at[g])
     loop(1, planes, lambda d: pass_on(plane_from(d), 0).start())
     loop(BLOCKS // 8, BLOCKS // 4, receive)
-    arrived(all_far(feat, *GROUPS[2]), ps_s.at[2], ps_r.at[2])
+    arrived(all_far(feat, *GROUPS[3]), ps_s.at[3], ps_r.at[3])
     loop(1, planes, lambda d: pass_on(plane_from(d), 1).start())
 
     def project(start, size):
@@ -475,7 +481,7 @@
         src = far_s.at[pl.ds(pl.multiple_of(to * PER + low * QUOTA, QUOTA), (high - low) * QUOTA)]
         return remote(src, far_r.at[xy, low * QUOTA : high * QUOTA], fb_s.at[g], fb_r.at[g], to * RING + z, feat)
 
-    for g in (2, 1, 0):
+    for g in (3, 2, 1, 0):
         loop(1, planes, lambda d: far_copy(g, d).start())
     far_r[xy] = far_s[rows_of(xy, PER), :]
     back[...] = mm(recv_grad_b, recv_w[...], NT)
@@ -516,15 +522,13 @@
     total = wire_br[0].astype(F32)
     for p in range(1, planes):
         total = total + wire_br[p].astype(F32)
-    part_b = chunk_b // RING
-    zsum_bs[...] = total.reshape(RING, part_b, 128)
+    zsum_bs[...] = total.astype(BF16)
 
     def zsum_b_copy(d):
-        to = lax.rem(z + d, RING)
-        return remote(zsum_bs.at[to], zsum_br.at[z], zx_s.at[0], zx_r.at[0], ring_peer(d), feat)
+        return remote(zsum_bs, zsum_br.at[z], zx_s.at[0], zx_r.at[0], ring_peer(d), feat)
 
     loop(1, RING, lambda d: zsum_b_copy(d).start())
-    zsum_br[z] = zsum_bs[z]
+    zsum_br[z] = zsum_bs[...]
 
     arrived(zall.at[0:around], za_s.at[0], za_r.at[0])
     plane_s[...] = zall[...].reshape(chunk_a, 128).astype(BF16)
@@ -539,69 +543,73 @@
     keep_plane.start()
 
     arrived(zsum_br.at[0:around], zx_s.at[0], zx_r.at[0])
-    whole = zsum_br[0]
+    whole = zsum_br[0].astype(F32)
     for k in range(1, RING):
-        whole = whole + zsum_br[k]
-    zall_b[z] = whole
-
-    def zall_b_copy(d):
-        return remote(zall_b.at[z], zall_b.at[z], zy_s.at[0], zy_r.at[0], ring_peer(d), feat)
-
-    loop(1, RING, lambda d: zall_b_copy(d).start())
+        whole = whole + zsum_br[k].astype(F32)
+    plane_bs[...] = whole.astype(BF16)
+
+    def all_b_copy(d):
+        return remote(
+            plane_bs, plane_all.at[xy, chunk_a : chunk_a + chunk_b], pb_s.at[0], pb_r.at[0], plane_at(d) * RING + z, feat
+        )
+
+    loop(1, planes, lambda d: all_b_copy(d).start())
+    keep_plane_b = pltpu.make_async_copy(plane_bs, plane_all.at[xy, chunk_a : chunk_a + chunk_b], loc.at[8])
+    keep_plane_b.start()
+
+    back_below.wait()
+    back_up.wait()
+    rest = dtab[HALO + COARSE : 2 * HALO, :] + rim_r[0, COARSE:HALO, :].astype(F32)
+    end = dtab[ROWS : ROWS + HALO, :] + rim_r[1].astype(F32)
+    send_grad = jnp.concatenate([rest, dtab[2 * HALO : ROWS, :], end], axis=0).astype(BF16)
+    terms = back[COARSE:, :] + mm(send_grad, send_w[...], NT)
+    back_s[0, COARSE:] = terms[:, 0:HALF]
+    back_s[1, COARSE:] = terms[:, HALF:]
+    swap_back = remote(back_s.at[other, COARSE:ROWS], back_r.at[COARSE:ROWS], os_s.at[5], os_r.at[5], me, other)
+    swap_back.start()
 
     def sum_owners(g):
         low, high = GROUPS[g]
         arrived(far_r.at[0:others, low * QUOTA : high * QUOTA], fb_s.at[g], fb_r.at[g])
         for at in range(low, high):
             k = ORDER[at]
-            pick = hot32(asked_z[:, k : k + 1] == lane32)
             rows = far_r[:, at * QUOTA : (at + 1) * QUOTA, :].reshape(planes * QUOTA, HALF)
-            zfar_s[k] = mm(pick, rows, TN)[0:COARSE].astype(BF16)
+            zfar_s[k] = mm(picks[k], rows).astype(BF16)
             if k:
                 zfar_copy(k).start()
 
     def zfar_copy(d):
         return remote(zfar_s.at[d], zfar_r.at[d], zf_s.at[0], zf_r.at[0], ring_peer(d), feat)
 
-    def all_b_copy(d):
-        return remote(
-            plane_bs, plane_all.at[xy, chunk_a : chunk_a + chunk_b], pb_s.at[0], pb_r.at[0], plane_at(d) * RING + z, feat
-        )
-
+    sum_owners(3)
     sum_owners(2)
-    arrived(zall_b.at[0:around], zy_s.at[0], zy_r.at[0])
-    plane_bs[...] = zall_b[...].reshape(chunk_b, 128).astype(BF16)
-    loop(1, planes, lambda d: all_b_copy(d).start())
-    keep_plane_b = pltpu.make_async_copy(plane_bs, plane_all.at[xy, chunk_a : chunk_a + chunk_b], loc.at[8])
-    keep_plane_b.start()
-
     sum_owners(1)
     sum_owners(0)
     zfar_r[0] = zfar_s[0]
-    back_below.wait()
-    back_up.wait()
     arrived(zfar_r.at[0:around], zf_s.at[0], zf_r.at[0])
     head = zfar_r[0].astype(F32)
     for k in range(1, RING):
         head = head + zfar_r[k].astype(F32)
     head = head + dtab[HALO : HALO + COARSE, :] + rim_r[0, 0:COARSE, :].astype(F32)
-    rest = dtab[HALO + COARSE : 2 * HALO, :] + rim_r[0, COARSE:HALO, :].astype(F32)
-    end = dtab[ROWS : ROWS + HALO, :] + rim_r[1].astype(F32)
-    send_grad = jnp.concatenate([head, rest, dtab[2 * HALO : ROWS, :], end], axis=0).astype(BF16)
-    terms = back[...] + mm(send_grad, send_w[...], NT)
-    back_s[0] = terms[:, 0:HALF]
-    back_s[1] = terms[:, HALF:]
-    swap_back = remote(back_s.at[other], back_r, os_s.at[5], os_r.at[5], me, other)
-    swap_back.start()
+    terms = back[0:COARSE, :] + mm(head.astype(BF16), send_w[...], NT)
+    back_s[0, 0:COARSE] = terms[:, 0:HALF]
+    back_s[1, 0:COARSE] = terms[:, HALF:]
+    swap_head = remote(back_s.at[other, 0:COARSE], back_r.at[0:COARSE], os_s.at[6], os_r.at[6], me, other)
+    swap_head.start()
     swap_back.wait()
-    nodes_v[...] = (cots[feat].astype(F32) + back_s[feat] + back_r[...]).astype(BF16)
-    keep_nodes = pltpu.make_async_copy(nodes_v, grad_nodes, loc.at[0])
+    nodes_v[COARSE:, :] = (cots[feat, COARSE:, :].astype(F32) + back_s[feat, COARSE:] + back_r[COARSE:, :]).astype(BF16)
+    keep_rest = pltpu.make_async_copy(nodes_v.at[COARSE:ROWS], grad_nodes.at[COARSE:ROWS], loc.at[1])
+    keep_rest.start()
+    swap_head.wait()
+    nodes_v[0:COARSE, :] = (cots[feat, 0:COARSE, :].astype(F32) + back_s[feat, 0:COARSE] + back_r[0:COARSE, :]).astype(BF16)
+    keep_nodes = pltpu.make_async_copy(nodes_v.at[0:COARSE], grad_nodes.at[0:COARSE], loc.at[0])
     keep_nodes.start()
 
     arrived(plane_all.at[0:others, 0:chunk_a], pa_s.at[0], pa_r.at[0])
     arrived(plane_all.at[0:others, chunk_a : chunk_a + chunk_b], pb_s.at[0], pb_r.at[0])
     keep_updated.wait()
     keep_nodes.wait()
+    keep_rest.wait()
     keep_plane.wait()
     keep_plane_b.wait()
 
@@ -614,8 +622,7 @@
     for g, (low, high) in enumerate(GROUPS):
         departed(far_r.at[0:others, low * QUOTA : high * QUOTA], fb_s.at[g], fb_r.at[g])
     departed(plane_all.at[0:others, chunk_a : chunk_a + chunk_b], pb_s.at[0], pb_r.at[0])
-    departed(zsum_bs.at[0:around], zx_s.at[0], zx_r.at[0])
-    departed(zall_b.at[0:around], zy_s.at[0], zy_r.at[0])
+    departed(zsum_br.at[0:around], zx_s.at[0], zx_r.at[0])
     departed(plane_all.at[0:others, 0:chunk_a], pa_s.at[0], pa_r.at[0])
     departed(zsum_s.at[0:around], zw_s.at[0], zw_r.at[0])
     departed(zall.at[0:around], za_s.at[0], za_r.at[0])
@@ -658,6 +665,7 @@
             pltpu.VMEM((RING, HALO, HALF), BF16),
             pltpu.VMEM((planes, PER, HALF), BF16),
             pltpu.VMEM((planes * QUOTA, 128), I32),
+            pltpu.VMEM((RING, COARSE, planes * QUOTA), BF16),
             pltpu.VMEM((PAIRS, 128), I32),
             pltpu.VMEM((128, 128), I32),
             pltpu.VMEM((8, 128), I32),
@@ -695,14 +703,13 @@
             pltpu.VMEM((RING, part + 8, 128), F32),
             pltpu.VMEM((RING, part, 128), F32),
             pltpu.VMEM((chunk_a, 128), BF16),
-            pltpu.VMEM((RING, chunk_b // RING, 128), F32),
-            pltpu.VMEM((RING, chunk_b // RING, 128), F32),
-            pltpu.VMEM((RING, chunk_b // RING, 128), F32),
+            pltpu.VMEM((chunk_b, 128), BF16),
+            pltpu.VMEM((RING, chunk_b, 128), BF16),
             pltpu.VMEM((chunk_b, 128), BF16),
             pltpu.VMEM((ROWS, HALF), BF16),
             pltpu.VMEM((ROWS, HALF), BF16),
             dma((9,)),
-            *both(2), *both(1), *both(3), *both(3), *both(2), *both(6), *both(1), *both(1), *both(3), *both(2), *both(1), *both(1), *both(1), *both(1), *both(1), *both(1), *both(1),
+            *both(3), *both(1), *both(4), *both(3), *both(2), *both(7), *both(1), *both(1), *both(4), *both(2), *both(1), *both(1), *both(1), *both(1), *both(1), *both(1),
         ],
         compiler_params=pltpu.CompilerParams(
             collective_id=0, has_side_effects=True, vmem_limit_bytes=60 * 2**20
@@ -714,34 +721,51 @@
 def finish_kernel(
     chunk_a, updated, grad_nodes, weights, bias,
     updated_o, grad_nodes_o, g_send, g_recv, g_out, g_bias,
-    weights_v, sems,
+    a_v, b_v, updated_v, nodes_v, send_v, recv_v, out_v, sems,
 ):
-    copies = [
-        pltpu.make_async_copy(weights, weights_v, sems.at[0]),
-        pltpu.make_async_copy(updated, updated_o, sems.at[1]),
-        pltpu.make_async_copy(grad_nodes, grad_nodes_o, sems.at[2]),
-    ]
-    for copy in copies:
+    chunk = weights.shape[1]
+    a_in = pltpu.make_async_copy(weights.at[:, 0:chunk_a], a_v, sems.at[0])
+    b_in = pltpu.make_async_copy(weights.at[:, chunk_a:chunk], b_v, sems.at[1])
+    updated_in = pltpu.make_async_copy(updated, updated_v, sems.at[2])
+    nodes_in = pltpu.make_async_copy(grad_nodes, nodes_v, sems.at[3])
+    for copy in (a_in, b_in, updated_in, nodes_in):
         copy.start()
     g_bias[...] = bias[...]
-    copies[0].wait()
-    a = weights_v[:, 0:chunk_a, :].reshape(2048, 128).astype(F32)
+    outs = [
+        pltpu.make_async_copy(recv_v, g_recv, sems.at[4]),
+        pltpu.make_async_copy(out_v, g_out, sems.at[5]),
+        pltpu.make_async_copy(send_v, g_send, sems.at[6]),
+        pltpu.make_async_copy(updated_v, updated_o, sems.at[7]),
+        pltpu.make_async_copy(nodes_v, grad_nodes_o, sems.at[8]),
+    ]
+    a_in.wait()
+    a = a_v[...].reshape(2048, 128)
     for m in range(2):
-        g_recv[:, 128 * m : 128 * (m + 1)] = a[512 * m : 512 * (m + 1)]
+        recv_v[:, 128 * m : 128 * (m + 1)] = a[512 * m : 512 * (m + 1)].astype(F32)
+    outs[0].start()
     for m in range(4):
-        g_out[:, 128 * m : 128 * (m + 1)] = a[1024 + 256 * m : 1024 + 256 * (m + 1)]
-    b = weights_v[:, chunk_a:, :].reshape(1024, 128).astype(F32)
+        out_v[:, 128 * m : 128 * (m + 1)] = a[1024 + 256 * m : 1024 + 256 * (m + 1)].astype(F32)
+    outs[1].start()
+    b_in.wait()
+    b = b_v[...].reshape(1024, 128)
     for m in range(2):
-        g_send[:, 128 * m : 128 * (m + 1)] = b[512 * m : 512 * (m + 1)]
-    copies[1].wait()
-    copies[2].wait()
+        send_v[:, 128 * m : 128 * (m + 1)] = b[512 * m : 512 * (m + 1)].astype(F32)
+    outs[2].start()
+    updated_in.wait()
+    outs[3].start()
+    nodes_in.wait()
+    outs[4].start()
+    for copy in outs:
+        copy.wait()
 
 
 def finish(*args):
     vmem = pl.BlockSpec(memory_space=pltpu.VMEM)
     hbm = pl.BlockSpec(memory_space=pltpu.HBM)
+    planes, chunk, _ = args[2].shape
+    chunk_a = 2048 // planes
     return pl.pallas_call(
-        functools.partial(finish_kernel, 2048 // args[2].shape[0]),
+        functools.partial(finish_kernel, chunk_a),
         out_shape=(
             jax.ShapeDtypeStruct((ROWS, HALF), BF16),
             jax.ShapeDtypeStruct((ROWS, HALF), BF16),
@@ -751,10 +775,16 @@
             jax.ShapeDtypeStruct((1, HALF), F32),
         ),
         in_specs=[hbm] * 3 + [vmem],
-        out_specs=(vmem,) * 6,
+        out_specs=(hbm,) * 5 + (vmem,),
         scratch_shapes=[
-            pltpu.VMEM(args[2].shape, BF16),
-            pltpu.SemaphoreType.DMA((3,)),
+            pltpu.VMEM((planes, chunk_a, 128), BF16),
+            pltpu.VMEM((planes, chunk - chunk_a, 128), BF16),
+            pltpu.VMEM((ROWS, HALF), BF16),
+            pltpu.VMEM((ROWS, HALF), BF16),
+            pltpu.VMEM((2 * HALF, HALF), F32),
+            pltpu.VMEM((2 * HALF, HALF), F32),
+            pltpu.VMEM((HALF, 2 * HALF), F32),
+            pltpu.SemaphoreType.DMA((9,)),
         ],
         compiler_params=pltpu.CompilerParams(vmem_limit_bytes=62 * 2**20),
         name="finish",

time: 94.4 us -> 90.3 us (0.957)
  the two profiles are of different devices: /device:TPU:3 before, /device:TPU:23 now
where the time goes in v6:
time: 90.3 us; the launch traced here: 90.1 us
  Pallas kernels  89.5 us (99%)
    pallas_call x1, Pallas kernels, layer(): pl.pallas_call(functools.partial(layer_kernel, n_patch), out_shape=(jax.S...  85.8 us
    pallas_call x1, Pallas kernels, finish(): pl.pallas_call(functools.partial(finish_kernel, chunk_a), out_shape=(jax....  3.74 us

profile of v6, /device:TPU:23, one launch (start us, length us, event | category | flops | bytes accessed | tf_op | source)
XLA Modules:
  0.0 90.1 jit_solution(17192203519158149475)
XLA Ops:
  0.6 85.8 %layer.1 = (bf16[640,256]{1,0:T(8,128)(2,1)}, bf16[640,256]{1,0:T(8,128)(2,1)}, bf16[16,192,128]{2,1,0:T(8,128)(2,1)}, f32[1,256]{1,0:T(1,128)}) custom-call(s32[64,128]{1,0:T(8,128)} %bitcast.7, s32[64,128]{1,0:T(8,128)} %bitcast.8, s32[16,128]{1,0:T(8,128)} %bitcast.9, f32[1,256]{1,0:T(1,128)} %bitcast.10, bf16[640,256]{1,0:T(8,128)(2,1)} %feats.1, ...), custom_call_target="tpu_custom_call" | custom-call | tf_op jit(solution)/shard_map/layer/pallas_call | solution.py:647
  86.4 3.7 %finish.1 = (bf16[640,256]{1,0:T(8,128)(2,1)}, bf16[640,256]{1,0:T(8,128)(2,1)}, f32[512,256]{1,0:T(8,128)}, f32[512,256]{1,0:T(8,128)}, f32[256,512]{1,0:T(8,128)}, /*index=5*/f32[1,256]{1,0:T(1,128)}) custom-call(bf16[640,256]{1,0:T(8,128)(2,1)} %get-tuple-element.16.updated, bf16[640,256]{1,0:T(8,128)(2,1)} %get-tuple-element.17.grad_nodes, ...), custom_call_target="tpu_custom_call" | custom-call | tf_op jit(solution)/shard_map/finish/pallas_call | solution.py:767

commit v7 on v6

--- a/solution.py
+++ b/solution.py
@@ -440,11 +440,6 @@
 
     loop(1, planes, lambda d: wire_copy(wire_a, wire_ar, wa_s, wa_r, d).start())
     wire_ar[xy] = wire_a[xy]
-    mixed = mm(edge_sum, out_w[...])
-    mix[0] = mixed[:, 0:HALF]
-    mix[1] = mixed[:, HALF:]
-    swap_mix = remote(mix.at[other], mix_r, os_s.at[4], os_r.at[4], me, other)
-    swap_mix.start()
 
     def scatter(i):
         for u in range(UNROLL):
@@ -481,9 +476,13 @@
         src = far_s.at[pl.ds(pl.multiple_of(to * PER + low * QUOTA, QUOTA), (high - low) * QUOTA)]
         return remote(src, far_r.at[xy, low * QUOTA : high * QUOTA], fb_s.at[g], fb_r.at[g], to * RING + z, feat)
 
-    for g in (3, 2, 1, 0):
-        loop(1, planes, lambda d: far_copy(g, d).start())
+    loop(1, planes, lambda d: far_copy(3, d).start())
     far_r[xy] = far_s[rows_of(xy, PER), :]
+    mixed = mm(edge_sum, out_w[...])
+    mix[0] = mixed[:, 0:HALF]
+    mix[1] = mixed[:, HALF:]
+    swap_mix = remote(mix.at[other], mix_r, os_s.at[4], os_r.at[4], me, other)
+    swap_mix.start()
     back[...] = mm(recv_grad_b, recv_w[...], NT)
     swap_mix.wait()
     updated_v[...] = (table[feat, own, :].astype(F32) + mix[feat] + mix_r[...]).astype(BF16)
@@ -529,6 +528,8 @@
 
     loop(1, RING, lambda d: zsum_b_copy(d).start())
     zsum_br[z] = zsum_bs[...]
+    for g in (2, 1, 0):
+        loop(1, planes, lambda d: far_copy(g, d).start())
 
     arrived(zall.at[0:around], za_s.at[0], za_r.at[0])
     plane_s[...] = zall[...].reshape(chunk_a, 128).astype(BF16)
@@ -721,51 +722,34 @@
 def finish_kernel(
     chunk_a, updated, grad_nodes, weights, bias,
     updated_o, grad_nodes_o, g_send, g_recv, g_out, g_bias,
-    a_v, b_v, updated_v, nodes_v, send_v, recv_v, out_v, sems,
+    weights_v, sems,
 ):
-    chunk = weights.shape[1]
-    a_in = pltpu.make_async_copy(weights.at[:, 0:chunk_a], a_v, sems.at[0])
-    b_in = pltpu.make_async_copy(weights.at[:, chunk_a:chunk], b_v, sems.at[1])
-    updated_in = pltpu.make_async_copy(updated, updated_v, sems.at[2])
-    nodes_in = pltpu.make_async_copy(grad_nodes, nodes_v, sems.at[3])
-    for copy in (a_in, b_in, updated_in, nodes_in):
+    copies = [
+        pltpu.make_async_copy(weights, weights_v, sems.at[0]),
+        pltpu.make_async_copy(updated, updated_o, sems.at[1]),
+        pltpu.make_async_copy(grad_nodes, grad_nodes_o, sems.at[2]),
+    ]
+    for copy in copies:
         copy.start()
     g_bias[...] = bias[...]
-    outs = [
-        pltpu.make_async_copy(recv_v, g_recv, sems.at[4]),
-        pltpu.make_async_copy(out_v, g_out, sems.at[5]),
-        pltpu.make_async_copy(send_v, g_send, sems.at[6]),
-        pltpu.make_async_copy(updated_v, updated_o, sems.at[7]),
-        pltpu.make_async_copy(nodes_v, grad_nodes_o, sems.at[8]),
-    ]
-    a_in.wait()
-    a = a_v[...].reshape(2048, 128)
+    copies[0].wait()
+    a = weights_v[:, 0:chunk_a, :].reshape(2048, 128).astype(F32)
     for m in range(2):
-        recv_v[:, 128 * m : 128 * (m + 1)] = a[512 * m : 512 * (m + 1)].astype(F32)
-    outs[0].start()
+        g_recv[:, 128 * m : 128 * (m + 1)] = a[512 * m : 512 * (m + 1)]
     for m in range(4):
-        out_v[:, 128 * m : 128 * (m + 1)] = a[1024 + 256 * m : 1024 + 256 * (m + 1)].astype(F32)
-    outs[1].start()
-    b_in.wait()
-    b = b_v[...].reshape(1024, 128)
+        g_out[:, 128 * m : 128 * (m + 1)] = a[1024 + 256 * m : 1024 + 256 * (m + 1)]
+    b = weights_v[:, chunk_a:, :].reshape(1024, 128).astype(F32)
     for m in range(2):
-        send_v[:, 128 * m : 128 * (m + 1)] = b[512 * m : 512 * (m + 1)].astype(F32)
-    outs[2].start()
-    updated_in.wait()
-    outs[3].start()
-    nodes_in.wait()
-    outs[4].start()
-    for copy in outs:
-        copy.wait()
+        g_send[:, 128 * m : 128 * (m + 1)] = b[512 * m : 512 * (m + 1)]
+    copies[1].wait()
+    copies[2].wait()
 
 
 def finish(*args):
     vmem = pl.BlockSpec(memory_space=pltpu.VMEM)
     hbm = pl.BlockSpec(memory_space=pltpu.HBM)
-    planes, chunk, _ = args[2].shape
-    chunk_a = 2048 // planes
     return pl.pallas_call(
-        functools.partial(finish_kernel, chunk_a),
+        functools.partial(finish_kernel, 2048 // args[2].shape[0]),
         out_shape=(
             jax.ShapeDtypeStruct((ROWS, HALF), BF16),
             jax.ShapeDtypeStruct((ROWS, HALF), BF16),
@@ -775,16 +759,10 @@
             jax.ShapeDtypeStruct((1, HALF), F32),
         ),
         in_specs=[hbm] * 3 + [vmem],
-        out_specs=(hbm,) * 5 + (vmem,),
+        out_specs=(vmem,) * 6,
         scratch_shapes=[
-            pltpu.VMEM((planes, chunk_a, 128), BF16),
-            pltpu.VMEM((planes, chunk - chunk_a, 128), BF16),
-            pltpu.VMEM((ROWS, HALF), BF16),
-            pltpu.VMEM((ROWS, HALF), BF16),
-            pltpu.VMEM((2 * HALF, HALF), F32),
-            pltpu.VMEM((2 * HALF, HALF), F32),
-            pltpu.VMEM((HALF, 2 * HALF), F32),
-            pltpu.SemaphoreType.DMA((9,)),
+            pltpu.VMEM(args[2].shape, BF16),
+            pltpu.SemaphoreType.DMA((3,)),
         ],
         compiler_params=pltpu.CompilerParams(vmem_limit_bytes=62 * 2**20),
         name="finish",

time: 90.3 us -> 89.3 us (0.989)
  the two profiles are of different devices: /device:TPU:23 before, /device:TPU:8 now
where the time goes in v7:
time: 89.3 us; the launch traced here: 87.5 us
  Pallas kernels  86.9 us (97%)
    pallas_call x1, Pallas kernels, layer(): pl.pallas_call(functools.partial(layer_kernel, n_patch), out_shape=(jax.S...  83.5 us
    pallas_call x1, Pallas kernels, finish(): pl.pallas_call(functools.partial(finish_kernel, 2048 // args[2].shape[0])...  3.36 us

profile of v7, /device:TPU:8, one launch (start us, length us, event | category | flops | bytes accessed | tf_op | source)
XLA Modules:
  0.0 87.5 jit_solution(10387303260174118346)
XLA Ops:
  0.6 83.5 %layer.1 = (bf16[640,256]{1,0:T(8,128)(2,1)}, bf16[640,256]{1,0:T(8,128)(2,1)}, bf16[16,192,128]{2,1,0:T(8,128)(2,1)}, f32[1,256]{1,0:T(1,128)}) custom-call(s32[64,128]{1,0:T(8,128)} %bitcast.7, s32[64,128]{1,0:T(8,128)} %bitcast.8, s32[16,128]{1,0:T(8,128)} %bitcast.9, f32[1,256]{1,0:T(1,128)} %bitcast.10, bf16[640,256]{1,0:T(8,128)(2,1)} %feats.1, ...), custom_call_target="tpu_custom_call" | custom-call | tf_op jit(solution)/shard_map/layer/pallas_call | solution.py:648
  84.2 3.4 %finish.1 = (bf16[640,256]{1,0:T(8,128)(2,1)}, bf16[640,256]{1,0:T(8,128)(2,1)}, f32[512,256]{1,0:T(8,128)}, f32[512,256]{1,0:T(8,128)}, f32[256,512]{1,0:T(8,128)}, /*index=5*/f32[1,256]{1,0:T(1,128)}) custom-call(bf16[640,256]{1,0:T(8,128)(2,1)} %get-tuple-element.16.updated, bf16[640,256]{1,0:T(8,128)(2,1)} %get-tuple-element.17.grad_nodes, ...), custom_call_target="tpu_custom_call" | custom-call | tf_op jit(solution)/shard_map/finish/pallas_call | solution.py:751
